TPU v7x, 256 devices: a whole 4x4x8 slice. The times are simulated.
256 devices in a mesh: mem: 8 (over z_lo, x), dp: 32 (over z_hi, y, core).
Axes of the slice: x: 4, y: 4, z: 8 (z_hi: 4, z_lo: 2; z = z_hi * 2 + z_lo), core: 2. Of those that a mesh axis runs over, the one named last changes fastest.
Arguments:
- member_fields: bfloat16 [32, 16, 256, 1024], P('dp', 'mem'), may hold values from -6 to 6
- weight_first: bfloat16 [7, 256, 256], P(None, 'dp'), may hold values from -0.125 to 0.125
- weight_second: bfloat16 [7, 256, 256], P(None, 'dp'), may hold values from -0.125 to 0.125
- weight_head: bfloat16 [69, 256], P(None, 'dp'), may hold values from -0.375 to 0.375
- neighbours_fine: int32 [7, 1024], replicated, may hold values from -1 to 1023, as said below
- neighbours_mid: int32 [7, 256], replicated, may hold values from -1 to 255, as said below
- parents_fine: int32 [1024], replicated, may hold values from 0 to 255, as said below
- parents_mid: int32 [256], replicated, may hold values from 0 to 63, as said below
- observations: float32 [32, 69, 64], P('dp'), may hold values from -4 to 4
Outputs:
- grad_first: float32 [7, 256, 256], P(None, 'dp')
- grad_second: float32 [7, 256, 256], P(None, 'dp')
- grad_head: float32 [69, 256], P(None, 'dp')
Inputs may be any that keep to these rules, and one draw needn't show every extreme that they name: `neighbours_fine`: row 0 lists each cell itself; rows 1 to 6 list its hex neighbours among the 1024 cells of the window, -1 where a neighbour lies outside the window or is missing at a pentagon. `neighbours_mid`: row 0 lists each cell itself; rows 1 to 6 list its hex neighbours among the 256 cells of the window, -1 where a neighbour lies outside the window or is missing at a pentagon. `parents_fine`: every one of the 256 cells is the parent of exactly 4 cells. `parents_mid`: every one of the 64 cells is the parent of exactly 4 cells.
All inputs are finite; a program needn't handle non-finite values.
Results may differ from a plain program's by a relative error of at most 0.014.
Values may be sent and summed in bfloat16 or wider, within the bound.
No kernel may reach another device: no remote copies, remote signals or barrier semaphores. Data moves between devices by JAX's collectives and lax.ppermute only.
A program may use at most 64 MiB of HBM per device.

v0:
```python
import math

import jax
import jax.numpy as jnp
from jax import lax
from jax.sharding import PartitionSpec as P

MEMBERS = 16


SMOOTH = 0.0001


def silu_slope(preact):
    sigmoid_value = jax.nn.sigmoid(preact)
    return sigmoid_value * (1.0 + preact * (1.0 - sigmoid_value))


def build_tiles(fields, neighbours):
    present = (neighbours >= 0).astype(fields.dtype)
    return [
        jnp.take(fields, jnp.maximum(neighbours[direction], 0), axis=2) * present[direction]
        for direction in range(neighbours.shape[0])
    ]


def conv_forward(tiles, weight, fields):
    running = jnp.zeros((fields.shape[0], weight.shape[1], fields.shape[2]), jnp.float32)
    for direction in range(len(tiles)):
        running = running + jnp.einsum(
            "oi,min->mon", weight[direction], tiles[direction], preferred_element_type=jnp.float32
        )
    return running


def conv_weight_grad(slope, tiles):
    return jnp.stack(
        [
            jnp.einsum("mon,min->oi", slope, tiles[direction], preferred_element_type=jnp.float32)
            for direction in range(len(tiles))
        ]
    )


def conv_input_grad(start_value, slope, weight, neighbours):
    present = (neighbours >= 0).astype(jnp.float32)
    spread_back = (
        jnp.einsum("joi,mon->mijn", weight, slope, preferred_element_type=jnp.float32) * present
    )
    spread_back = spread_back.reshape(spread_back.shape[0], spread_back.shape[1], -1)
    return start_value.at[:, :, jnp.maximum(neighbours, 0).reshape(-1)].add(spread_back)


def pooling(parents, coarse):
    return (parents[:, None] == jnp.arange(coarse, dtype=jnp.int32)[None, :]).astype(jnp.bfloat16)


def score_derivative(local_members, member_cohort, truth_states, normalizing_multiplier):
    ensemble_size = member_cohort.shape[0]
    error_term = local_members - truth_states[None]
    skill_term = error_term / jnp.sqrt(error_term * error_term + SMOOTH) / ensemble_size
    pairwise = local_members[:, None] - member_cohort[None, :]
    spread_term = jnp.sum(pairwise / jnp.sqrt(pairwise * pairwise + SMOOTH), axis=1) / (
        ensemble_size * (ensemble_size - 1)
    )
    return normalizing_multiplier * (skill_term - spread_term)


def per_device(
    member_fields,
    weight_first,
    weight_second,
    weight_head,
    neighbours_fine,
    neighbours_mid,
    parents_fine,
    parents_mid,
    observations,
):
    first_full, second_full, head_complete = (
        lax.all_gather(weight_first, "dp", axis=1, tiled=True),
        lax.all_gather(weight_second, "dp", axis=1, tiled=True),
        lax.all_gather(weight_head, "dp", axis=1, tiled=True),
    )
    fields_in = member_fields[0]
    truth_states = observations[0]
    cells_mid = neighbours_mid.shape[1]
    cells_out = truth_states.shape[1]
    normalizing_multiplier = MEMBERS / math.sqrt(lax.axis_size("dp") * cells_out)
    tiles_in = build_tiles(fields_in, neighbours_fine)
    pre_first = conv_forward(tiles_in, first_full, fields_in)
    hidden_first = (fields_in.astype(jnp.float32) + jax.nn.silu(pre_first)).astype(jnp.bfloat16)
    fields_mid = (
        jnp.einsum(
            "mcf,fp->mcp",
            hidden_first,
            pooling(parents_fine, cells_mid),
            preferred_element_type=jnp.float32,
        )
        * 0.25
    ).astype(jnp.bfloat16)
    tiles_mid = build_tiles(fields_mid, neighbours_mid)
    pre_second = conv_forward(tiles_mid, second_full, fields_mid)
    hidden_second = (fields_mid.astype(jnp.float32) + jax.nn.silu(pre_second)).astype(jnp.bfloat16)
    output_fields = (
        jnp.einsum(
            "mcf,fp->mcp",
            hidden_second,
            pooling(parents_mid, cells_out),
            preferred_element_type=jnp.float32,
        )
        * 0.25
    ).astype(jnp.bfloat16)
    predicted_states = jnp.einsum(
        "mt,ctq->cmq", head_complete, output_fields, preferred_element_type=jnp.float32
    )
    member_cohort = lax.all_to_all(predicted_states, "mem", split_axis=2, concat_axis=0, tiled=True)
    slice_width = member_cohort.shape[2]
    observed_slice = lax.dynamic_slice_in_dim(
        truth_states, lax.axis_index("mem") * slice_width, slice_width, 1
    )
    slope_points = score_derivative(
        member_cohort, member_cohort, observed_slice, normalizing_multiplier
    ).astype(jnp.bfloat16)
    predicted_derivative = lax.all_to_all(
        slope_points, "mem", split_axis=0, concat_axis=2, tiled=True
    )
    grad_head = jnp.einsum(
        "mfp,mcp->fc", predicted_derivative, output_fields, preferred_element_type=jnp.float32
    )
    back_out = jnp.einsum(
        "fc,mfp->mcp", head_complete, predicted_derivative, preferred_element_type=jnp.float32
    )
    back_second = jnp.take(back_out, parents_mid, axis=2) * 0.25
    slope_second = (back_second * silu_slope(pre_second)).astype(jnp.bfloat16)
    grad_second = conv_weight_grad(slope_second, tiles_mid)
    back_mid = conv_input_grad(back_second, slope_second, second_full, neighbours_mid)
    back_first = jnp.take(back_mid, parents_fine, axis=2) * 0.25
    slope_first = (back_first * silu_slope(pre_first)).astype(jnp.bfloat16)
    grad_first = conv_weight_grad(slope_first, tiles_in)
    shares = (
        lax.psum_scatter(
            grad_first.astype(jnp.bfloat16), "dp", scatter_dimension=1, tiled=True
        ).astype(jnp.float32),
        lax.psum_scatter(
            grad_second.astype(jnp.bfloat16), "dp", scatter_dimension=1, tiled=True
        ).astype(jnp.float32),
        lax.psum_scatter(
            grad_head.astype(jnp.bfloat16), "dp", scatter_dimension=1, tiled=True
        ).astype(jnp.float32),
    )
    result = (
        lax.psum(shares[0].astype(jnp.bfloat16), "mem").astype(jnp.float32),
        lax.psum(shares[1].astype(jnp.bfloat16), "mem").astype(jnp.float32),
        lax.psum(shares[2].astype(jnp.bfloat16), "mem").astype(jnp.float32),
    )
    return (result[0], result[1], result[2])


def solution(mesh):
    placed = (
        P("dp", "mem", None, None),
        P(None, "dp", None),
        P(None, "dp", None),
        P(None, "dp"),
        P(),
        P(),
        P(),
        P(),
        P("dp", None, None),
    )
    return jax.shard_map(
        per_device,
        mesh=mesh,
        in_specs=placed,
        out_specs=(P(None, "dp", None), P(None, "dp", None), P(None, "dp")),
        check_vma=False,
    )
```

profile of v0, /device:TPU:6, one launch (start us, length us, event | category | flops | bytes accessed | tf_op | source)
XLA Modules:
  0.0 689.7 jit_solution(13077724556080265814)
XLA Ops:
  15.8 4.2 gather_fusion.6
  19.9 5.7 bitcast_multiply_fusion.6
  27.1 53.9 %all_gather.9 = bf16[7,256,256]{2,1,0:T(8,128)(2,1)} all-gather(bf16[7,8,256]{2,1,0:T(8,128)(2,1)S(1)} %copy-done.33), channel_id=1, replica_groups=mesh['mem'=8,'dp'=32] {'dp'}, dimensions={1}, use_global_device_ids=true | all-gather | bytes 946176 | tf_op jit(solution)/shard_map/all_gather | solution.py:81
  81.0 4.2 gather_fusion.5
  85.2 6.3 bitcast_multiply_fusion.7
  99.6 4.2 gather_fusion.4
  103.7 5.7 bitcast_multiply_fusion.8
  113.8 4.2 gather_fusion.3
  117.9 6.3 bitcast_multiply_fusion.9
  129.6 4.2 gather_fusion.2
  133.8 6.3 bitcast_multiply_fusion.10
  145.5 4.2 gather_fusion.7
  149.7 6.3 bitcast_multiply_fusion.5
  161.4 4.2 gather_fusion.8
  165.5 5.7 bitcast_multiply_fusion.4
  171.2 13.0 %copy.311 = bf16[2,256,1024]{2,1,0:T(8,128)(2,1)S(1)} copy(bf16[2,256,1024]{1,0,2:T(2,128)(2,1)S(1)} %bitcast_multiply_fusion.4) | data formatting | bytes 2097152 | tf_op jit(solution)/shard_map/mul | solution.py:22
  184.3 6.0 add_add_fusion
  195.9 41.9 %all_gather.10 = bf16[7,256,256]{2,1,0:T(8,128)(2,1)S(1)} all-gather(bf16[7,8,256]{2,1,0:T(8,128)(2,1)S(1)} %copy-done.34), channel_id=1, replica_groups=mesh['mem'=8,'dp'=32] {'dp'}, dimensions={1}, use_global_device_ids=true | all-gather | bytes 946176 | tf_op jit(solution)/shard_map/all_gather | solution.py:82
  246.5 3.1 bitcast_multiply_fusion.15
  253.4 3.1 bitcast_multiply_fusion.14
  260.2 3.1 bitcast_multiply_fusion.13
  274.0 3.2 bitcast_multiply_fusion.11
  279.0 40.5 %all_gather.11 = bf16[69,256]{0,1:T(8,128)(2,1)S(1)} all-gather(bf16[69,8]{0,1:T(8,128)(2,1)S(1)} %copy-done.36), channel_id=1, replica_groups=mesh['mem'=8,'dp'=32] {'dp'}, dimensions={1}, use_global_device_ids=true | all-gather | bytes 36432 | tf_op jit(solution)/shard_map/all_gather | solution.py:83
  324.4 4.8 all-to-all-start
  329.3 4.1 all-to-all-done
  334.3 5.3 all-to-all-start.1
  339.6 4.2 all-to-all-done.1
  356.1 11.4 %copy.368 = f32[2,256,1792]{1,0,2:T(2,128)} copy(f32[2,256,1792]{1,2,0:T(8,128)S(1)} %bitcast.420) | data formatting | bytes 7340032 | tf_op jit(solution)/shard_map/reshape | solution.py:50
  367.7 123.3 %scatter_fusion = f32[2,256,256]{1,0,2:T(2,128)S(1)} fusion(f32[2,256,256]{1,0,2:T(2,128)S(1)} %copy.296, s32[1792]{0:T(1024)S(1)} %fusion.80, f32[1792,2,256]{2,1,0:T(2,128)} %bitcast.421), kind=kCustom, calls=%fused_computation.16 | custom fusion | flops 917504 | bytes 11017216 | tf_op jit(solution)/shard_map/scatter-add | solution.py:51
  491.0 8.8 %gather_fusion.1 = f32[1024,2,256]{2,1,0:T(2,128)} fusion(f32[2,256,256]{1,0,2:T(2,128)S(1)} %scatter_fusion, s32[1024]{0:T(1024)S(1)} %fusion.81), kind=kCustom, calls=%fused_computation.15 | custom fusion | bytes 4198400 | tf_op jit(solution)/shard_map/jit(_take)/gather | solution.py:138
  509.7 138.5 %all-reduce = bf16[69,256]{0,1:T(8,128)(2,1)S(1)} all-reduce(bf16[69,256]{0,1:T(8,128)(2,1)S(1)} %fusion.54), channel_id=4, replica_groups=mesh['mem'=8,'dp'=32] {'dp'}, use_global_device_ids=true, to_apply=%region_6.9.clone | all-reduce | flops 17664 | bytes 70656
  649.9 30.9 %all-reduce.1 = (bf16[7,8,256]{2,1,0:T(8,128)(2,1)S(1)}, bf16[7,8,256]{2,1,0:T(8,128)(2,1)S(1)}, bf16[69,8]{0,1:T(8,128)(2,1)S(1)}) all-reduce(bf16[7,8,256]{2,1,0:T(8,128)(2,1)S(1)} %copy.345, bf16[7,8,256]{2,1,0:T(8,128)(2,1)S(1)} %copy.347, bf16[69,8]{0,1:T(8,128)(2,1)S(1)} %constant_dynamic-slice_fusion), channel_id=1, replica_groups=mesh['mem'=8,'dp'=32] {'mem'}, use_global_device_ids=true, to_apply=%region_3.6 | all-reduce | flops 29224 | bytes 116896 | tf_op jit(solution)/shard_map/psum | solution.py:153
  (211 shorter events, 103.0 us)
Async XLA Ops:
  7.2 322.1 %copy-start = (f32[1,69,64]{1,2,0:T(8,128)S(1)}, f32[1,69,64]{1,2,0:T(8,128)}, u32[]{:S(2)}) copy-start(f32[1,69,64]{1,2,0:T(8,128)} %param.21) | copy-start | bytes 52996
  7.2 7.6 %copy-start.13 = (bf16[1,2,256,1024]{3,2,1,0:T(8,128)(2,1)S(1)}, bf16[1,2,256,1024]{3,2,1,0:T(8,128)(2,1)}, u32[]{:S(2)}) copy-start(bf16[1,2,256,1024]{3,2,1,0:T(8,128)(2,1)} %param.13) | copy-start | bytes 3145732
  19.9 7.2 %copy-start.33 = (bf16[7,8,256]{2,1,0:T(8,128)(2,1)S(1)}, bf16[7,8,256]{2,1,0:T(8,128)(2,1)}, u32[]{:S(2)}) copy-start(bf16[7,8,256]{2,1,0:T(8,128)(2,1)} %param.14) | copy-start | bytes 86020
  27.1 66.9 %copy-start.1 = (bf16[2,256,1024]{2,1,0:T(8,128)(2,1)}, bf16[2,256,1024]{2,1,0:T(8,128)(2,1)S(1)}, u32[]{:S(2)}) copy-start(bf16[2,256,1024]{2,1,0:T(8,128)(2,1)S(1)} %copy.307) | copy-start | bytes 3145732
  94.0 5.6 copy-start.3
  110.9 7.0 %copy-start.5 = (bf16[2,256,1024]{2,1,0:T(8,128)(2,1)}, bf16[2,256,1024]{2,1,0:T(8,128)(2,1)S(1)}, u32[]{:S(2)}) copy-start(bf16[2,256,1024]{2,1,0:T(8,128)(2,1)S(1)} %copy.303) | copy-start | bytes 3145732
  126.7 7.1 %copy-start.7 = (bf16[2,256,1024]{2,1,0:T(8,128)(2,1)}, bf16[2,256,1024]{2,1,0:T(8,128)(2,1)S(1)}, u32[]{:S(2)}) copy-start(bf16[2,256,1024]{2,1,0:T(8,128)(2,1)S(1)} %copy.301) | copy-start | bytes 3145732
  142.6 7.1 %copy-start.11 = (bf16[2,256,1024]{2,1,0:T(8,128)(2,1)}, bf16[2,256,1024]{2,1,0:T(8,128)(2,1)S(1)}, u32[]{:S(2)}) copy-start(bf16[2,256,1024]{2,1,0:T(8,128)(2,1)S(1)} %copy.299) | copy-start | bytes 3145732
  158.5 7.0 %copy-start.9 = (bf16[2,256,1024]{2,1,0:T(8,128)(2,1)}, bf16[2,256,1024]{2,1,0:T(8,128)(2,1)S(1)}, u32[]{:S(2)}) copy-start(bf16[2,256,1024]{2,1,0:T(8,128)(2,1)S(1)} %copy.309) | copy-start | bytes 3145732
  184.3 6.0 copy-start.14
  184.3 6.0 copy-start.29
  184.3 6.0 copy-start.35
  191.3 3.7 copy-start.30
  191.3 4.6 copy-start.34
  192.8 53.7 %copy-start.38 = (pred[256]{0:T(512)(128)(4,1)S(1)}, pred[256]{0:T(512)(128)(4,1)}, u32[]{:S(2)}) copy-start(pred[256]{0:T(512)(128)(4,1)} %compare_and_fusion.12) | copy-start | bytes 772
  260.2 18.8 %copy-start.36 = (bf16[69,8]{0,1:T(8,128)(2,1)S(1)}, bf16[69,8]{0,1:T(8,128)(2,1)}, u32[]{:S(2)}) copy-start(bf16[69,8]{0,1:T(8,128)(2,1)} %param.16) | copy-start | bytes 3316
  274.0 46.7 %copy-start.16 = (bf16[2,256,256]{2,1,0:T(8,128)(2,1)S(1)}, bf16[2,256,256]{2,1,0:T(8,128)(2,1)}, u32[]{:S(2)}) copy-start(bf16[2,256,256]{2,1,0:T(8,128)(2,1)} %copy.313) | copy-start | bytes 786436
  279.0 42.0 %copy-start.17 = (bf16[2,256,256]{2,1,0:T(8,128)(2,1)S(1)}, bf16[2,256,256]{2,1,0:T(8,128)(2,1)}, u32[]{:S(2)}) copy-start(bf16[2,256,256]{2,1,0:T(8,128)(2,1)} %copy.314) | copy-start | bytes 786436
  279.0 42.2 %copy-start.19 = (bf16[2,256,256]{2,1,0:T(8,128)(2,1)S(1)}, bf16[2,256,256]{2,1,0:T(8,128)(2,1)}, u32[]{:S(2)}) copy-start(bf16[2,256,256]{2,1,0:T(8,128)(2,1)} %copy.315) | copy-start | bytes 786436
  322.2 6.9 %copy-start.32 = (s32[7,256]{1,0:T(8,128)S(1)}, s32[7,256]{1,0:T(8,128)}, u32[]{:S(2)}) copy-start(s32[7,256]{1,0:T(8,128)} %param.18) | copy-start | bytes 21508
  324.4 9.1 %all-to-all-start = ((f32[2,69,64]{1,0,2:T(2,128)}), f32[2,69,64]{1,0,2:T(2,128)S(1)}, u32[]{:S(2)}, u32[]{:S(2)}) async-start(f32[2,69,64]{1,0,2:T(2,128)} %copy.288), calls=%async_computation | async-start | bytes 131072 | tf_op jit(solution)/shard_map/all_to_all | solution.py:117
  334.3 9.5 %all-to-all-start.1 = ((bf16[16,69,8]{1,2,0:T(8,128)(2,1)}), bf16[16,69,8]{1,2,0:T(8,128)(2,1)S(1)}, u32[]{:S(2)}, u32[]{:S(2)}) async-start(bf16[16,69,8]{1,2,0:T(8,128)(2,1)} %multiply_convert_fusion.1), calls=%async_computation.1 | async-start | bytes 65536 | tf_op jit(solution)/shard_map/all_to_all | solution.py:125
  339.6 308.6 %reduce-scatter.9.cloned.1.call-start = ((), (), s32[]{:S(2)}) async-start(), calls=%async_computation.5 | async-start | bytes 946176
  348.2 4.8 copy-start.18
  348.2 5.0 copy-start.20
  348.2 5.3 copy-start.22
  350.4 3.3 copy-start.24
  350.4 3.6 copy-start.26
  355.3 293.7 %reduce-scatter.7.cloned.1.call-start = ((), (), s32[]{:S(2)}) async-start(), calls=%async_computation.4 | async-start | bytes 946176
  356.1 11.4 %copy-start.27 = (f32[2,256,256]{2,1,0:T(8,128)S(1)}, f32[2,256,256]{2,1,0:T(8,128)}, u32[]{:S(2)}) copy-start(f32[2,256,256]{2,1,0:T(8,128)} %get-tuple-element.23) | copy-start | bytes 1572868
  499.8 2.5 copy-start.12
  502.4 1.7 copy-start.6
  (12 other events, 14.8 us)
Sparse Core Ops, SparseCore 0:
  355.4 81.6 reduce-scatter.8
  508.3 81.6 reduce-scatter.6
where the time goes:
time: 704 us; the launch traced here: 690 us
  blocking collectives  306 us (43%)
  other arithmetic  199 us (28%)
  local copies, waits for them, and re-layouts  115 us (16%)
  matrix products  35.3 us (5%)
  between operations  15.9 us (2%)
  starting transfers between devices  10.1 us (1%)
  waiting for transfers between devices  8.39 us (1%)
    unnamed x1, blocking collectives  139 us
    scatter-add x1, other arithmetic, conv_input_grad(): start_value.at[:, :, jnp.maximum(neighbours, 0).reshape(-1)]  123 us
    mul x14, other arithmetic, build_tiles(): jnp.take(fields, jnp.maximum(neighbours[direction], 0), axis=2)  63.3 us
    all_gather x1, blocking collectives, per_device(): lax.all_gather(weight_first, 'dp', axis=1, tiled=True)  53.9 us
    all_gather x1, blocking collectives, per_device(): lax.all_gather(weight_second, 'dp', axis=1, tiled=True)  41.9 us
    gather x14, local copies, waits for them, and re-layouts, build_tiles(): jnp.take(fields, jnp.maximum(neighbours[direction], 0), axis=2)  41.8 us
    all_gather x1, blocking collectives, per_device(): lax.all_gather(weight_head, 'dp', axis=1, tiled=True)  40.5 us
    mul x14, local copies, waits for them, and re-layouts, build_tiles(): jnp.take(fields, jnp.maximum(neighbours[direction], 0), axis=2)  37.6 us
  transfers between devices with their start and end apart: 4, of which 2 were waited for; matrix products, arithmetic and copies ran while one was open for 22% of the time, Pallas kernels for 0%

commit v1 on v0

v1 whole, which is shorter than its diff:
```python
import math

import jax
import jax.numpy as jnp
from jax import lax
from jax.experimental import pallas as pl
from jax.experimental.pallas import tpu as pltpu
from jax.sharding import Mesh
from jax.sharding import PartitionSpec as P

DP = ("z_hi", "y", "core")
MEM = ("z_lo", "x")

MEMBERS = 16
CHANNELS = 256
SLOTS = 7
FIELDS = 69
FIELD_ROWS = 72
CELLS_OUT = 64
CELLS_MID = 256
CELLS_IN = 1024
SAMPLES = 32
LOCAL = 2
PIECE = 512
SMOOTH = 0.0001
NORM = MEMBERS / math.sqrt(SAMPLES * CELLS_OUT)
SECOND_AT = SLOTS * CHANNELS
HEAD_AT = 2 * SLOTS * CHANNELS
WIDTH = 4096
VMEM_BYTES = 48 * 1024 * 1024

f32 = jnp.float32
bf16 = jnp.bfloat16


def dot(a, b):
    return lax.dot_general(a, b, (((1,), (0,)), ((), ())), preferred_element_type=f32)


def dot_bt(a, b):
    return lax.dot_general(a, b, (((1,), (1,)), ((), ())), preferred_element_type=f32)


def dot_at(a, b):
    return lax.dot_general(a, b, (((0,), (0,)), ((), ())), preferred_element_type=f32)


def one_hot(index_row, rows):
    shape = (rows, index_row.shape[1])
    return jnp.where(lax.broadcasted_iota(jnp.int32, shape, 0) == index_row, 1.0, 0.0).astype(bf16)


def tiles_kernel(x_ref, nb_ref, out_ref):
    tile = dot(x_ref[...], one_hot(nb_ref[0], CELLS_IN)).astype(bf16)
    for m in range(LOCAL):
        out_ref[m, 0] = tile[m * CHANNELS : (m + 1) * CHANNELS]


def fine_tiles(x0, nb):
    return pl.pallas_call(
        tiles_kernel,
        grid=(SLOTS - 1,),
        in_specs=[
            pl.BlockSpec((LOCAL * CHANNELS, CELLS_IN), lambda j: (0, 0)),
            pl.BlockSpec((1, 1, CELLS_IN), lambda j: (j, 0, 0)),
        ],
        out_specs=pl.BlockSpec((LOCAL, 1, CHANNELS, CELLS_IN), lambda j: (0, j, 0, 0)),
        out_shape=jax.ShapeDtypeStruct((LOCAL, SLOTS - 1, CHANNELS, CELLS_IN), bf16),
        compiler_params=pltpu.CompilerParams(vmem_limit_bytes=VMEM_BYTES),
        cost_estimate=pl.CostEstimate(flops=6_500_000_000, bytes_accessed=8_000_000, transcendentals=0),
        name="fine_tiles",
    )(x0, nb)


def forward_kernel(
    place_ref, mine_ref, other_ref, x_ref, tiles_ref, parents_ref, nb_mid_ref, parents_mid_ref,
    slope1_ref, w_ref, tiles_mid_ref, slope2_ref, x2_ref, pred_ref, pooled_ref,
):
    m, k = pl.program_id(0), pl.program_id(1)

    @pl.when((m == 0) & (k == 0))
    def _():
        core, z = place_ref[0], place_ref[1]
        for source, here in ((mine_ref, core), (other_ref, 1 - core)):
            for x in range(4):
                column = pl.multiple_of(x * 2 * PIECE + here * PIECE, PIECE)
                for y in range(4):
                    for back in range(4):
                        row = pl.multiple_of((lax.rem(z - back + 4, 4) * 4 + y) * 16, 16)
                        w_ref[pl.ds(row, 16), pl.ds(column, PIECE)] = source[x * 4 + y, back]

    a1 = dot(w_ref[:, 0:CHANNELS], x_ref[0])
    for j in range(1, SLOTS):
        a1 = a1 + dot(w_ref[:, j * CHANNELS : (j + 1) * CHANNELS], tiles_ref[0, j - 1])
    gate = jax.nn.sigmoid(a1)
    slope1_ref[0] = (gate * (1.0 + a1 * (1.0 - gate))).astype(bf16)
    h1 = (x_ref[0].astype(f32) + a1 * gate).astype(bf16)
    part = dot_bt(h1, one_hot(parents_ref[...], CELLS_MID))

    @pl.when(k == 0)
    def _():
        pooled_ref[m] = part

    @pl.when(k > 0)
    def _():
        pooled_ref[m] += part

    @pl.when((m == LOCAL - 1) & (k == pl.num_programs(1) - 1))
    def _():
        x1 = (pooled_ref[...].reshape(LOCAL * CHANNELS, CELLS_MID) * 0.25).astype(bf16)
        for i in range(LOCAL):
            tiles_mid_ref[i, 0:CHANNELS] = x1[i * CHANNELS : (i + 1) * CHANNELS]
        for j in range(1, SLOTS):
            tile = dot(x1, one_hot(nb_mid_ref[j : j + 1, :], CELLS_MID)).astype(bf16)
            for i in range(LOCAL):
                tiles_mid_ref[i, j * CHANNELS : (j + 1) * CHANNELS] = tile[i * CHANNELS : (i + 1) * CHANNELS]
        pool = one_hot(parents_mid_ref[...], CELLS_OUT)
        for i in range(LOCAL):
            a2 = dot(w_ref[:, SECOND_AT:HEAD_AT], tiles_mid_ref[i])
            gate2 = jax.nn.sigmoid(a2)
            slope2_ref[i] = gate2 * (1.0 + a2 * (1.0 - gate2))
            h2 = (x1[i * CHANNELS : (i + 1) * CHANNELS].astype(f32) + a2 * gate2).astype(bf16)
            x2_ref[:, i * CELLS_OUT : (i + 1) * CELLS_OUT] = (dot_bt(h2, pool) * 0.25).astype(bf16)
        pred = dot_at(w_ref[:, HEAD_AT : HEAD_AT + 128], x2_ref[...])
        pred_ref[...] = pred[0:FIELD_ROWS]


def forward(place, mine, other, x0, tiles, parents_fine, nb_mid, parents_mid):
    chunk = 256
    whole = lambda *shape: pl.BlockSpec(shape, lambda m, k: (0,) * len(shape))
    return pl.pallas_call(
        forward_kernel,
        grid=(LOCAL, CELLS_IN // chunk),
        in_specs=[
            pl.BlockSpec(memory_space=pltpu.SMEM),
            whole(16, 4, 16, PIECE),
            whole(16, 4, 16, PIECE),
            pl.BlockSpec((1, CHANNELS, chunk), lambda m, k: (m, 0, k)),
            pl.BlockSpec((1, SLOTS - 1, CHANNELS, chunk), lambda m, k: (m, 0, 0, k)),
            pl.BlockSpec((1, chunk), lambda m, k: (0, k)),
            whole(SLOTS, CELLS_MID),
            whole(1, CELLS_MID),
        ],
        out_specs=[
            pl.BlockSpec((1, CHANNELS, chunk), lambda m, k: (m, 0, k)),
            whole(CHANNELS, WIDTH),
            whole(LOCAL, SECOND_AT, CELLS_MID),
            whole(LOCAL, CHANNELS, CELLS_MID),
            whole(CHANNELS, LOCAL * CELLS_OUT),
            whole(FIELD_ROWS, LOCAL * CELLS_OUT),
        ],
        out_shape=[
            jax.ShapeDtypeStruct((LOCAL, CHANNELS, CELLS_IN), bf16),
            jax.ShapeDtypeStruct((CHANNELS, WIDTH), bf16),
            jax.ShapeDtypeStruct((LOCAL, SECOND_AT, CELLS_MID), bf16),
            jax.ShapeDtypeStruct((LOCAL, CHANNELS, CELLS_MID), f32),
            jax.ShapeDtypeStruct((CHANNELS, LOCAL * CELLS_OUT), bf16),
            jax.ShapeDtypeStruct((FIELD_ROWS, LOCAL * CELLS_OUT), f32),
        ],
        scratch_shapes=[pltpu.VMEM((LOCAL, CHANNELS, CELLS_MID), f32)],
        compiler_params=pltpu.CompilerParams(vmem_limit_bytes=VMEM_BYTES),
        cost_estimate=pl.CostEstimate(flops=3_200_000_000, bytes_accessed=14_000_000, transcendentals=700_000),
        name="forward",
    )(place, mine, other, x0, tiles, parents_fine, nb_mid, parents_mid)


def sign_smooth(v):
    return v * lax.rsqrt(v * v + SMOOTH)


def backward_kernel(
    cohort_ref, own_ref, obs_ref, w_ref, tiles_mid_ref, slope2_ref, x2_ref, slope1_ref, x_ref, tiles_ref,
    parents_ref, nb_mid_ref, parents_mid_ref, out_ref, g1_ref,
):
    j = pl.program_id(0)

    def put(piece, half, lanes, value):
        for z in range(4):
            for y in range(4):
                row = (z * 4 + y) * 16
                out_ref[lax.rem(piece, 2), lax.div(piece, 2), y, z, :, pl.ds(half, lanes)] = value[row : row + 16].astype(bf16)

    @pl.when(j == 0)
    def _():
        own = own_ref[...]
        spread = jnp.zeros_like(own)
        for peer in range(MEMBERS // LOCAL):
            theirs = cohort_ref[peer]
            spread = spread + sign_smooth(own - theirs) + sign_smooth(own - pltpu.roll(theirs, CELLS_OUT, 1))
        skill = sign_smooth(own - obs_ref[...])
        slope = NORM * (skill / MEMBERS - spread / (MEMBERS * (MEMBERS - 1)))
        slope = jnp.concatenate([slope, jnp.zeros((128 - FIELD_ROWS, 128), f32)], 0).astype(bf16)
        put(7, 0, 128, dot_bt(x2_ref[...], slope))
        put(7, 128, PIECE - 128, jnp.zeros((CHANNELS, PIECE - 128), f32))
        pool = one_hot(parents_mid_ref[...], CELLS_OUT)
        head_t = w_ref[:, HEAD_AT : HEAD_AT + 128]
        dh2, g2 = [], []
        for i in range(LOCAL):
            wide = dot(slope[:, i * CELLS_OUT : (i + 1) * CELLS_OUT], pool).astype(bf16)
            dh2.append(dot(head_t, wide) * 0.25)
            g2.append((dh2[i] * slope2_ref[i]).astype(bf16))
        for q in range(SLOTS):
            rows = slice(q * CHANNELS, (q + 1) * CHANNELS)
            grad = dot_bt(g2[0], tiles_mid_ref[0, rows]) + dot_bt(g2[1], tiles_mid_ref[1, rows])
            put((SLOTS + q) // 2, (SLOTS + q) % 2 * 256, 256, grad)
        both = jnp.concatenate(g2, 0)
        back = [dh2[i] + dot_at(w_ref[:, SECOND_AT : SECOND_AT + CHANNELS], g2[i]) for i in range(LOCAL)]
        for q in range(1, SLOTS):
            spread_back = dot_bt(both, one_hot(nb_mid_ref[q : q + 1, :], CELLS_MID)).astype(bf16)
            weight = w_ref[:, SECOND_AT + q * CHANNELS : SECOND_AT + (q + 1) * CHANNELS]
            for i in range(LOCAL):
                back[i] = back[i] + dot_at(weight, spread_back[i * CHANNELS : (i + 1) * CHANNELS])
        unpool = one_hot(parents_ref[...], CELLS_MID)
        for i in range(LOCAL):
            dh1 = dot((back[i] * 0.25).astype(bf16), unpool)
            g1_ref[i] = (dh1 * slope1_ref[i].astype(f32)).astype(bf16)
        put(0, 0, 256, dot_bt(g1_ref[0], x_ref[0]) + dot_bt(g1_ref[1], x_ref[1]))

    @pl.when(j > 0)
    def _():
        grad = dot_bt(g1_ref[0], tiles_ref[0, 0]) + dot_bt(g1_ref[1], tiles_ref[1, 0])
        put(lax.div(j, 2), pl.multiple_of(lax.rem(j, 2) * 256, 256), 256, grad)


def backward(cohort, own, obs, w, tiles_mid, slope2, x2, slope1, x0, tiles, parents_fine, nb_mid, parents_mid):
    whole = lambda *shape: pl.BlockSpec(shape, lambda j: (0,) * len(shape))
    return pl.pallas_call(
        backward_kernel,
        grid=(SLOTS,),
        in_specs=[
            whole(*cohort.shape), whole(*own.shape), whole(*obs.shape), whole(*w.shape), whole(*tiles_mid.shape),
            whole(*slope2.shape), whole(*x2.shape), whole(*slope1.shape), whole(*x0.shape),
            pl.BlockSpec((LOCAL, 1, CHANNELS, CELLS_IN), lambda j: (0, jnp.maximum(j - 1, 0), 0, 0)),
            whole(*parents_fine.shape), whole(*nb_mid.shape), whole(*parents_mid.shape),
        ],
        out_specs=whole(2, 4, 4, 4, 16, PIECE),
        out_shape=jax.ShapeDtypeStruct((2, 4, 4, 4, 16, PIECE), bf16),
        scratch_shapes=[pltpu.VMEM((LOCAL, CHANNELS, CELLS_IN), bf16)],
        compiler_params=pltpu.CompilerParams(vmem_limit_bytes=VMEM_BYTES),
        cost_estimate=pl.CostEstimate(flops=4_000_000_000, bytes_accessed=16_000_000, transcendentals=200_000),
        name="backward",
    )(cohort, own, obs, w, tiles_mid, slope2, x2, slope1, x0, tiles, parents_fine, nb_mid, parents_mid)


def shift(v, axis, n, by):
    return lax.ppermute(v, axis, [(i, (i + by) % n) for i in range(n)])


def gather_weights(weight_first, weight_second, weight_head, core, x):
    rows = weight_first.shape[1]
    flat = jnp.concatenate(
        [
            weight_first.transpose(1, 0, 2).reshape(rows, SECOND_AT),
            weight_second.transpose(1, 0, 2).reshape(rows, SECOND_AT),
            weight_head.T,
            jnp.zeros((rows, WIDTH - HEAD_AT - FIELDS), bf16),
        ],
        1,
    )
    pair = lax.dynamic_slice_in_dim(flat, x * 2 * PIECE, 2 * PIECE, 1)
    kept = lax.dynamic_slice_in_dim(pair, core * PIECE, PIECE, 1)
    sent = lax.dynamic_slice_in_dim(pair, (1 - core) * PIECE, PIECE, 1)
    came = shift(sent, "core", 2, 1)
    mine = jnp.where(core == 0, jnp.concatenate([kept, came], 0), jnp.concatenate([came, kept], 0))
    column = jnp.stack([mine] + [shift(mine, "z_hi", 4, s) for s in (1, 2, 3)])
    plane = lax.all_to_all(jnp.broadcast_to(column, (16,) + column.shape), ("x", "y"), 0, 0)
    return plane, shift(plane, "core", 2, 1)


def reduce_gradients(parts, core, x):
    kept = lax.dynamic_index_in_dim(parts, core, 0, keepdims=False)
    sent = lax.dynamic_index_in_dim(parts, 1 - core, 0, keepdims=False)
    total = (kept.astype(f32) + shift(sent, "core", 2, 1).astype(f32)).astype(bf16)
    plane = lax.all_to_all(total.reshape(16, 4, 16, PIECE), ("x", "y"), 0, 0)
    total = jnp.sum(plane.astype(f32), 0).astype(bf16)
    column = jnp.broadcast_to(total[:, None], (4, 2, 16, PIECE)).reshape(8, 16, PIECE)
    column = lax.all_to_all(column, ("z_hi", "z_lo"), 0, 0)
    total = jnp.sum(column.astype(f32), 0).astype(bf16).reshape(2, 8, PIECE)
    kept = lax.dynamic_index_in_dim(total, core, 0, keepdims=False)
    came = shift(lax.dynamic_index_in_dim(total, 1 - core, 0, keepdims=False), "core", 2, 1)
    pair = jnp.where(core == 0, jnp.concatenate([kept, came], 1), jnp.concatenate([came, kept], 1))
    back = [pair] + [shift(pair, "x", 4, s) for s in (1, 2, 3)]
    ring = jnp.stack([back[i] for i in (3, 2, 1, 0, 3, 2, 1)])
    return lax.dynamic_slice_in_dim(ring, 3 - x, 4, 0).astype(f32).transpose(1, 0, 2).reshape(8, WIDTH)


def per_device(
    member_fields, weight_first, weight_second, weight_head,
    neighbours_fine, neighbours_mid, parents_fine, parents_mid, observations,
):
    core, x = lax.axis_index("core"), lax.axis_index("x")
    place = jnp.stack([core, lax.axis_index("z_hi")]).astype(jnp.int32)
    x0 = member_fields[0]
    parents_fine = parents_fine.reshape(1, CELLS_IN)
    parents_mid = parents_mid.reshape(1, CELLS_MID)
    truth = jnp.pad(observations[0], ((0, FIELD_ROWS - FIELDS), (0, 0)))
    truth = jnp.concatenate([truth] * LOCAL, 1)

    mine, other = gather_weights(weight_first, weight_second, weight_head, core, x)
    tiles = fine_tiles(x0.reshape(LOCAL * CHANNELS, CELLS_IN), neighbours_fine[1:].reshape(SLOTS - 1, 1, CELLS_IN))
    slope1, w, tiles_mid, slope2, x2, pred = forward(
        place, mine, other, x0, tiles, parents_fine, neighbours_mid, parents_mid
    )
    cohort = lax.all_to_all(jnp.broadcast_to(pred, (MEMBERS // LOCAL,) + pred.shape), MEM, 0, 0)
    parts = backward(
        cohort, pred, truth, w, tiles_mid, slope2, x2, slope1, x0, tiles, parents_fine, neighbours_mid, parents_mid
    )
    rows = reduce_gradients(parts, core, x)
    return (
        rows[:, :SECOND_AT].reshape(8, SLOTS, CHANNELS).transpose(1, 0, 2),
        rows[:, SECOND_AT:HEAD_AT].reshape(8, SLOTS, CHANNELS).transpose(1, 0, 2),
        rows[:, HEAD_AT : HEAD_AT + FIELDS].T,
    )


def solution(mesh):
    fine_mesh = Mesh(mesh.devices.reshape(2, 4, 4, 4, 2), ("z_lo", "x", "z_hi", "y", "core"))
    placed = (
        P(DP, MEM, None, None),
        P(None, DP, None),
        P(None, DP, None),
        P(None, DP),
        P(),
        P(),
        P(),
        P(),
        P(DP, None, None),
    )
    return jax.shard_map(
        per_device,
        mesh=fine_mesh,
        in_specs=placed,
        out_specs=(P(None, DP, None), P(None, DP, None), P(None, DP)),
        check_vma=False,
    )
```

time: 704 us -> 141 us (0.20); the launches traced: 690 us -> 141 us
  blocking collectives: 306 us -> 55.7 us
  other arithmetic: 199 us -> 2.06 us
  local copies, waits for them, and re-layouts: 115 us -> 10.3 us
  matrix products: 35.3 us -> 0 us
  Pallas kernels: 0 us -> 32.8 us
  between operations: 15.9 us -> 0.85 us
  waiting for transfers between devices: 8.39 us -> 19.6 us
  starting transfers between devices: 10.1 us -> 19.4 us
    unnamed x1 -> x0, blocking collectives: 139 us -> none
    all_gather x3 -> x0, blocking collectives: 136 us -> none  [the longest x1 53.9 us: per_device(): lax.all_gather(weight_first, 'dp', axis=1, tiled=True)]
    scatter-add x1 -> x0, other arithmetic: 123 us -> none  [conv_input_grad(): start_value.at[:, :, jnp.maximum(neighbours, 0).reshape(-1)]]
    mul x14 -> x0, other arithmetic: 63.3 us -> none  [build_tiles(): jnp.take(fields, jnp.maximum(neighbours[direction], 0), axis=2)]
    all_to_all x0 -> x3, blocking collectives: none -> 55.7 us  [the longest x1 21.1 us: gather_weights(): lax.all_to_all(jnp.broadcast_to(column, (16,) + column.shape), ('x', 'y')...]
    gather x17 -> x0, local copies, waits for them, and re-layouts: 54.7 us -> none  [the longest x14 41.8 us: build_tiles(): jnp.take(fields, jnp.maximum(neighbours[direction], 0), axis=2)]
    mul x15 -> x0, local copies, waits for them, and re-layouts: 37.8 us -> none  [the longest x14 37.6 us: build_tiles(): jnp.take(fields, jnp.maximum(neighbours[direction], 0), axis=2)]
    dot_general x34 -> x0, matrix products: 35.3 us -> none  [the longest x14 25.6 us: conv_forward(): jnp.einsum('oi,min->mon', weight[direction], tiles[direction], preferred_...]
  transfers between devices with their start and end apart: 4 -> 11, of which waited for: 2 -> 7; matrix products, arithmetic and copies ran while one was open for 22% -> 0% of each run, Pallas kernels for 0% -> 6%
where the time goes in v1:
time: 141 us
  blocking collectives  55.7 us (40%)
  Pallas kernels  32.8 us (23%)
  waiting for transfers between devices  19.6 us (14%)
  starting transfers between devices  19.4 us (14%)
  local copies, waits for them, and re-layouts  10.3 us (7%)
  other arithmetic  2.06 us (1%)
    all_to_all x1, blocking collectives, gather_weights(): lax.all_to_all(jnp.broadcast_to(column, (16,) + column.shape), ('x', 'y')...  21.1 us
    all_to_all x1, blocking collectives, reduce_gradients(): plane = lax.all_to_all(total.reshape(16, 4, 16, PIECE), ('x', 'y'), 0, 0)  20.5 us
    all_to_all x1, blocking collectives, reduce_gradients(): column = lax.all_to_all(column, ('z_hi', 'z_lo'), 0, 0)  14.1 us
    ppermute x10, starting transfers between devices, shift(): return lax.ppermute(v, axis, [(i, (i + by) % n) for i in range(n)])  14 us
    ppermute x10, waiting for transfers between devices, shift(): return lax.ppermute(v, axis, [(i, (i + by) % n) for i in range(n)])  13.9 us
    pallas_call x1, Pallas kernels, forward(): pl.pallas_call(forward_kernel, grid=(LOCAL, CELLS_IN // chunk), in_specs=...  12.4 us
    pallas_call x1, Pallas kernels, backward(): pl.pallas_call(backward_kernel, grid=(SLOTS,), in_specs=[whole(*cohort.sh...  11.8 us
    pallas_call x1, Pallas kernels, fine_tiles(): pl.pallas_call(tiles_kernel, grid=(SLOTS - 1,), in_specs=[pl.BlockSpec((L...  8.64 us
  transfers between devices with their start and end apart: 11, of which 7 were waited for; matrix products, arithmetic and copies ran while one was open for 0% of the time, Pallas kernels for 6%

profile of v1, /device:TPU:6, one launch (start us, length us, event | category | flops | bytes accessed | tf_op | source)
XLA Modules:
  0.0 140.7 jit_solution(10847947218797907880)
XLA Ops:
  0.7 0.9 concatenate.60
  1.8 1.2 collective-permute-done
  2.9 6.3 %collective-permute-start.3 = (bf16[16,512]{1,0:T(8,128)(2,1)S(1)}, bf16[16,512]{1,0:T(8,128)(2,1)S(1)}, u32[]{:S(2)}, u32[]{:S(2)}) collective-permute-start(bf16[16,512]{1,0:T(8,128)(2,1)S(1)} %maximum_select_fusion.1), channel_id=1, source_target_pairs={{0,24},{8,0},{16,8},{24,16},{1,25},{9,1},{17,9},{25,17},{2,26},{10... | collective-permute-start | bytes 49160 | tf_op jit(solution)/shard_map/ppermute | solution.py:246
  9.2 1.0 collective-permute-start.2
  10.2 2.8 %collective-permute-start.1 = (bf16[16,512]{1,0:T(8,128)(2,1)S(1)}, bf16[16,512]{1,0:T(8,128)(2,1)S(1)}, u32[]{:S(2)}, u32[]{:S(2)}) collective-permute-start(bf16[16,512]{1,0:T(8,128)(2,1)S(1)} %maximum_select_fusion.1), channel_id=1, source_target_pairs={{0,8},{8,16},{16,24},{24,0},{1,9},{9,17},{17,25},{25,1},{2,10},{10... | collective-permute-start | bytes 49160 | tf_op jit(solution)/shard_map/ppermute | solution.py:246
  13.1 3.9 %collective-permute-done.2 = bf16[16,512]{1,0:T(8,128)(2,1)S(1)} collective-permute-done((bf16[16,512]{1,0:T(8,128)(2,1)S(1)}, bf16[16,512]{1,0:T(8,128)(2,1)S(1)}, u32[]{:S(2)}, u32[]{:S(2)}) %collective-permute-start.2) | collective-permute-done | bytes 16416 | tf_op jit(solution)/shard_map/ppermute | solution.py:246
  17.1 21.1 %all_to_all.20.mine_ref = bf16[16,4,16,512]{3,2,1,0:T(8,128)(2,1)S(1)} all-to-all(bf16[16,4,16,512]{3,2,1,0:T(8,128)(2,1)S(1)} %broadcast_in_dim.16), channel_id=1, replica_groups=mesh['z_lo'=2,'x'=4,'z_hi'=4,'y'=4,'core'=2] {'x','y'}, dimensions={0} | all-to-all | bytes 2097152 | tf_op jit(solution)/shard_map/all_to_all | solution.py:266
  38.3 8.6 %fine_tiles.1.tiles_ref = bf16[2,6,256,1024]{3,2,1,0:T(8,128)(2,1)} custom-call(bf16[512,1024]{1,0:T(8,128)(2,1)S(1)} %bitcast.51, s32[6,1,1024]{2,1,0:T(1,128)S(1)} %reshape.153.nb_ref), custom_call_target="tpu_custom_call" | custom-call | flops 6499999744 | bytes 8000000 | tf_op jit(solution)/shard_map/fine_tiles/pallas_call | solution.py:60
  47.0 1.0 copy-done.7
  48.0 1.2 copy-done.8
  49.2 12.4 %forward.1 = (bf16[2,256,1024]{2,1,0:T(8,128)(2,1)S(1)}, bf16[256,4096]{1,0:T(8,128)(2,1)}, bf16[2,1792,256]{2,1,0:T(8,128)(2,1)}, f32[2,256,256]{2,1,0:T(8,128)...) custom-call(s32[2]{0:T(128)S(1)} %pad_add_fusion.place_ref, bf16[16,4,16,512]{3,2,1,0:T(8,128)(2,1)S(1)} %all_to_all.20.mine_ref, ...), custom_call_target="tpu_custom_call" | custom-call | flops 3200000000 | bytes 14000000 | tf_op jit(solution)/shard_map/forward/pallas_call | solution.py:131
  61.6 0.8 copy-done.2
  62.4 0.7 broadcast_in_dim.17
  63.1 5.5 %all-to-all-start.1 = ((f32[8,72,128]{2,1,0:T(8,128)}), f32[8,72,128]{2,1,0:T(8,128)S(1)}, u32[]{:S(2)}, u32[]{:S(2)}) async-start(f32[8,72,128]{2,1,0:T(8,128)} %broadcast_in_dim.17), calls=%async_computation.1 | async-start | bytes 589824 | tf_op jit(solution)/shard_map/all_to_all | solution.py:304
  68.8 5.8 %all-to-all-done.1.cohort_ref = f32[8,72,128]{2,1,0:T(8,128)S(1)} async-done(((f32[8,72,128]{2,1,0:T(8,128)}), f32[8,72,128]{2,1,0:T(8,128)S(1)}, u32[]{:S(2)}, u32[]{:S(2)}) %all-to-all-start.1) | async-done | bytes 294944 | tf_op jit(solution)/shard_map/all_to_all | solution.py:304
  74.6 1.5 %copy-done = bf16[2,1792,256]{2,1,0:T(8,128)(2,1)S(1)} copy-done((bf16[2,1792,256]{2,1,0:T(8,128)(2,1)S(1)}, bf16[2,1792,256]{2,1,0:T(8,128)(2,1)}, u32[]{:S(2)}) %copy-start) | copy-done | bytes 1835032
  76.1 1.0 copy-done.3
  77.1 11.8 %backward.1 = bf16[2,4,4,4,16,512]{5,4,3,2,1,0:T(8,128)(2,1)} custom-call(f32[8,72,128]{2,1,0:T(8,128)S(1)} %all-to-all-done.1.cohort_ref, f32[72,128]{1,0:T(8,128)S(1)} %get-tuple-element.9.own_ref, f32[72,128]{1,0:T(8,128)S(1)} %pad_maximum_fusion.1.obs_ref, bf16[256,4096]{1,0:T(8,128)(2,1)} %get-tuple-element.10.w_ref, bf16[2,1792,256]{2,1,0:T(8,128)(2,1)S(1)} %copy-done, ...), custom_call_target="tpu_custom_call" | custom-call | flops 4000000000 | bytes 16000000 | tf_op jit(solution)/shard_map/backward/pallas_call | solution.py:227
  88.9 1.5 %dynamic-slice_bitcast_fusion = bf16[4,4,4,16,512]{4,3,2,1,0:T(8,128)(2,1)S(1)} fusion(bf16[2,4,4,4,16,512]{5,4,3,2,1,0:T(8,128)(2,1)} %backward.1, s32[]{:T(128)S(6)} %select_n.78), kind=kLoop, calls=%fused_computation.2 | loop fusion | bytes 2097156 | tf_op jit(solution)/shard_map/jit(dynamic_index_in_dim)/squeeze | solution.py:272
  90.4 2.8 %collective-permute-done.5 = bf16[4,4,4,16,512]{4,3,2,1,0:T(8,128)(2,1)} collective-permute-done((bf16[4,4,4,16,512]{4,3,2,1,0:T(8,128)(2,1)S(1)}, bf16[4,4,4,16,512]{4,3,2,1,0:T(8,128)(2,1)}, u32[]{:S(2)}, u32[]{:S(2)}) %collective-permute-start.5) | collective-permute-done | bytes 1048608 | tf_op jit(solution)/shard_map/ppermute | solution.py:246
  93.2 1.6 %fusion = bf16[4,4,4,16,512]{4,3,2,1,0:T(8,128)(2,1)S(1)} fusion(bf16[4,4,4,16,512]{4,3,2,1,0:T(8,128)(2,1)} %collective-permute-done.5, bf16[2,4,4,4,16,512]{5,4,3,2,1,0:T(8,128)(2,1)S(1)} %copy-done.9, s32[]{:T(128)S(6)} %select_n.77), kind=kLoop, calls=%fused_computation.1 | loop fusion | flops 2097152 | bytes 3145732 | tf_op jit(solution)/shard_map/convert_element_type | solution.py:273
  94.8 20.5 %all_to_all.21 = bf16[16,4,16,512]{3,2,1,0:T(8,128)(2,1)S(1)} all-to-all(bf16[16,4,16,512]{3,2,1,0:T(8,128)(2,1)S(1)} %bitcast.58), channel_id=1, replica_groups=mesh['z_lo'=2,'x'=4,'z_hi'=4,'y'=4,'core'=2] {'x','y'}, dimensions={0} | all-to-all | bytes 2097152 | tf_op jit(solution)/shard_map/all_to_all | solution.py:274
  115.3 0.2 reduce_sum.24
  115.6 14.1 %all_to_all.22 = bf16[8,16,512]{2,1,0:T(8,128)(2,1)S(1)} all-to-all(bf16[8,16,512]{2,1,0:T(8,128)(2,1)S(1)} %bitcast.59), channel_id=1, replica_groups=mesh['z_lo'=2,'x'=4,'z_hi'=4,'y'=4,'core'=2] {'z_hi','z_lo'}, dimensions={0} | all-to-all | bytes 262144 | tf_op jit(solution)/shard_map/all_to_all | solution.py:277
  129.8 1.2 collective-permute-done.6
  130.9 0.5 collective-permute-start.7
  131.5 2.7 %collective-permute-start.9 = (bf16[8,1024]{1,0:T(8,128)(2,1)S(1)}, bf16[8,1024]{1,0:T(8,128)(2,1)S(1)}, u32[]{:S(2)}, u32[]{:S(2)}) collective-permute-start(bf16[8,1024]{1,0:T(8,128)(2,1)S(1)} %maximum_select_fusion.2), channel_id=1, source_target_pairs={{0,32},{32,64},{64,96},{96,0},{1,33},{33,65},{65,97},{97,1},{2,34}... | collective-permute-start | bytes 49160 | tf_op jit(solution)/shard_map/ppermute | solution.py:246
  134.2 0.4 collective-permute-start.8
  134.5 1.4 collective-permute-done.7
  135.9 3.5 %collective-permute-done.8 = bf16[8,1024]{1,0:T(8,128)(2,1)S(1)} collective-permute-done((bf16[8,1024]{1,0:T(8,128)(2,1)S(1)}, bf16[8,1024]{1,0:T(8,128)(2,1)S(1)}, u32[]{:S(2)}, u32[]{:S(2)}) %collective-permute-start.8) | collective-permute-done | bytes 16416 | tf_op jit(solution)/shard_map/ppermute | solution.py:246
  139.5 0.6 slice_bitcast_fusion
  140.1 0.6 fusion.2
  (51 shorter events, 0.9 us)
Async XLA Ops:
  0.6 37.6 %copy-start.10 = (s32[7,1024]{1,0:T(8,128)S(1)}, s32[7,1024]{1,0:T(8,128)}, u32[]{:S(2)}) copy-start(s32[7,1024]{1,0:T(8,128)} %param.13) | copy-start | bytes 86020
  0.6 37.7 %copy-start.1 = (bf16[1,2,256,1024]{3,2,1,0:T(8,128)(2,1)S(1)}, bf16[1,2,256,1024]{3,2,1,0:T(8,128)(2,1)}, u32[]{:S(2)}) copy-start(bf16[1,2,256,1024]{3,2,1,0:T(8,128)(2,1)} %param.9) | copy-start | bytes 3145732
  1.7 1.2 collective-permute-start
  2.9 10.1 %collective-permute-start.3 = (bf16[16,512]{1,0:T(8,128)(2,1)S(1)}, bf16[16,512]{1,0:T(8,128)(2,1)S(1)}, u32[]{:S(2)}, u32[]{:S(2)}) collective-permute-start(bf16[16,512]{1,0:T(8,128)(2,1)S(1)} %maximum_select_fusion.1), channel_id=1, source_target_pairs={{0,24},{8,0},{16,8},{24,16},{1,25},{9,1},{17,9},{25,17},{2,26},{10... | collective-permute-start | bytes 49160 | tf_op jit(solution)/shard_map/ppermute | solution.py:246
  9.2 7.7 %collective-permute-start.2 = (bf16[16,512]{1,0:T(8,128)(2,1)S(1)}, bf16[16,512]{1,0:T(8,128)(2,1)S(1)}, u32[]{:S(2)}, u32[]{:S(2)}) collective-permute-start(bf16[16,512]{1,0:T(8,128)(2,1)S(1)} %maximum_select_fusion.1), channel_id=1, source_target_pairs={{0,16},{8,24},{16,0},{24,8},{1,17},{9,25},{17,1},{25,9},{2,18},{10... | collective-permute-start | bytes 49160 | tf_op jit(solution)/shard_map/ppermute | solution.py:246
  10.2 6.7 %collective-permute-start.1 = (bf16[16,512]{1,0:T(8,128)(2,1)S(1)}, bf16[16,512]{1,0:T(8,128)(2,1)S(1)}, u32[]{:S(2)}, u32[]{:S(2)}) collective-permute-start(bf16[16,512]{1,0:T(8,128)(2,1)S(1)} %maximum_select_fusion.1), channel_id=1, source_target_pairs={{0,8},{8,16},{16,24},{24,0},{1,9},{9,17},{17,25},{25,1},{2,10},{10... | collective-permute-start | bytes 49160 | tf_op jit(solution)/shard_map/ppermute | solution.py:246
  38.2 8.8 %collective-permute-start.4 = (bf16[16,4,16,512]{3,2,1,0:T(8,128)(2,1)S(1)}, bf16[16,4,16,512]{3,2,1,0:T(8,128)(2,1)S(1)}, u32[]{:S(2)}, u32[]{:S(2)}) collective-permute-start(bf16[16,4,16,512]{3,2,1,0:T(8,128)(2,1)S(1)} %all_to_all.20.mine_ref), channel_id=1, source_target_pairs={{0,1},{1,0},{2,3},{3,2},{4,5},{5,4},{6,7},{7,6},{8,9},{9,8},{10,11... | collective-permute-start | bytes 3145736 | tf_op jit(solution)/shard_map/ppermute | solution.py:246
  38.3 9.6 %copy-start.4 = (s32[7,256]{1,0:T(8,128)S(1)}, s32[7,256]{1,0:T(8,128)}, u32[]{:S(2)}) copy-start(s32[7,256]{1,0:T(8,128)} %nb_mid_ref.3) | copy-start | bytes 21508
  38.3 9.6 %copy-start.5 = (s32[1024]{0:T(1024)S(1)}, s32[1024]{0:T(1024)}, u32[]{:S(2)}) copy-start(s32[1024]{0:T(1024)} %param.15) | copy-start | bytes 12292
  38.3 9.6 %copy-start.6 = (s32[256]{0:T(256)S(1)}, s32[256]{0:T(256)}, u32[]{:S(2)}) copy-start(s32[256]{0:T(256)} %param.16) | copy-start | bytes 3076
  47.0 1.0 copy-start.7
  48.0 1.2 copy-start.8
  49.2 19.4 %copy-start.11 = (f32[1,69,64]{1,2,0:T(8,128)S(1)}, f32[1,69,64]{1,2,0:T(8,128)}, u32[]{:S(2)}) copy-start(f32[1,69,64]{1,2,0:T(8,128)} %param.17) | copy-start | bytes 52996
  61.6 0.8 copy-start.2
  63.1 11.4 %all-to-all-start.1 = ((f32[8,72,128]{2,1,0:T(8,128)}), f32[8,72,128]{2,1,0:T(8,128)S(1)}, u32[]{:S(2)}, u32[]{:S(2)}) async-start(f32[8,72,128]{2,1,0:T(8,128)} %broadcast_in_dim.17), calls=%async_computation.1 | async-start | bytes 589824 | tf_op jit(solution)/shard_map/all_to_all | solution.py:304
  74.6 1.5 %copy-start = (bf16[2,1792,256]{2,1,0:T(8,128)(2,1)S(1)}, bf16[2,1792,256]{2,1,0:T(8,128)(2,1)}, u32[]{:S(2)}) copy-start(bf16[2,1792,256]{2,1,0:T(8,128)(2,1)} %get-tuple-element.11.tiles_mid_ref) | copy-start | bytes 5505028
  76.1 1.0 copy-start.3
  88.9 4.4 %copy-start.9 = (bf16[2,4,4,4,16,512]{5,4,3,2,1,0:T(8,128)(2,1)S(1)}, bf16[2,4,4,4,16,512]{5,4,3,2,1,0:T(8,128)(2,1)}, u32[]{:S(2)}) copy-start(bf16[2,4,4,4,16,512]{5,4,3,2,1,0:T(8,128)(2,1)} %backward.1) | copy-start | bytes 6291460
  90.3 2.9 %collective-permute-start.5 = (bf16[4,4,4,16,512]{4,3,2,1,0:T(8,128)(2,1)S(1)}, bf16[4,4,4,16,512]{4,3,2,1,0:T(8,128)(2,1)}, u32[]{:S(2)}, u32[]{:S(2)}) collective-permute-start(bf16[4,4,4,16,512]{4,3,2,1,0:T(8,128)(2,1)S(1)} %dynamic-slice_bitcast_fusion), channel_id=1, source_target_pairs={{0,1},{1,0},{2,3},{3,2},{4,5},{5,4},{6,7},{7,6},{8,9},{9,8},{10,11... | collective-permute-start | bytes 3145736 | tf_op jit(solution)/shard_map/ppermute | solution.py:246
  129.7 1.3 collective-permute-start.6
  130.9 4.9 %collective-permute-start.7 = (bf16[8,1024]{1,0:T(8,128)(2,1)S(1)}, bf16[8,1024]{1,0:T(8,128)(2,1)S(1)}, u32[]{:S(2)}, u32[]{:S(2)}) collective-permute-start(bf16[8,1024]{1,0:T(8,128)(2,1)S(1)} %maximum_select_fusion.2), channel_id=1, source_target_pairs={{0,96},{32,0},{64,32},{96,64},{1,97},{33,1},{65,33},{97,65},{2,98}... | collective-permute-start | bytes 49160 | tf_op jit(solution)/shard_map/ppermute | solution.py:246
  131.5 8.0 %collective-permute-start.9 = (bf16[8,1024]{1,0:T(8,128)(2,1)S(1)}, bf16[8,1024]{1,0:T(8,128)(2,1)S(1)}, u32[]{:S(2)}, u32[]{:S(2)}) collective-permute-start(bf16[8,1024]{1,0:T(8,128)(2,1)S(1)} %maximum_select_fusion.2), channel_id=1, source_target_pairs={{0,32},{32,64},{64,96},{96,0},{1,33},{33,65},{65,97},{97,1},{2,34}... | collective-permute-start | bytes 49160 | tf_op jit(solution)/shard_map/ppermute | solution.py:246
  134.2 5.2 %collective-permute-start.8 = (bf16[8,1024]{1,0:T(8,128)(2,1)S(1)}, bf16[8,1024]{1,0:T(8,128)(2,1)S(1)}, u32[]{:S(2)}, u32[]{:S(2)}) collective-permute-start(bf16[8,1024]{1,0:T(8,128)(2,1)S(1)} %maximum_select_fusion.2), channel_id=1, source_target_pairs={{0,64},{32,96},{64,0},{96,32},{1,65},{33,97},{65,1},{97,33},{2,66}... | collective-permute-start | bytes 49160 | tf_op jit(solution)/shard_map/ppermute | solution.py:246

commit v2 on v1

--- a/solution.py
+++ b/solution.py
@@ -21,13 +21,13 @@
 CELLS_IN = 1024
 SAMPLES = 32
 LOCAL = 2
-PIECE = 512
+QUARTER = 1024
 SMOOTH = 0.0001
 NORM = MEMBERS / math.sqrt(SAMPLES * CELLS_OUT)
 SECOND_AT = SLOTS * CHANNELS
 HEAD_AT = 2 * SLOTS * CHANNELS
 WIDTH = 4096
-VMEM_BYTES = 48 * 1024 * 1024
+MIB = 1024 * 1024
 
 f32 = jnp.float32
 bf16 = jnp.bfloat16
@@ -51,7 +51,8 @@
 
 
 def tiles_kernel(x_ref, nb_ref, out_ref):
-    tile = dot(x_ref[...], one_hot(nb_ref[0], CELLS_IN)).astype(bf16)
+    row = nb_ref[pl.ds(pl.program_id(0) + 1, 1), :]
+    tile = dot(x_ref[...], one_hot(row, CELLS_IN)).astype(bf16)
     for m in range(LOCAL):
         out_ref[m, 0] = tile[m * CHANNELS : (m + 1) * CHANNELS]
 
@@ -62,11 +63,11 @@
         grid=(SLOTS - 1,),
         in_specs=[
             pl.BlockSpec((LOCAL * CHANNELS, CELLS_IN), lambda j: (0, 0)),
-            pl.BlockSpec((1, 1, CELLS_IN), lambda j: (j, 0, 0)),
+            pl.BlockSpec((SLOTS, CELLS_IN), lambda j: (0, 0)),
         ],
         out_specs=pl.BlockSpec((LOCAL, 1, CHANNELS, CELLS_IN), lambda j: (0, j, 0, 0)),
         out_shape=jax.ShapeDtypeStruct((LOCAL, SLOTS - 1, CHANNELS, CELLS_IN), bf16),
-        compiler_params=pltpu.CompilerParams(vmem_limit_bytes=VMEM_BYTES),
+        compiler_params=pltpu.CompilerParams(vmem_limit_bytes=56 * MIB),
         cost_estimate=pl.CostEstimate(flops=6_500_000_000, bytes_accessed=8_000_000, transcendentals=0),
         name="fine_tiles",
     )(x0, nb)
@@ -80,14 +81,14 @@
 
     @pl.when((m == 0) & (k == 0))
     def _():
-        core, z = place_ref[0], place_ref[1]
-        for source, here in ((mine_ref, core), (other_ref, 1 - core)):
-            for x in range(4):
-                column = pl.multiple_of(x * 2 * PIECE + here * PIECE, PIECE)
-                for y in range(4):
-                    for back in range(4):
-                        row = pl.multiple_of((lax.rem(z - back + 4, 4) * 4 + y) * 16, 16)
-                        w_ref[pl.ds(row, 16), pl.ds(column, PIECE)] = source[x * 4 + y, back]
+        first, z = place_ref[0] == 0, place_ref[1]
+        for x in range(4):
+            for y in range(4):
+                for back in range(4):
+                    mine, other = mine_ref[x * 4 + y, back].astype(f32), other_ref[x * 4 + y, back].astype(f32)
+                    pair = jnp.concatenate([jnp.where(first, mine, other), jnp.where(first, other, mine)], 0)
+                    row = pl.multiple_of((lax.rem(z - back + 4, 4) * 4 + y) * 16, 16)
+                    w_ref[pl.ds(row, 16), x * QUARTER : (x + 1) * QUARTER] = pair.astype(bf16)
 
     a1 = dot(w_ref[:, 0:CHANNELS], x_ref[0])
     for j in range(1, SLOTS):
@@ -125,6 +126,39 @@
         pred_ref[...] = pred[0:FIELD_ROWS]
 
 
+def spread_kernel(own_ref, back1_ref, back2_ref, back3_ref, out_ref):
+    for block in range(16):
+        for back, source in enumerate((own_ref, back1_ref, back2_ref, back3_ref)):
+            out_ref[block, back] = source[...]
+
+
+def spread(pieces):
+    return pl.pallas_call(
+        spread_kernel,
+        in_specs=[pl.BlockSpec(memory_space=pltpu.VMEM)] * 4,
+        out_specs=pl.BlockSpec(memory_space=pltpu.VMEM),
+        out_shape=jax.ShapeDtypeStruct((16, 4, 8, QUARTER), bf16),
+        compiler_params=pltpu.CompilerParams(vmem_limit_bytes=8 * MIB),
+        name="spread",
+    )(*pieces)
+
+
+def after_kernel(value_ref, first_ref, out_ref):
+    del value_ref, first_ref, out_ref
+
+
+def after(value, first):
+    return pl.pallas_call(
+        after_kernel,
+        in_specs=[pl.BlockSpec(memory_space=pl.ANY)] * 2,
+        out_specs=pl.BlockSpec(memory_space=pl.ANY),
+        out_shape=jax.ShapeDtypeStruct(value.shape, value.dtype),
+        input_output_aliases={0: 0},
+        compiler_params=pltpu.CompilerParams(vmem_limit_bytes=48 * MIB),
+        name="after",
+    )(value, first)
+
+
 def forward(place, mine, other, x0, tiles, parents_fine, nb_mid, parents_mid):
     chunk = 256
     whole = lambda *shape: pl.BlockSpec(shape, lambda m, k: (0,) * len(shape))
@@ -133,8 +167,8 @@
         grid=(LOCAL, CELLS_IN // chunk),
         in_specs=[
             pl.BlockSpec(memory_space=pltpu.SMEM),
-            whole(16, 4, 16, PIECE),
-            whole(16, 4, 16, PIECE),
+            whole(16, 4, 8, QUARTER),
+            whole(16, 4, 8, QUARTER),
             pl.BlockSpec((1, CHANNELS, chunk), lambda m, k: (m, 0, k)),
             pl.BlockSpec((1, SLOTS - 1, CHANNELS, chunk), lambda m, k: (m, 0, 0, k)),
             pl.BlockSpec((1, chunk), lambda m, k: (0, k)),
@@ -150,15 +184,15 @@
             whole(FIELD_ROWS, LOCAL * CELLS_OUT),
         ],
         out_shape=[
-            jax.ShapeDtypeStruct((LOCAL, CHANNELS, CELLS_IN), bf16),
-            jax.ShapeDtypeStruct((CHANNELS, WIDTH), bf16),
-            jax.ShapeDtypeStruct((LOCAL, SECOND_AT, CELLS_MID), bf16),
-            jax.ShapeDtypeStruct((LOCAL, CHANNELS, CELLS_MID), f32),
+            pltpu.HBM((LOCAL, CHANNELS, CELLS_IN), bf16),
+            pltpu.HBM((CHANNELS, WIDTH), bf16),
+            pltpu.HBM((LOCAL, SECOND_AT, CELLS_MID), bf16),
+            pltpu.HBM((LOCAL, CHANNELS, CELLS_MID), f32),
             jax.ShapeDtypeStruct((CHANNELS, LOCAL * CELLS_OUT), bf16),
             jax.ShapeDtypeStruct((FIELD_ROWS, LOCAL * CELLS_OUT), f32),
         ],
         scratch_shapes=[pltpu.VMEM((LOCAL, CHANNELS, CELLS_MID), f32)],
-        compiler_params=pltpu.CompilerParams(vmem_limit_bytes=VMEM_BYTES),
+        compiler_params=pltpu.CompilerParams(vmem_limit_bytes=48 * MIB),
         cost_estimate=pl.CostEstimate(flops=3_200_000_000, bytes_accessed=14_000_000, transcendentals=700_000),
         name="forward",
     )(place, mine, other, x0, tiles, parents_fine, nb_mid, parents_mid)
@@ -169,29 +203,34 @@
 
 
 def backward_kernel(
-    cohort_ref, own_ref, obs_ref, w_ref, tiles_mid_ref, slope2_ref, x2_ref, slope1_ref, x_ref, tiles_ref,
-    parents_ref, nb_mid_ref, parents_mid_ref, out_ref, g1_ref,
+    place_ref, cohort0_ref, cohort1_ref, cohort2_ref, cohort3_ref, own_ref, obs_ref, w_ref, tiles_mid_ref, slope2_ref, x2_ref, slope1_ref, x_ref, tiles_ref,
+    parents_ref, nb_mid_ref, parents_mid_ref, kept_ref, sent_ref, g1_ref,
 ):
     j = pl.program_id(0)
-
-    def put(piece, half, lanes, value):
+    first = place_ref[0] == 0
+    cohort_refs = (cohort0_ref, cohort1_ref, cohort2_ref, cohort3_ref)
+
+    def put(quarter, at, lanes, value):
         for z in range(4):
             for y in range(4):
                 row = (z * 4 + y) * 16
-                out_ref[lax.rem(piece, 2), lax.div(piece, 2), y, z, :, pl.ds(half, lanes)] = value[row : row + 16].astype(bf16)
+                low, high = value[row : row + 8], value[row + 8 : row + 16]
+                kept_ref[quarter, y, z, :, pl.ds(at, lanes)] = jnp.where(first, low, high).astype(bf16)
+                sent_ref[quarter, y, z, :, pl.ds(at, lanes)] = jnp.where(first, high, low).astype(bf16)
 
     @pl.when(j == 0)
     def _():
         own = own_ref[...]
         spread = jnp.zeros_like(own)
-        for peer in range(MEMBERS // LOCAL):
-            theirs = cohort_ref[peer]
-            spread = spread + sign_smooth(own - theirs) + sign_smooth(own - pltpu.roll(theirs, CELLS_OUT, 1))
+        for pair_ref in cohort_refs:
+            for peer in range(2):
+                theirs = pair_ref[peer]
+                spread = spread + sign_smooth(own - theirs) + sign_smooth(own - pltpu.roll(theirs, CELLS_OUT, 1))
         skill = sign_smooth(own - obs_ref[...])
         slope = NORM * (skill / MEMBERS - spread / (MEMBERS * (MEMBERS - 1)))
         slope = jnp.concatenate([slope, jnp.zeros((128 - FIELD_ROWS, 128), f32)], 0).astype(bf16)
-        put(7, 0, 128, dot_bt(x2_ref[...], slope))
-        put(7, 128, PIECE - 128, jnp.zeros((CHANNELS, PIECE - 128), f32))
+        put(3, 512, 128, dot_bt(x2_ref[...], slope))
+        put(3, 640, 384, jnp.zeros((CHANNELS, 384), f32))
         pool = one_hot(parents_mid_ref[...], CELLS_OUT)
         head_t = w_ref[:, HEAD_AT : HEAD_AT + 128]
         dh2, g2 = [], []
@@ -202,7 +241,7 @@
         for q in range(SLOTS):
             rows = slice(q * CHANNELS, (q + 1) * CHANNELS)
             grad = dot_bt(g2[0], tiles_mid_ref[0, rows]) + dot_bt(g2[1], tiles_mid_ref[1, rows])
-            put((SLOTS + q) // 2, (SLOTS + q) % 2 * 256, 256, grad)
+            put((SLOTS + q) // 4, (SLOTS + q) % 4 * 256, 256, grad)
         both = jnp.concatenate(g2, 0)
         back = [dh2[i] + dot_at(w_ref[:, SECOND_AT : SECOND_AT + CHANNELS], g2[i]) for i in range(LOCAL)]
         for q in range(1, SLOTS):
@@ -219,34 +258,34 @@
     @pl.when(j > 0)
     def _():
         grad = dot_bt(g1_ref[0], tiles_ref[0, 0]) + dot_bt(g1_ref[1], tiles_ref[1, 0])
-        put(lax.div(j, 2), pl.multiple_of(lax.rem(j, 2) * 256, 256), 256, grad)
-
-
-def backward(cohort, own, obs, w, tiles_mid, slope2, x2, slope1, x0, tiles, parents_fine, nb_mid, parents_mid):
+        put(lax.div(j, 4), pl.multiple_of(lax.rem(j, 4) * 256, 256), 256, grad)
+
+
+def backward(place, cohort, own, obs, w, tiles_mid, slope2, x2, slope1, x0, tiles, parents_fine, nb_mid, parents_mid):
     whole = lambda *shape: pl.BlockSpec(shape, lambda j: (0,) * len(shape))
     return pl.pallas_call(
         backward_kernel,
         grid=(SLOTS,),
         in_specs=[
-            whole(*cohort.shape), whole(*own.shape), whole(*obs.shape), whole(*w.shape), whole(*tiles_mid.shape),
+            pl.BlockSpec(memory_space=pltpu.SMEM), *[whole(*pair.shape) for pair in cohort], whole(*own.shape), whole(*obs.shape), whole(*w.shape), whole(*tiles_mid.shape),
             whole(*slope2.shape), whole(*x2.shape), whole(*slope1.shape), whole(*x0.shape),
             pl.BlockSpec((LOCAL, 1, CHANNELS, CELLS_IN), lambda j: (0, jnp.maximum(j - 1, 0), 0, 0)),
             whole(*parents_fine.shape), whole(*nb_mid.shape), whole(*parents_mid.shape),
         ],
-        out_specs=whole(2, 4, 4, 4, 16, PIECE),
-        out_shape=jax.ShapeDtypeStruct((2, 4, 4, 4, 16, PIECE), bf16),
+        out_specs=[whole(4, 4, 4, 8, QUARTER)] * 2,
+        out_shape=[jax.ShapeDtypeStruct((4, 4, 4, 8, QUARTER), bf16)] * 2,
         scratch_shapes=[pltpu.VMEM((LOCAL, CHANNELS, CELLS_IN), bf16)],
-        compiler_params=pltpu.CompilerParams(vmem_limit_bytes=VMEM_BYTES),
+        compiler_params=pltpu.CompilerParams(vmem_limit_bytes=50 * MIB),
         cost_estimate=pl.CostEstimate(flops=4_000_000_000, bytes_accessed=16_000_000, transcendentals=200_000),
         name="backward",
-    )(cohort, own, obs, w, tiles_mid, slope2, x2, slope1, x0, tiles, parents_fine, nb_mid, parents_mid)
+    )(place, *cohort, own, obs, w, tiles_mid, slope2, x2, slope1, x0, tiles, parents_fine, nb_mid, parents_mid)
 
 
 def shift(v, axis, n, by):
     return lax.ppermute(v, axis, [(i, (i + by) % n) for i in range(n)])
 
 
-def gather_weights(weight_first, weight_second, weight_head, core, x):
+def gather_weights(weight_first, weight_second, weight_head, x, tiles):
     rows = weight_first.shape[1]
     flat = jnp.concatenate(
         [
@@ -257,29 +296,20 @@
         ],
         1,
     )
-    pair = lax.dynamic_slice_in_dim(flat, x * 2 * PIECE, 2 * PIECE, 1)
-    kept = lax.dynamic_slice_in_dim(pair, core * PIECE, PIECE, 1)
-    sent = lax.dynamic_slice_in_dim(pair, (1 - core) * PIECE, PIECE, 1)
-    came = shift(sent, "core", 2, 1)
-    mine = jnp.where(core == 0, jnp.concatenate([kept, came], 0), jnp.concatenate([came, kept], 0))
-    column = jnp.stack([mine] + [shift(mine, "z_hi", 4, s) for s in (1, 2, 3)])
-    plane = lax.all_to_all(jnp.broadcast_to(column, (16,) + column.shape), ("x", "y"), 0, 0)
+    mine = lax.dynamic_slice_in_dim(flat, x * QUARTER, QUARTER, 1)
+    column = spread([mine] + [shift(mine, "z_hi", 4, s) for s in (1, 2, 3)])
+    plane = after(lax.all_to_all(column, ("x", "y"), 0, 0), tiles)
     return plane, shift(plane, "core", 2, 1)
 
 
-def reduce_gradients(parts, core, x):
-    kept = lax.dynamic_index_in_dim(parts, core, 0, keepdims=False)
-    sent = lax.dynamic_index_in_dim(parts, 1 - core, 0, keepdims=False)
+def reduce_gradients(kept, sent, x):
     total = (kept.astype(f32) + shift(sent, "core", 2, 1).astype(f32)).astype(bf16)
-    plane = lax.all_to_all(total.reshape(16, 4, 16, PIECE), ("x", "y"), 0, 0)
+    plane = lax.all_to_all(total.reshape(16, 4, 8, QUARTER), ("x", "y"), 0, 0)
     total = jnp.sum(plane.astype(f32), 0).astype(bf16)
-    column = jnp.broadcast_to(total[:, None], (4, 2, 16, PIECE)).reshape(8, 16, PIECE)
+    column = jnp.broadcast_to(total[:, None], (4, 2, 8, QUARTER)).reshape(8, 8, QUARTER)
     column = lax.all_to_all(column, ("z_hi", "z_lo"), 0, 0)
-    total = jnp.sum(column.astype(f32), 0).astype(bf16).reshape(2, 8, PIECE)
-    kept = lax.dynamic_index_in_dim(total, core, 0, keepdims=False)
-    came = shift(lax.dynamic_index_in_dim(total, 1 - core, 0, keepdims=False), "core", 2, 1)
-    pair = jnp.where(core == 0, jnp.concatenate([kept, came], 1), jnp.concatenate([came, kept], 1))
-    back = [pair] + [shift(pair, "x", 4, s) for s in (1, 2, 3)]
+    total = jnp.sum(column.astype(f32), 0).astype(bf16)
+    back = [total] + [shift(total, "x", 4, s) for s in (1, 2, 3)]
     ring = jnp.stack([back[i] for i in (3, 2, 1, 0, 3, 2, 1)])
     return lax.dynamic_slice_in_dim(ring, 3 - x, 4, 0).astype(f32).transpose(1, 0, 2).reshape(8, WIDTH)
 
@@ -296,16 +326,17 @@
     truth = jnp.pad(observations[0], ((0, FIELD_ROWS - FIELDS), (0, 0)))
     truth = jnp.concatenate([truth] * LOCAL, 1)
 
-    mine, other = gather_weights(weight_first, weight_second, weight_head, core, x)
-    tiles = fine_tiles(x0.reshape(LOCAL * CHANNELS, CELLS_IN), neighbours_fine[1:].reshape(SLOTS - 1, 1, CELLS_IN))
+    tiles = fine_tiles(x0.reshape(LOCAL * CHANNELS, CELLS_IN), neighbours_fine)
+    mine, other = gather_weights(weight_first, weight_second, weight_head, x, tiles)
     slope1, w, tiles_mid, slope2, x2, pred = forward(
         place, mine, other, x0, tiles, parents_fine, neighbours_mid, parents_mid
     )
-    cohort = lax.all_to_all(jnp.broadcast_to(pred, (MEMBERS // LOCAL,) + pred.shape), MEM, 0, 0)
-    parts = backward(
-        cohort, pred, truth, w, tiles_mid, slope2, x2, slope1, x0, tiles, parents_fine, neighbours_mid, parents_mid
-    )
-    rows = reduce_gradients(parts, core, x)
+    pair = jnp.stack([pred, shift(pred, "z_lo", 2, 1)])
+    cohort = [pair] + [shift(pair, "x", 4, s) for s in (1, 2, 3)]
+    kept, sent = backward(
+        place, cohort, pred, truth, w, tiles_mid, slope2, x2, slope1, x0, tiles, parents_fine, neighbours_mid, parents_mid
+    )
+    rows = reduce_gradients(kept, sent, x)
     return (
         rows[:, :SECOND_AT].reshape(8, SLOTS, CHANNELS).transpose(1, 0, 2),
         rows[:, SECOND_AT:HEAD_AT].reshape(8, SLOTS, CHANNELS).transpose(1, 0, 2),

time: 141 us -> 127 us (0.901)
  blocking collectives: 55.7 us -> 34.8 us
  starting transfers between devices: 19.4 us -> 26.7 us
  local copies, waits for them, and re-layouts: 10.3 us -> 4.51 us
  waiting for transfers between devices: 19.6 us -> 24.3 us
  Pallas kernels: 32.8 us -> 34.9 us
    all_to_all x2 -> x1, blocking collectives: 41.6 us -> 20.7 us  [reduce_gradients(): plane = lax.all_to_all(total.reshape(16, 4, 8, QUARTER), ('x', 'y'), 0, 0)]
    ppermute x10 -> x12, waiting for transfers between devices: 13.9 us -> 20.4 us  [shift(): return lax.ppermute(v, axis, [(i, (i + by) % n) for i in range(n)])]
    ppermute x10 -> x12, starting transfers between devices: 14 us -> 19.2 us  [shift(): return lax.ppermute(v, axis, [(i, (i + by) % n) for i in range(n)])]
    unnamed x30 -> x21, local copies, waits for them, and re-layouts: 5.69 us -> 2.39 us
    all_to_all x1, starting transfers between devices: 5.46 us -> 7.43 us  [gather_weights(): plane = after(lax.all_to_all(column, ('x', 'y'), 0, 0), tiles)]
    all_to_all x1, waiting for transfers between devices: 5.79 us -> 3.85 us  [gather_weights(): plane = after(lax.all_to_all(column, ('x', 'y'), 0, 0), tiles)]
    squeeze x1 -> x0, local copies, waits for them, and re-layouts: 1.46 us -> none  [reduce_gradients(): sent = lax.dynamic_index_in_dim(parts, 1 - core, 0, keepdims=False)]
    pallas_call x1 -> x3, Pallas kernels: 11.8 us -> 12.3 us  [the longest x1 11.2 us: backward(): pl.pallas_call(backward_kernel, grid=(SLOTS,), in_specs=[pl.BlockSpec(mem...]
  transfers between devices with their start and end apart: 11 -> 13, of which waited for: 7 -> 10; matrix products, arithmetic and copies ran while one was open for 0% -> 0% of each run, Pallas kernels for 6% -> 8%
where the time goes in v2:
time: 127 us
  Pallas kernels  34.9 us (27%)
  blocking collectives  34.8 us (27%)
  starting transfers between devices  26.7 us (21%)
  waiting for transfers between devices  24.3 us (19%)
  local copies, waits for them, and re-layouts  4.51 us (4%)
    all_to_all x1, blocking collectives, reduce_gradients(): plane = lax.all_to_all(total.reshape(16, 4, 8, QUARTER), ('x', 'y'), 0, 0)  20.7 us
    ppermute x12, waiting for transfers between devices, shift(): return lax.ppermute(v, axis, [(i, (i + by) % n) for i in range(n)])  20.4 us
    ppermute x12, starting transfers between devices, shift(): return lax.ppermute(v, axis, [(i, (i + by) % n) for i in range(n)])  19.2 us
    all_to_all x1, blocking collectives, reduce_gradients(): column = lax.all_to_all(column, ('z_hi', 'z_lo'), 0, 0)  14 us
    pallas_call x1, Pallas kernels, forward(): pl.pallas_call(forward_kernel, grid=(LOCAL, CELLS_IN // chunk), in_specs=...  12.7 us
    pallas_call x1, Pallas kernels, backward(): pl.pallas_call(backward_kernel, grid=(SLOTS,), in_specs=[pl.BlockSpec(mem...  11.2 us
    pallas_call x1, Pallas kernels, fine_tiles(): pl.pallas_call(tiles_kernel, grid=(SLOTS - 1,), in_specs=[pl.BlockSpec((L...  9.93 us
    all_to_all x1, starting transfers between devices, gather_weights(): plane = after(lax.all_to_all(column, ('x', 'y'), 0, 0), tiles)  7.43 us
  transfers between devices with their start and end apart: 13, of which 10 were waited for; matrix products, arithmetic and copies ran while one was open for 0% of the time, Pallas kernels for 8%

profile of v2, /device:TPU:6, one launch (start us, length us, event | category | flops | bytes accessed | tf_op | source)
XLA Modules:
  0.0 126.7 jit_solution(4891726109429079275)
XLA Ops:
  0.6 0.8 concatenate.6
  1.5 6.4 %collective-permute-start.2 = (bf16[8,1024]{1,0:T(8,128)(2,1)S(1)}, bf16[8,1024]{1,0:T(8,128)(2,1)S(1)}, u32[]{:S(2)}, u32[]{:S(2)}) collective-permute-start(bf16[8,1024]{1,0:T(8,128)(2,1)S(1)} %constant_dynamic-slice_fusion.own_ref), channel_id=1, source_target_pairs={{0,24},{8,0},{16,8},{24,16},{1,25},{9,1},{17,9},{25,17},{2,26},{10... | collective-permute-start | bytes 49160 | tf_op jit(solution)/shard_map/ppermute | solution.py:285
  7.9 1.0 collective-permute-start.1
  8.9 2.8 %collective-permute-start = (bf16[8,1024]{1,0:T(8,128)(2,1)S(1)}, bf16[8,1024]{1,0:T(8,128)(2,1)S(1)}, u32[]{:S(2)}, u32[]{:S(2)}) collective-permute-start(bf16[8,1024]{1,0:T(8,128)(2,1)S(1)} %constant_dynamic-slice_fusion.own_ref), channel_id=1, source_target_pairs={{0,8},{8,16},{16,24},{24,0},{1,9},{9,17},{17,25},{25,1},{2,10},{10... | collective-permute-start | bytes 49160 | tf_op jit(solution)/shard_map/ppermute | solution.py:285
  11.7 3.8 %collective-permute-done.1.back2_ref = bf16[8,1024]{1,0:T(8,128)(2,1)S(1)} collective-permute-done((bf16[8,1024]{1,0:T(8,128)(2,1)S(1)}, bf16[8,1024]{1,0:T(8,128)(2,1)S(1)}, u32[]{:S(2)}, u32[]{:S(2)}) %collective-permute-start.1) | collective-permute-done | bytes 16416 | tf_op jit(solution)/shard_map/ppermute | solution.py:285
  15.5 1.1 spread.1
  16.6 7.4 %all-to-all-start = ((bf16[16,4,8,1024]{3,2,1,0:T(8,128)(2,1)}), bf16[16,4,8,1024]{3,2,1,0:T(8,128)(2,1)S(1)}, u32[]{:S(2)}, u32[]{:S(2)}) async-start(bf16[16,4,8,1024]{3,2,1,0:T(8,128)(2,1)} %spread.1), calls=%async_computation | async-start | bytes 2097152 | tf_op jit(solution)/shard_map/all_to_all | solution.py:301
  24.0 9.9 %fine_tiles.1.first_ref.tiles_ref = bf16[2,6,256,1024]{3,2,1,0:T(8,128)(2,1)} custom-call(bf16[512,1024]{1,0:T(8,128)(2,1)} %bitcast.41, s32[7,1024]{1,0:T(8,128)} %nb_ref.1), custom_call_target="tpu_custom_call" | custom-call | flops 6499999744 | bytes 8000000 | tf_op jit(solution)/shard_map/fine_tiles/pallas_call | solution.py:61
  34.0 3.8 %all-to-all-done.value_ref = bf16[16,4,8,1024]{3,2,1,0:T(8,128)(2,1)S(1)} async-done(((bf16[16,4,8,1024]{3,2,1,0:T(8,128)(2,1)}), bf16[16,4,8,1024]{3,2,1,0:T(8,128)(2,1)S(1)}, u32[]{:S(2)}, u32[]{:S(2)}) %all-to-all-start) | async-done | bytes 1048608 | tf_op jit(solution)/shard_map/all_to_all | solution.py:301
  37.9 2.6 %collective-permute-done.3.other_ref = bf16[16,4,8,1024]{3,2,1,0:T(8,128)(2,1)S(1)} collective-permute-done((bf16[16,4,8,1024]{3,2,1,0:T(8,128)(2,1)S(1)}, bf16[16,4,8,1024]{3,2,1,0:T(8,128)(2,1)S(1)}, u32[]{:S(2)}, u32[]{:S(2)}) %collective-permute-start.3) | collective-permute-done | bytes 1048608 | tf_op jit(solution)/shard_map/ppermute | solution.py:285
  40.5 12.7 %forward.1 = (bf16[2,256,1024]{2,1,0:T(8,128)(2,1)}, bf16[256,4096]{1,0:T(8,128)(2,1)}, bf16[2,1792,256]{2,1,0:T(8,128)(2,1)}, f32[2,256,256]{2,1,0:T(8,128)}, b...) custom-call(s32[2]{0:T(128)S(1)} %pad_add_fusion.place_ref, bf16[16,4,8,1024]{3,2,1,0:T(8,128)(2,1)S(1)} %after.1.mine_ref, ...), custom_call_target="tpu_custom_call" | custom-call | flops 3200000000 | bytes 14000000 | tf_op jit(solution)/shard_map/forward/pallas_call | solution.py:165
  53.2 1.0 collective-permute-start.4
  54.3 2.8 %collective-permute-done.4 = f32[72,128]{1,0:T(8,128)S(1)} collective-permute-done((f32[72,128]{1,0:T(8,128)S(1)}, f32[72,128]{1,0:T(8,128)S(1)}, u32[]{:S(2)}, u32[]{:S(2)}) %collective-permute-start.4) | collective-permute-done | bytes 36896 | tf_op jit(solution)/shard_map/ppermute | solution.py:285
  57.2 0.4 collective-permute-start.7
  57.6 3.0 %collective-permute-start.6 = (f32[2,72,128]{2,1,0:T(8,128)S(1)}, f32[2,72,128]{2,1,0:T(8,128)S(1)}, u32[]{:S(2)}, u32[]{:S(2)}) collective-permute-start(f32[2,72,128]{2,1,0:T(8,128)S(1)} %pad_maximum_fusion.cohort0_ref), channel_id=1, source_target_pairs={{0,64},{32,96},{64,0},{96,32},{1,65},{33,97},{65,1},{97,33},{2,66}... | collective-permute-start | bytes 221192 | tf_op jit(solution)/shard_map/ppermute | solution.py:285
  60.6 0.6 collective-permute-start.5
  61.3 1.4 %collective-permute-done.7.cohort3_ref = f32[2,72,128]{2,1,0:T(8,128)S(1)} collective-permute-done((f32[2,72,128]{2,1,0:T(8,128)S(1)}, f32[2,72,128]{2,1,0:T(8,128)S(1)}, u32[]{:S(2)}, u32[]{:S(2)}) %collective-permute-start.7) | collective-permute-done | bytes 73760 | tf_op jit(solution)/shard_map/ppermute | solution.py:285
  62.7 1.0 collective-permute-done.6.cohort2_ref
  63.7 1.2 collective-permute-done.5.cohort1_ref
  65.0 1.2 copy-done.4
  66.2 1.0 copy-done.5
  67.3 11.2 %backward.1 = (bf16[4,4,4,8,1024]{4,3,2,1,0:T(8,128)(2,1)S(1)}, bf16[4,4,4,8,1024]{4,3,2,1,0:T(8,128)(2,1)S(1)}) custom-call(s32[2]{0:T(128)S(1)} %pad_add_fusion.place_ref, f32[2,72,128]{2,1,0:T(8,128)S(1)} %pad_maximum_fusion.cohort0_ref, f32[2,72,128]{2,1,0:T(8,128)S(1)} %collective-permute-done.5.cohort1_ref, ...), custom_call_target="tpu_custom_call" | custom-call | flops 4000000000 | bytes 16000000 | tf_op jit(solution)/shard_map/backward/pallas_call | solution.py:266
  78.8 2.6 %collective-permute-done.8 = bf16[4,4,4,8,1024]{4,3,2,1,0:T(8,128)(2,1)S(1)} collective-permute-done((bf16[4,4,4,8,1024]{4,3,2,1,0:T(8,128)(2,1)S(1)}, bf16[4,4,4,8,1024]{4,3,2,1,0:T(8,128)(2,1)S(1)}, u32[]{:S(2)}, u32[]{:S(2)}) %collective-permute-start.8) | collective-permute-done | bytes 1048608 | tf_op jit(solution)/shard_map/ppermute | solution.py:285
  81.4 0.4 add_convert_fusion
  81.8 20.7 %all_to_all.15 = bf16[16,4,8,1024]{3,2,1,0:T(8,128)(2,1)S(1)} all-to-all(bf16[16,4,8,1024]{3,2,1,0:T(8,128)(2,1)S(1)} %bitcast.48), channel_id=1, replica_groups=mesh['z_lo'=2,'x'=4,'z_hi'=4,'y'=4,'core'=2] {'x','y'}, dimensions={0} | all-to-all | bytes 2097152 | tf_op jit(solution)/shard_map/all_to_all | solution.py:307
  102.8 14.0 %all_to_all.16 = bf16[8,8,1024]{2,1,0:T(8,128)(2,1)S(1)} all-to-all(bf16[8,8,1024]{2,1,0:T(8,128)(2,1)S(1)} %bitcast.49), channel_id=1, replica_groups=mesh['z_lo'=2,'x'=4,'z_hi'=4,'y'=4,'core'=2] {'z_hi','z_lo'}, dimensions={0} | all-to-all | bytes 262144 | tf_op jit(solution)/shard_map/all_to_all | solution.py:310
  116.8 0.6 collective-permute-start.9
  117.4 2.7 %collective-permute-start.11 = (bf16[8,1024]{1,0:T(8,128)(2,1)S(1)}, bf16[8,1024]{1,0:T(8,128)(2,1)S(1)}, u32[]{:S(2)}, u32[]{:S(2)}) collective-permute-start(bf16[8,1024]{1,0:T(8,128)(2,1)S(1)} %reduce_sum.25), channel_id=1, source_target_pairs={{0,32},{32,64},{64,96},{96,0},{1,33},{33,65},{65,97},{97,1},{2,34}... | collective-permute-start | bytes 49160 | tf_op jit(solution)/shard_map/ppermute | solution.py:285
  120.5 1.4 %collective-permute-done.9 = bf16[8,1024]{1,0:T(8,128)(2,1)S(1)} collective-permute-done((bf16[8,1024]{1,0:T(8,128)(2,1)S(1)}, bf16[8,1024]{1,0:T(8,128)(2,1)S(1)}, u32[]{:S(2)}, u32[]{:S(2)}) %collective-permute-start.9) | collective-permute-done | bytes 16416 | tf_op jit(solution)/shard_map/ppermute | solution.py:285
  121.9 3.5 %collective-permute-done.10 = bf16[8,1024]{1,0:T(8,128)(2,1)S(1)} collective-permute-done((bf16[8,1024]{1,0:T(8,128)(2,1)S(1)}, bf16[8,1024]{1,0:T(8,128)(2,1)S(1)}, u32[]{:S(2)}, u32[]{:S(2)}) %collective-permute-start.10) | collective-permute-done | bytes 16416 | tf_op jit(solution)/shard_map/ppermute | solution.py:285
  125.5 0.6 slice_bitcast_fusion
  126.1 0.6 fusion
  (37 shorter events, 1.2 us)
Async XLA Ops:
  1.5 10.2 %collective-permute-start.2 = (bf16[8,1024]{1,0:T(8,128)(2,1)S(1)}, bf16[8,1024]{1,0:T(8,128)(2,1)S(1)}, u32[]{:S(2)}, u32[]{:S(2)}) collective-permute-start(bf16[8,1024]{1,0:T(8,128)(2,1)S(1)} %constant_dynamic-slice_fusion.own_ref), channel_id=1, source_target_pairs={{0,24},{8,0},{16,8},{24,16},{1,25},{9,1},{17,9},{25,17},{2,26},{10... | collective-permute-start | bytes 49160 | tf_op jit(solution)/shard_map/ppermute | solution.py:285
  7.9 7.6 %collective-permute-start.1 = (bf16[8,1024]{1,0:T(8,128)(2,1)S(1)}, bf16[8,1024]{1,0:T(8,128)(2,1)S(1)}, u32[]{:S(2)}, u32[]{:S(2)}) collective-permute-start(bf16[8,1024]{1,0:T(8,128)(2,1)S(1)} %constant_dynamic-slice_fusion.own_ref), channel_id=1, source_target_pairs={{0,16},{8,24},{16,0},{24,8},{1,17},{9,25},{17,1},{25,9},{2,18},{10... | collective-permute-start | bytes 49160 | tf_op jit(solution)/shard_map/ppermute | solution.py:285
  8.9 6.7 %collective-permute-start = (bf16[8,1024]{1,0:T(8,128)(2,1)S(1)}, bf16[8,1024]{1,0:T(8,128)(2,1)S(1)}, u32[]{:S(2)}, u32[]{:S(2)}) collective-permute-start(bf16[8,1024]{1,0:T(8,128)(2,1)S(1)} %constant_dynamic-slice_fusion.own_ref), channel_id=1, source_target_pairs={{0,8},{8,16},{16,24},{24,0},{1,9},{9,17},{17,25},{25,1},{2,10},{10... | collective-permute-start | bytes 49160 | tf_op jit(solution)/shard_map/ppermute | solution.py:285
  16.6 21.2 %all-to-all-start = ((bf16[16,4,8,1024]{3,2,1,0:T(8,128)(2,1)}), bf16[16,4,8,1024]{3,2,1,0:T(8,128)(2,1)S(1)}, u32[]{:S(2)}, u32[]{:S(2)}) async-start(bf16[16,4,8,1024]{3,2,1,0:T(8,128)(2,1)} %spread.1), calls=%async_computation | async-start | bytes 2097152 | tf_op jit(solution)/shard_map/all_to_all | solution.py:301
  33.9 6.5 %copy-start = (bf16[1,2,256,1024]{3,2,1,0:T(8,128)(2,1)S(1)}, bf16[1,2,256,1024]{3,2,1,0:T(8,128)(2,1)}, u32[]{:S(2)}) copy-start(bf16[1,2,256,1024]{3,2,1,0:T(8,128)(2,1)} %param.9) | copy-start | bytes 3145732
  33.9 6.5 %copy-start.1 = (s32[7,256]{1,0:T(8,128)S(1)}, s32[7,256]{1,0:T(8,128)}, u32[]{:S(2)}) copy-start(s32[7,256]{1,0:T(8,128)} %nb_mid_ref.3) | copy-start | bytes 21508
  33.9 6.5 %copy-start.2 = (s32[1024]{0:T(1024)S(1)}, s32[1024]{0:T(1024)}, u32[]{:S(2)}) copy-start(s32[1024]{0:T(1024)} %param.15) | copy-start | bytes 12292
  33.9 6.5 %copy-start.3 = (s32[256]{0:T(256)S(1)}, s32[256]{0:T(256)}, u32[]{:S(2)}) copy-start(s32[256]{0:T(256)} %param.16) | copy-start | bytes 3076
  37.8 2.7 %collective-permute-start.3 = (bf16[16,4,8,1024]{3,2,1,0:T(8,128)(2,1)S(1)}, bf16[16,4,8,1024]{3,2,1,0:T(8,128)(2,1)S(1)}, u32[]{:S(2)}, u32[]{:S(2)}) collective-permute-start(bf16[16,4,8,1024]{3,2,1,0:T(8,128)(2,1)S(1)} %after.1.mine_ref), channel_id=1, source_target_pairs={{0,1},{1,0},{2,3},{3,2},{4,5},{5,4},{6,7},{7,6},{8,9},{9,8},{10,11... | collective-permute-start | bytes 3145736 | tf_op jit(solution)/shard_map/ppermute | solution.py:285
  40.5 13.7 %copy-start.6 = (f32[1,69,64]{1,2,0:T(8,128)S(1)}, f32[1,69,64]{1,2,0:T(8,128)}, u32[]{:S(2)}) copy-start(f32[1,69,64]{1,2,0:T(8,128)} %param.17) | copy-start | bytes 52996
  53.2 4.0 %collective-permute-start.4 = (f32[72,128]{1,0:T(8,128)S(1)}, f32[72,128]{1,0:T(8,128)S(1)}, u32[]{:S(2)}, u32[]{:S(2)}) collective-permute-start(f32[72,128]{1,0:T(8,128)S(1)} %get-tuple-element.11.own_ref), channel_id=1, source_target_pairs={{0,128},{128,0},{1,129},{129,1},{2,130},{130,2},{3,131},{131,3},{4... | collective-permute-start | bytes 110600 | tf_op jit(solution)/shard_map/ppermute | solution.py:285
  57.2 5.6 %collective-permute-start.7 = (f32[2,72,128]{2,1,0:T(8,128)S(1)}, f32[2,72,128]{2,1,0:T(8,128)S(1)}, u32[]{:S(2)}, u32[]{:S(2)}) collective-permute-start(f32[2,72,128]{2,1,0:T(8,128)S(1)} %pad_maximum_fusion.cohort0_ref), channel_id=1, source_target_pairs={{0,96},{32,0},{64,32},{96,64},{1,97},{33,1},{65,33},{97,65},{2,98}... | collective-permute-start | bytes 221192 | tf_op jit(solution)/shard_map/ppermute | solution.py:285
  57.6 6.2 %collective-permute-start.6 = (f32[2,72,128]{2,1,0:T(8,128)S(1)}, f32[2,72,128]{2,1,0:T(8,128)S(1)}, u32[]{:S(2)}, u32[]{:S(2)}) collective-permute-start(f32[2,72,128]{2,1,0:T(8,128)S(1)} %pad_maximum_fusion.cohort0_ref), channel_id=1, source_target_pairs={{0,64},{32,96},{64,0},{96,32},{1,65},{33,97},{65,1},{97,33},{2,66}... | collective-permute-start | bytes 221192 | tf_op jit(solution)/shard_map/ppermute | solution.py:285
  60.6 4.4 %collective-permute-start.5 = (f32[2,72,128]{2,1,0:T(8,128)S(1)}, f32[2,72,128]{2,1,0:T(8,128)S(1)}, u32[]{:S(2)}, u32[]{:S(2)}) collective-permute-start(f32[2,72,128]{2,1,0:T(8,128)S(1)} %pad_maximum_fusion.cohort0_ref), channel_id=1, source_target_pairs={{0,32},{32,64},{64,96},{96,0},{1,33},{33,65},{65,97},{97,1},{2,34}... | collective-permute-start | bytes 221192 | tf_op jit(solution)/shard_map/ppermute | solution.py:285
  65.0 1.2 copy-start.4
  66.2 1.0 copy-start.5
  78.5 2.9 %collective-permute-start.8 = (bf16[4,4,4,8,1024]{4,3,2,1,0:T(8,128)(2,1)S(1)}, bf16[4,4,4,8,1024]{4,3,2,1,0:T(8,128)(2,1)S(1)}, u32[]{:S(2)}, u32[]{:S(2)}) collective-permute-start(bf16[4,4,4,8,1024]{4,3,2,1,0:T(8,128)(2,1)S(1)} %get-tuple-element.18), channel_id=1, source_target_pairs={{0,1},{1,0},{2,3},{3,2},{4,5},{5,4},{6,7},{7,6},{8,9},{9,8},{10,11... | collective-permute-start | bytes 3145736 | tf_op jit(solution)/shard_map/ppermute | solution.py:285
  116.8 5.0 %collective-permute-start.9 = (bf16[8,1024]{1,0:T(8,128)(2,1)S(1)}, bf16[8,1024]{1,0:T(8,128)(2,1)S(1)}, u32[]{:S(2)}, u32[]{:S(2)}) collective-permute-start(bf16[8,1024]{1,0:T(8,128)(2,1)S(1)} %reduce_sum.25), channel_id=1, source_target_pairs={{0,96},{32,0},{64,32},{96,64},{1,97},{33,1},{65,33},{97,65},{2,98}... | collective-permute-start | bytes 49160 | tf_op jit(solution)/shard_map/ppermute | solution.py:285
  117.4 8.0 %collective-permute-start.11 = (bf16[8,1024]{1,0:T(8,128)(2,1)S(1)}, bf16[8,1024]{1,0:T(8,128)(2,1)S(1)}, u32[]{:S(2)}, u32[]{:S(2)}) collective-permute-start(bf16[8,1024]{1,0:T(8,128)(2,1)S(1)} %reduce_sum.25), channel_id=1, source_target_pairs={{0,32},{32,64},{64,96},{96,0},{1,33},{33,65},{65,97},{97,1},{2,34}... | collective-permute-start | bytes 49160 | tf_op jit(solution)/shard_map/ppermute | solution.py:285
  120.2 5.2 %collective-permute-start.10 = (bf16[8,1024]{1,0:T(8,128)(2,1)S(1)}, bf16[8,1024]{1,0:T(8,128)(2,1)S(1)}, u32[]{:S(2)}, u32[]{:S(2)}) collective-permute-start(bf16[8,1024]{1,0:T(8,128)(2,1)S(1)} %reduce_sum.25), channel_id=1, source_target_pairs={{0,64},{32,96},{64,0},{96,32},{1,65},{33,97},{65,1},{97,33},{2,66}... | collective-permute-start | bytes 49160 | tf_op jit(solution)/shard_map/ppermute | solution.py:285

commit v3 on v2

v3 whole, which is shorter than its diff:
```python
import math

import jax
import jax.numpy as jnp
from jax import lax
from jax.experimental import pallas as pl
from jax.experimental.pallas import tpu as pltpu
from jax.sharding import Mesh
from jax.sharding import PartitionSpec as P

DP = ("z_hi", "y", "core")
MEM = ("z_lo", "x")

MEMBERS = 16
CHANNELS = 256
SLOTS = 7
FIELDS = 69
FIELD_ROWS = 72
CELLS_OUT = 64
CELLS_MID = 256
CELLS_IN = 1024
SAMPLES = 32
LOCAL = 2
QUARTER = 1024
SMOOTH = 0.0001
NORM = MEMBERS / math.sqrt(SAMPLES * CELLS_OUT)
SECOND_AT = SLOTS * CHANNELS
HEAD_AT = 2 * SLOTS * CHANNELS
WIDTH = 4096
MIB = 1024 * 1024

f32 = jnp.float32
bf16 = jnp.bfloat16


def dot(a, b):
    return lax.dot_general(a, b, (((1,), (0,)), ((), ())), preferred_element_type=f32)


def dot_bt(a, b):
    return lax.dot_general(a, b, (((1,), (1,)), ((), ())), preferred_element_type=f32)


def dot_at(a, b):
    return lax.dot_general(a, b, (((0,), (0,)), ((), ())), preferred_element_type=f32)


def one_hot(index_row, rows):
    shape = (rows, index_row.shape[1])
    return jnp.where(lax.broadcasted_iota(jnp.int32, shape, 0) == index_row, 1.0, 0.0).astype(bf16)


def tiles_kernel(x_ref, nb_ref, out_ref):
    row = nb_ref[pl.ds(pl.program_id(0) + 1, 1), :]
    tile = dot(x_ref[...], one_hot(row, CELLS_IN)).astype(bf16)
    for m in range(LOCAL):
        out_ref[m, 0] = tile[m * CHANNELS : (m + 1) * CHANNELS]


def fine_tiles(x0, nb):
    return pl.pallas_call(
        tiles_kernel,
        grid=(SLOTS - 1,),
        in_specs=[
            pl.BlockSpec((LOCAL * CHANNELS, CELLS_IN), lambda j: (0, 0)),
            pl.BlockSpec((SLOTS, CELLS_IN), lambda j: (0, 0)),
        ],
        out_specs=pl.BlockSpec((LOCAL, 1, CHANNELS, CELLS_IN), lambda j: (0, j, 0, 0)),
        out_shape=jax.ShapeDtypeStruct((LOCAL, SLOTS - 1, CHANNELS, CELLS_IN), bf16),
        compiler_params=pltpu.CompilerParams(vmem_limit_bytes=56 * MIB),
        cost_estimate=pl.CostEstimate(flops=6_500_000_000, bytes_accessed=8_000_000, transcendentals=0),
        name="fine_tiles",
    )(x0, nb)


def forward_kernel(
    place_ref, mine_ref, other_ref, x_ref, parents_ref, nb_mid_ref, parents_mid_ref, tiles_hbm,
    x2_ref, pred_ref, slope1_hbm, w_hbm, tiles_mid_hbm, slope2_hbm,
    tiles_ref, w_ref, slope1_ref, tiles_mid_ref, slope2_ref, in_sem, out_sem,
):
    loads = [pltpu.make_async_copy(tiles_hbm.at[m], tiles_ref.at[m], in_sem.at[m]) for m in range(LOCAL)]
    for load in loads:
        load.start()
    first, z = place_ref[0] == 0, place_ref[1]
    for x in range(4):
        for y in range(4):
            for back in range(4):
                mine, other = mine_ref[x * 4 + y, back].astype(f32), other_ref[x * 4 + y, back].astype(f32)
                pair = jnp.concatenate([jnp.where(first, mine, other), jnp.where(first, other, mine)], 0)
                row = pl.multiple_of((lax.rem(z - back + 4, 4) * 4 + y) * 16, 16)
                w_ref[pl.ds(row, 16), x * QUARTER : (x + 1) * QUARTER] = pair.astype(bf16)
    stores = [pltpu.make_async_copy(w_ref.at[:, SECOND_AT : HEAD_AT + 128], w_hbm, out_sem.at[0])]
    stores[0].start()
    unpool = one_hot(parents_ref[...], CELLS_MID)
    x1 = []
    for m in range(LOCAL):
        loads[m].wait()
        pooled = jnp.zeros((CHANNELS, CELLS_MID), f32)
        for at in range(0, CELLS_IN, 512):
            cells = slice(at, at + 512)
            a1 = dot(w_ref[:, 0:CHANNELS], x_ref[m, :, cells])
            for j in range(1, SLOTS):
                a1 = a1 + dot(w_ref[:, j * CHANNELS : (j + 1) * CHANNELS], tiles_ref[m, j - 1, :, cells])
            gate = jax.nn.sigmoid(a1)
            slope1_ref[m, :, cells] = (gate * (1.0 + a1 * (1.0 - gate))).astype(bf16)
            h1 = (x_ref[m, :, cells].astype(f32) + a1 * gate).astype(bf16)
            pooled = pooled + dot_bt(h1, unpool[:, cells])
        stores.append(pltpu.make_async_copy(slope1_ref.at[m], slope1_hbm.at[m], out_sem.at[1 + m]))
        stores[-1].start()
        x1.append((pooled * 0.25).astype(bf16))
        tiles_mid_ref[m, 0:CHANNELS] = x1[m]
    both = jnp.concatenate(x1, 0)
    for j in range(1, SLOTS):
        tile = dot(both, one_hot(nb_mid_ref[j : j + 1, :], CELLS_MID)).astype(bf16)
        for m in range(LOCAL):
            tiles_mid_ref[m, j * CHANNELS : (j + 1) * CHANNELS] = tile[m * CHANNELS : (m + 1) * CHANNELS]
    stores.append(pltpu.make_async_copy(tiles_mid_ref, tiles_mid_hbm, out_sem.at[3]))
    stores[-1].start()
    pool = one_hot(parents_mid_ref[...], CELLS_OUT)
    for m in range(LOCAL):
        a2 = dot(w_ref[:, SECOND_AT:HEAD_AT], tiles_mid_ref[m])
        gate2 = jax.nn.sigmoid(a2)
        slope2_ref[m] = gate2 * (1.0 + a2 * (1.0 - gate2))
        h2 = (x1[m].astype(f32) + a2 * gate2).astype(bf16)
        x2_ref[:, m * CELLS_OUT : (m + 1) * CELLS_OUT] = (dot_bt(h2, pool) * 0.25).astype(bf16)
    stores.append(pltpu.make_async_copy(slope2_ref, slope2_hbm, out_sem.at[4]))
    stores[-1].start()
    pred = dot_at(w_ref[:, HEAD_AT : HEAD_AT + 128], x2_ref[...])
    pred_ref[...] = pred[0:FIELD_ROWS]
    for store in stores:
        store.wait()


def spread_kernel(own_ref, back1_ref, back2_ref, back3_ref, out_ref):
    for block in range(16):
        for back, source in enumerate((own_ref, back1_ref, back2_ref, back3_ref)):
            out_ref[block, back] = source[...]


def spread(pieces):
    return pl.pallas_call(
        spread_kernel,
        in_specs=[pl.BlockSpec(memory_space=pltpu.VMEM)] * 4,
        out_specs=pl.BlockSpec(memory_space=pltpu.VMEM),
        out_shape=jax.ShapeDtypeStruct((16, 4, 8, QUARTER), bf16),
        compiler_params=pltpu.CompilerParams(vmem_limit_bytes=8 * MIB),
        name="spread",
    )(*pieces)


def after_kernel(value_ref, first_ref, out_ref):
    del value_ref, first_ref, out_ref


def after(value, first):
    return pl.pallas_call(
        after_kernel,
        in_specs=[pl.BlockSpec(memory_space=pl.ANY)] * 2,
        out_specs=pl.BlockSpec(memory_space=pl.ANY),
        out_shape=jax.ShapeDtypeStruct(value.shape, value.dtype),
        input_output_aliases={0: 0},
        compiler_params=pltpu.CompilerParams(vmem_limit_bytes=48 * MIB),
        name="after",
    )(value, first)


VMEM = pl.BlockSpec(memory_space=pltpu.VMEM)
HBM = pl.BlockSpec(memory_space=pltpu.HBM)
SMEM = pl.BlockSpec(memory_space=pltpu.SMEM)
TILES = (LOCAL, SLOTS - 1, CHANNELS, CELLS_IN)
BACK_W = SECOND_AT + 128


def forward(place, mine, other, x0, tiles, parents_fine, nb_mid, parents_mid):
    return pl.pallas_call(
        forward_kernel,
        in_specs=[SMEM, VMEM, VMEM, VMEM, VMEM, VMEM, VMEM, HBM],
        out_specs=[VMEM, VMEM, HBM, HBM, HBM, HBM],
        out_shape=[
            jax.ShapeDtypeStruct((CHANNELS, LOCAL * CELLS_OUT), bf16),
            jax.ShapeDtypeStruct((FIELD_ROWS, LOCAL * CELLS_OUT), f32),
            pltpu.HBM((LOCAL, CHANNELS, CELLS_IN), bf16),
            pltpu.HBM((CHANNELS, BACK_W), bf16),
            pltpu.HBM((LOCAL, SECOND_AT, CELLS_MID), bf16),
            pltpu.HBM((LOCAL, CHANNELS, CELLS_MID), f32),
        ],
        scratch_shapes=[
            pltpu.VMEM(TILES, bf16),
            pltpu.VMEM((CHANNELS, WIDTH), bf16),
            pltpu.VMEM((LOCAL, CHANNELS, CELLS_IN), bf16),
            pltpu.VMEM((LOCAL, SECOND_AT, CELLS_MID), bf16),
            pltpu.VMEM((LOCAL, CHANNELS, CELLS_MID), f32),
            pltpu.SemaphoreType.DMA((LOCAL,)),
            pltpu.SemaphoreType.DMA((5,)),
        ],
        compiler_params=pltpu.CompilerParams(vmem_limit_bytes=48 * MIB),
        cost_estimate=pl.CostEstimate(flops=3_200_000_000, bytes_accessed=14_000_000, transcendentals=700_000),
        name="forward",
    )(place, mine, other, x0, parents_fine, nb_mid, parents_mid, tiles)


def sign_smooth(v):
    return v * lax.rsqrt(v * v + SMOOTH)


def backward_kernel(
    place_ref, cohort0_ref, cohort1_ref, cohort2_ref, cohort3_ref, own_ref, obs_ref, x2_ref,
    parents_ref, nb_mid_ref, parents_mid_ref, w_hbm, tiles_mid_hbm, slope2_hbm, slope1_hbm, x_hbm, tiles_hbm,
    kept_ref, sent_ref,
    w_ref, tiles_mid_ref, slope2_ref, slope1_ref, x_ref, tiles_ref, g1_ref, sem,
):
    moves = ((w_hbm, w_ref), (slope2_hbm, slope2_ref), (tiles_mid_hbm, tiles_mid_ref), (slope1_hbm, slope1_ref), (x_hbm, x_ref), (tiles_hbm, tiles_ref))
    loads = [pltpu.make_async_copy(source, here, sem.at[i]) for i, (source, here) in enumerate(moves)]
    for load in loads:
        load.start()
    first = place_ref[0] == 0

    def put(quarter, at, lanes, value):
        for z in range(4):
            for y in range(4):
                row = (z * 4 + y) * 16
                low, high = value[row : row + 8], value[row + 8 : row + 16]
                kept_ref[quarter, y, z, :, at : at + lanes] = jnp.where(first, low, high).astype(bf16)
                sent_ref[quarter, y, z, :, at : at + lanes] = jnp.where(first, high, low).astype(bf16)

    own = own_ref[...]
    spread = jnp.zeros_like(own)
    for pair_ref in (cohort0_ref, cohort1_ref, cohort2_ref, cohort3_ref):
        for peer in range(2):
            theirs = pair_ref[peer]
            spread = spread + sign_smooth(own - theirs) + sign_smooth(own - pltpu.roll(theirs, CELLS_OUT, 1))
    skill = sign_smooth(own - obs_ref[...])
    slope = NORM * (skill / MEMBERS - spread / (MEMBERS * (MEMBERS - 1)))
    slope = jnp.concatenate([slope, jnp.zeros((128 - FIELD_ROWS, 128), f32)], 0).astype(bf16)
    put(3, 512, 128, dot_bt(x2_ref[...], slope))
    put(3, 640, 384, jnp.zeros((CHANNELS, 384), f32))
    pool = one_hot(parents_mid_ref[...], CELLS_OUT)
    wide = [dot(slope[:, m * CELLS_OUT : (m + 1) * CELLS_OUT], pool).astype(bf16) for m in range(LOCAL)]
    for load in loads[:4]:
        load.wait()
    head_t = w_ref[:, SECOND_AT:BACK_W]
    dh2 = [dot(head_t, wide[m]) * 0.25 for m in range(LOCAL)]
    g2 = [(dh2[m] * slope2_ref[m]).astype(bf16) for m in range(LOCAL)]
    both = jnp.concatenate(g2, 0)
    back = [dh2[m] + dot_at(w_ref[:, 0:CHANNELS], g2[m]) for m in range(LOCAL)]
    for q in range(1, SLOTS):
        spread_back = dot_bt(both, one_hot(nb_mid_ref[q : q + 1, :], CELLS_MID)).astype(bf16)
        weight = w_ref[:, q * CHANNELS : (q + 1) * CHANNELS]
        for m in range(LOCAL):
            back[m] = back[m] + dot_at(weight, spread_back[m * CHANNELS : (m + 1) * CHANNELS])
    unpool = one_hot(parents_ref[...], CELLS_MID)
    for m in range(LOCAL):
        dh1 = dot((back[m] * 0.25).astype(bf16), unpool)
        g1_ref[m] = (dh1 * slope1_ref[m].astype(f32)).astype(bf16)
    for load in loads[4:]:
        load.wait()
    for q in range(SLOTS):
        rows = slice(q * CHANNELS, (q + 1) * CHANNELS)
        grad = dot_bt(g2[0], tiles_mid_ref[0, rows]) + dot_bt(g2[1], tiles_mid_ref[1, rows])
        put((SLOTS + q) // 4, (SLOTS + q) % 4 * 256, 256, grad)
    put(0, 0, 256, dot_bt(g1_ref[0], x_ref[0]) + dot_bt(g1_ref[1], x_ref[1]))
    for j in range(1, SLOTS):
        grad = dot_bt(g1_ref[0], tiles_ref[0, j - 1]) + dot_bt(g1_ref[1], tiles_ref[1, j - 1])
        put(j // 4, j % 4 * 256, 256, grad)


def backward(place, cohort, own, obs, w, tiles_mid, slope2, x2, slope1, x0, tiles, parents_fine, nb_mid, parents_mid):
    return pl.pallas_call(
        backward_kernel,
        in_specs=[SMEM] + [VMEM] * 10 + [HBM] * 6,
        out_specs=[VMEM] * 2,
        out_shape=[jax.ShapeDtypeStruct((4, 4, 4, 8, QUARTER), bf16)] * 2,
        scratch_shapes=[
            pltpu.VMEM((CHANNELS, BACK_W), bf16),
            pltpu.VMEM((LOCAL, SECOND_AT, CELLS_MID), bf16),
            pltpu.VMEM((LOCAL, CHANNELS, CELLS_MID), f32),
            pltpu.VMEM((LOCAL, CHANNELS, CELLS_IN), bf16),
            pltpu.VMEM((LOCAL, CHANNELS, CELLS_IN), bf16),
            pltpu.VMEM(TILES, bf16),
            pltpu.VMEM((LOCAL, CHANNELS, CELLS_IN), bf16),
            pltpu.SemaphoreType.DMA((6,)),
        ],
        compiler_params=pltpu.CompilerParams(vmem_limit_bytes=50 * MIB),
        cost_estimate=pl.CostEstimate(flops=4_000_000_000, bytes_accessed=16_000_000, transcendentals=200_000),
        name="backward",
    )(place, *cohort, own, obs, x2, parents_fine, nb_mid, parents_mid, w, tiles_mid, slope2, slope1, x0, tiles)


def shift(v, axis, n, by):
    return lax.ppermute(v, axis, [(i, (i + by) % n) for i in range(n)])


def gather_weights(weight_first, weight_second, weight_head, x, tiles):
    rows = weight_first.shape[1]
    flat = jnp.concatenate(
        [
            weight_first.transpose(1, 0, 2).reshape(rows, SECOND_AT),
            weight_second.transpose(1, 0, 2).reshape(rows, SECOND_AT),
            weight_head.T,
            jnp.zeros((rows, WIDTH - HEAD_AT - FIELDS), bf16),
        ],
        1,
    )
    mine = lax.dynamic_slice_in_dim(flat, x * QUARTER, QUARTER, 1)
    column = spread([mine] + [shift(mine, "z_hi", 4, s) for s in (1, 2, 3)])
    plane = after(lax.all_to_all(column, ("x", "y"), 0, 0), tiles)
    return plane, shift(plane, "core", 2, 1)


def reduce_gradients(kept, sent, x):
    total = (kept.astype(f32) + shift(sent, "core", 2, 1).astype(f32)).astype(bf16)
    plane = lax.all_to_all(total.reshape(16, 4, 8, QUARTER), ("x", "y"), 0, 0)
    total = jnp.sum(plane.astype(f32), 0).astype(bf16)
    column = jnp.broadcast_to(total[:, None], (4, 2, 8, QUARTER)).reshape(8, 8, QUARTER)
    column = lax.all_to_all(column, ("z_hi", "z_lo"), 0, 0)
    total = jnp.sum(column.astype(f32), 0).astype(bf16)
    back = [total] + [shift(total, "x", 4, s) for s in (1, 2, 3)]
    ring = jnp.stack([back[i] for i in (3, 2, 1, 0, 3, 2, 1)])
    return lax.dynamic_slice_in_dim(ring, 3 - x, 4, 0).astype(f32).transpose(1, 0, 2).reshape(8, WIDTH)


def per_device(
    member_fields, weight_first, weight_second, weight_head,
    neighbours_fine, neighbours_mid, parents_fine, parents_mid, observations,
):
    core, x = lax.axis_index("core"), lax.axis_index("x")
    place = jnp.stack([core, lax.axis_index("z_hi")]).astype(jnp.int32)
    x0 = member_fields[0]
    parents_fine = parents_fine.reshape(1, CELLS_IN)
    parents_mid = parents_mid.reshape(1, CELLS_MID)
    truth = jnp.pad(observations[0], ((0, FIELD_ROWS - FIELDS), (0, 0)))
    truth = jnp.concatenate([truth] * LOCAL, 1)

    tiles = fine_tiles(x0.reshape(LOCAL * CHANNELS, CELLS_IN), neighbours_fine)
    mine, other = gather_weights(weight_first, weight_second, weight_head, x, tiles)
    x2, pred, slope1, w, tiles_mid, slope2 = forward(
        place, mine, other, x0, tiles, parents_fine, neighbours_mid, parents_mid
    )
    pair = jnp.stack([pred, shift(pred, "z_lo", 2, 1)])
    cohort = [pair] + [shift(pair, "x", 4, s) for s in (1, 2, 3)]
    kept, sent = backward(
        place, cohort, pred, truth, w, tiles_mid, slope2, x2, slope1, x0, tiles, parents_fine, neighbours_mid, parents_mid
    )
    rows = reduce_gradients(kept, sent, x)
    return (
        rows[:, :SECOND_AT].reshape(8, SLOTS, CHANNELS).transpose(1, 0, 2),
        rows[:, SECOND_AT:HEAD_AT].reshape(8, SLOTS, CHANNELS).transpose(1, 0, 2),
        rows[:, HEAD_AT : HEAD_AT + FIELDS].T,
    )


def solution(mesh):
    fine_mesh = Mesh(mesh.devices.reshape(2, 4, 4, 4, 2), ("z_lo", "x", "z_hi", "y", "core"))
    placed = (
        P(DP, MEM, None, None),
        P(None, DP, None),
        P(None, DP, None),
        P(None, DP),
        P(),
        P(),
        P(),
        P(),
        P(DP, None, None),
    )
    return jax.shard_map(
        per_device,
        mesh=fine_mesh,
        in_specs=placed,
        out_specs=(P(None, DP, None), P(None, DP, None), P(None, DP)),
        check_vma=False,
    )
```

time: 127 us -> 120 us (0.945)
  Pallas kernels: 34.9 us -> 27.7 us
    pallas_call x2, Pallas kernels: 24 us -> 16.7 us  [the longest x1 8.67 us: forward(): pl.pallas_call(forward_kernel, in_specs=[SMEM, VMEM, VMEM, VMEM, VMEM, VM...]
where the time goes in v3:
time: 120 us; the launch traced here: 119 us
  blocking collectives  34.7 us (29%)
  Pallas kernels  27.7 us (23%)
  starting transfers between devices  26.6 us (22%)
  waiting for transfers between devices  24.3 us (20%)
  local copies, waits for them, and re-layouts  4.49 us (4%)
    all_to_all x1, blocking collectives, reduce_gradients(): plane = lax.all_to_all(total.reshape(16, 4, 8, QUARTER), ('x', 'y'), 0, 0)  20.7 us
    ppermute x12, waiting for transfers between devices, shift(): return lax.ppermute(v, axis, [(i, (i + by) % n) for i in range(n)])  20.4 us
    ppermute x12, starting transfers between devices, shift(): return lax.ppermute(v, axis, [(i, (i + by) % n) for i in range(n)])  19.1 us
    all_to_all x1, blocking collectives, reduce_gradients(): column = lax.all_to_all(column, ('z_hi', 'z_lo'), 0, 0)  14 us
    pallas_call x1, Pallas kernels, fine_tiles(): pl.pallas_call(tiles_kernel, grid=(SLOTS - 1,), in_specs=[pl.BlockSpec((L...  9.93 us
    pallas_call x1, Pallas kernels, forward(): pl.pallas_call(forward_kernel, in_specs=[SMEM, VMEM, VMEM, VMEM, VMEM, VM...  8.67 us
    pallas_call x1, Pallas kernels, backward(): pl.pallas_call(backward_kernel, in_specs=[SMEM] + [VMEM] * 10 + [HBM] * 6...  8.07 us
    all_to_all x1, starting transfers between devices, gather_weights(): plane = after(lax.all_to_all(column, ('x', 'y'), 0, 0), tiles)  7.43 us
  transfers between devices with their start and end apart: 13, of which 10 were waited for; matrix products, arithmetic and copies ran while one was open for 0% of the time, Pallas kernels for 8%

profile of v3, /device:TPU:6, one launch (start us, length us, event | category | flops | bytes accessed | tf_op | source)
XLA Modules:
  0.0 119.4 jit_solution(14284456257327370792)
XLA Ops:
  0.6 0.8 concatenate.6
  1.5 6.4 %collective-permute-start.2 = (bf16[8,1024]{1,0:T(8,128)(2,1)S(1)}, bf16[8,1024]{1,0:T(8,128)(2,1)S(1)}, u32[]{:S(2)}, u32[]{:S(2)}) collective-permute-start(bf16[8,1024]{1,0:T(8,128)(2,1)S(1)} %constant_dynamic-slice_fusion.own_ref), channel_id=1, source_target_pairs={{0,24},{8,0},{16,8},{24,16},{1,25},{9,1},{17,9},{25,17},{2,26},{10... | collective-permute-start | bytes 49160 | tf_op jit(solution)/shard_map/ppermute | solution.py:290
  7.9 1.0 collective-permute-start.1
  8.9 2.8 %collective-permute-start = (bf16[8,1024]{1,0:T(8,128)(2,1)S(1)}, bf16[8,1024]{1,0:T(8,128)(2,1)S(1)}, u32[]{:S(2)}, u32[]{:S(2)}) collective-permute-start(bf16[8,1024]{1,0:T(8,128)(2,1)S(1)} %constant_dynamic-slice_fusion.own_ref), channel_id=1, source_target_pairs={{0,8},{8,16},{16,24},{24,0},{1,9},{9,17},{17,25},{25,1},{2,10},{10... | collective-permute-start | bytes 49160 | tf_op jit(solution)/shard_map/ppermute | solution.py:290
  11.7 3.8 %collective-permute-done.1.back2_ref = bf16[8,1024]{1,0:T(8,128)(2,1)S(1)} collective-permute-done((bf16[8,1024]{1,0:T(8,128)(2,1)S(1)}, bf16[8,1024]{1,0:T(8,128)(2,1)S(1)}, u32[]{:S(2)}, u32[]{:S(2)}) %collective-permute-start.1) | collective-permute-done | bytes 16416 | tf_op jit(solution)/shard_map/ppermute | solution.py:290
  15.5 1.1 spread.1
  16.6 7.4 %all-to-all-start = ((bf16[16,4,8,1024]{3,2,1,0:T(8,128)(2,1)}), bf16[16,4,8,1024]{3,2,1,0:T(8,128)(2,1)S(1)}, u32[]{:S(2)}, u32[]{:S(2)}) async-start(bf16[16,4,8,1024]{3,2,1,0:T(8,128)(2,1)} %spread.1), calls=%async_computation | async-start | bytes 2097152 | tf_op jit(solution)/shard_map/all_to_all | solution.py:306
  24.0 9.9 %fine_tiles.1.first_ref.tiles_hbm = bf16[2,6,256,1024]{3,2,1,0:T(8,128)(2,1)} custom-call(bf16[512,1024]{1,0:T(8,128)(2,1)} %bitcast.41, s32[7,1024]{1,0:T(8,128)} %nb_ref.1), custom_call_target="tpu_custom_call" | custom-call | flops 6499999744 | bytes 8000000 | tf_op jit(solution)/shard_map/fine_tiles/pallas_call | solution.py:61
  34.0 3.8 %all-to-all-done.value_ref = bf16[16,4,8,1024]{3,2,1,0:T(8,128)(2,1)S(1)} async-done(((bf16[16,4,8,1024]{3,2,1,0:T(8,128)(2,1)}), bf16[16,4,8,1024]{3,2,1,0:T(8,128)(2,1)S(1)}, u32[]{:S(2)}, u32[]{:S(2)}) %all-to-all-start) | async-done | bytes 1048608 | tf_op jit(solution)/shard_map/all_to_all | solution.py:306
  37.9 2.6 %collective-permute-done.3.other_ref = bf16[16,4,8,1024]{3,2,1,0:T(8,128)(2,1)S(1)} collective-permute-done((bf16[16,4,8,1024]{3,2,1,0:T(8,128)(2,1)S(1)}, bf16[16,4,8,1024]{3,2,1,0:T(8,128)(2,1)S(1)}, u32[]{:S(2)}, u32[]{:S(2)}) %collective-permute-start.3) | collective-permute-done | bytes 1048608 | tf_op jit(solution)/shard_map/ppermute | solution.py:290
  40.5 8.7 %forward.1 = (bf16[256,128]{1,0:T(8,128)(2,1)S(1)}, f32[72,128]{1,0:T(8,128)S(1)}, bf16[2,256,1024]{2,1,0:T(8,128)(2,1)}, bf16[256,1920]{1,0:T(8,128)(2,1)}, bf1...) custom-call(s32[2]{0:T(128)S(1)} %pad_add_fusion.place_ref, bf16[16,4,8,1024]{3,2,1,0:T(8,128)(2,1)S(1)} %after.1.mine_ref, ...), custom_call_target="tpu_custom_call" | custom-call | flops 3200000000 | bytes 14000000 | tf_op jit(solution)/shard_map/forward/pallas_call | solution.py:175
  49.2 1.1 collective-permute-start.4
  50.4 2.8 %collective-permute-done.4 = f32[72,128]{1,0:T(8,128)S(1)} collective-permute-done((f32[72,128]{1,0:T(8,128)S(1)}, f32[72,128]{1,0:T(8,128)S(1)}, u32[]{:S(2)}, u32[]{:S(2)}) %collective-permute-start.4) | collective-permute-done | bytes 36896 | tf_op jit(solution)/shard_map/ppermute | solution.py:290
  53.2 0.4 collective-permute-start.7
  53.7 3.0 %collective-permute-start.6 = (f32[2,72,128]{2,1,0:T(8,128)S(1)}, f32[2,72,128]{2,1,0:T(8,128)S(1)}, u32[]{:S(2)}, u32[]{:S(2)}) collective-permute-start(f32[2,72,128]{2,1,0:T(8,128)S(1)} %pad_maximum_fusion.cohort0_ref), channel_id=1, source_target_pairs={{0,64},{32,96},{64,0},{96,32},{1,65},{33,97},{65,1},{97,33},{2,66}... | collective-permute-start | bytes 221192 | tf_op jit(solution)/shard_map/ppermute | solution.py:290
  56.7 0.6 collective-permute-start.5
  57.4 1.4 %collective-permute-done.7.cohort3_ref = f32[2,72,128]{2,1,0:T(8,128)S(1)} collective-permute-done((f32[2,72,128]{2,1,0:T(8,128)S(1)}, f32[2,72,128]{2,1,0:T(8,128)S(1)}, u32[]{:S(2)}, u32[]{:S(2)}) %collective-permute-start.7) | collective-permute-done | bytes 73760 | tf_op jit(solution)/shard_map/ppermute | solution.py:290
  58.8 1.0 collective-permute-done.6.cohort2_ref
  59.8 1.2 %collective-permute-done.5.cohort1_ref = f32[2,72,128]{2,1,0:T(8,128)S(1)} collective-permute-done((f32[2,72,128]{2,1,0:T(8,128)S(1)}, f32[2,72,128]{2,1,0:T(8,128)S(1)}, u32[]{:S(2)}, u32[]{:S(2)}) %collective-permute-start.5) | collective-permute-done | bytes 73760 | tf_op jit(solution)/shard_map/ppermute | solution.py:290
  61.0 1.2 %copy-done.4 = bf16[256,1920]{1,0:T(8,128)(2,1)S(1)} copy-done((bf16[256,1920]{1,0:T(8,128)(2,1)S(1)}, bf16[256,1920]{1,0:T(8,128)(2,1)}, u32[]{:S(2)}) %copy-start.4) | copy-done | bytes 983064
  62.3 1.0 copy-done.5
  63.3 8.1 %backward.1 = (bf16[4,4,4,8,1024]{4,3,2,1,0:T(8,128)(2,1)S(1)}, bf16[4,4,4,8,1024]{4,3,2,1,0:T(8,128)(2,1)S(1)}) custom-call(s32[2]{0:T(128)S(1)} %pad_add_fusion.place_ref, f32[2,72,128]{2,1,0:T(8,128)S(1)} %pad_maximum_fusion.cohort0_ref, f32[2,72,128]{2,1,0:T(8,128)S(1)} %collective-permute-done.5.cohort1_ref, ...), custom_call_target="tpu_custom_call" | custom-call | flops 4000000000 | bytes 16000000 | tf_op jit(solution)/shard_map/backward/pallas_call | solution.py:268
  71.5 2.6 %collective-permute-done.8 = bf16[4,4,4,8,1024]{4,3,2,1,0:T(8,128)(2,1)S(1)} collective-permute-done((bf16[4,4,4,8,1024]{4,3,2,1,0:T(8,128)(2,1)S(1)}, bf16[4,4,4,8,1024]{4,3,2,1,0:T(8,128)(2,1)S(1)}, u32[]{:S(2)}, u32[]{:S(2)}) %collective-permute-start.8) | collective-permute-done | bytes 1048608 | tf_op jit(solution)/shard_map/ppermute | solution.py:290
  74.1 0.4 add_convert_fusion
  74.5 20.7 %all_to_all.15 = bf16[16,4,8,1024]{3,2,1,0:T(8,128)(2,1)S(1)} all-to-all(bf16[16,4,8,1024]{3,2,1,0:T(8,128)(2,1)S(1)} %bitcast.48), channel_id=1, replica_groups=mesh['z_lo'=2,'x'=4,'z_hi'=4,'y'=4,'core'=2] {'x','y'}, dimensions={0} | all-to-all | bytes 2097152 | tf_op jit(solution)/shard_map/all_to_all | solution.py:312
  95.5 14.0 %all_to_all.16 = bf16[8,8,1024]{2,1,0:T(8,128)(2,1)S(1)} all-to-all(bf16[8,8,1024]{2,1,0:T(8,128)(2,1)S(1)} %bitcast.49), channel_id=1, replica_groups=mesh['z_lo'=2,'x'=4,'z_hi'=4,'y'=4,'core'=2] {'z_hi','z_lo'}, dimensions={0} | all-to-all | bytes 262144 | tf_op jit(solution)/shard_map/all_to_all | solution.py:315
  109.5 0.6 collective-permute-start.9
  110.1 2.7 %collective-permute-start.11 = (bf16[8,1024]{1,0:T(8,128)(2,1)S(1)}, bf16[8,1024]{1,0:T(8,128)(2,1)S(1)}, u32[]{:S(2)}, u32[]{:S(2)}) collective-permute-start(bf16[8,1024]{1,0:T(8,128)(2,1)S(1)} %reduce_sum.25), channel_id=1, source_target_pairs={{0,32},{32,64},{64,96},{96,0},{1,33},{33,65},{65,97},{97,1},{2,34}... | collective-permute-start | bytes 49160 | tf_op jit(solution)/shard_map/ppermute | solution.py:290
  113.2 1.4 %collective-permute-done.9 = bf16[8,1024]{1,0:T(8,128)(2,1)S(1)} collective-permute-done((bf16[8,1024]{1,0:T(8,128)(2,1)S(1)}, bf16[8,1024]{1,0:T(8,128)(2,1)S(1)}, u32[]{:S(2)}, u32[]{:S(2)}) %collective-permute-start.9) | collective-permute-done | bytes 16416 | tf_op jit(solution)/shard_map/ppermute | solution.py:290
  114.5 3.5 %collective-permute-done.10 = bf16[8,1024]{1,0:T(8,128)(2,1)S(1)} collective-permute-done((bf16[8,1024]{1,0:T(8,128)(2,1)S(1)}, bf16[8,1024]{1,0:T(8,128)(2,1)S(1)}, u32[]{:S(2)}, u32[]{:S(2)}) %collective-permute-start.10) | collective-permute-done | bytes 16416 | tf_op jit(solution)/shard_map/ppermute | solution.py:290
  118.2 0.6 slice_bitcast_fusion
  118.7 0.6 fusion
  (37 shorter events, 1.0 us)
Async XLA Ops:
  1.5 10.2 %collective-permute-start.2 = (bf16[8,1024]{1,0:T(8,128)(2,1)S(1)}, bf16[8,1024]{1,0:T(8,128)(2,1)S(1)}, u32[]{:S(2)}, u32[]{:S(2)}) collective-permute-start(bf16[8,1024]{1,0:T(8,128)(2,1)S(1)} %constant_dynamic-slice_fusion.own_ref), channel_id=1, source_target_pairs={{0,24},{8,0},{16,8},{24,16},{1,25},{9,1},{17,9},{25,17},{2,26},{10... | collective-permute-start | bytes 49160 | tf_op jit(solution)/shard_map/ppermute | solution.py:290
  7.9 7.6 %collective-permute-start.1 = (bf16[8,1024]{1,0:T(8,128)(2,1)S(1)}, bf16[8,1024]{1,0:T(8,128)(2,1)S(1)}, u32[]{:S(2)}, u32[]{:S(2)}) collective-permute-start(bf16[8,1024]{1,0:T(8,128)(2,1)S(1)} %constant_dynamic-slice_fusion.own_ref), channel_id=1, source_target_pairs={{0,16},{8,24},{16,0},{24,8},{1,17},{9,25},{17,1},{25,9},{2,18},{10... | collective-permute-start | bytes 49160 | tf_op jit(solution)/shard_map/ppermute | solution.py:290
  8.9 6.7 %collective-permute-start = (bf16[8,1024]{1,0:T(8,128)(2,1)S(1)}, bf16[8,1024]{1,0:T(8,128)(2,1)S(1)}, u32[]{:S(2)}, u32[]{:S(2)}) collective-permute-start(bf16[8,1024]{1,0:T(8,128)(2,1)S(1)} %constant_dynamic-slice_fusion.own_ref), channel_id=1, source_target_pairs={{0,8},{8,16},{16,24},{24,0},{1,9},{9,17},{17,25},{25,1},{2,10},{10... | collective-permute-start | bytes 49160 | tf_op jit(solution)/shard_map/ppermute | solution.py:290
  16.6 21.2 %all-to-all-start = ((bf16[16,4,8,1024]{3,2,1,0:T(8,128)(2,1)}), bf16[16,4,8,1024]{3,2,1,0:T(8,128)(2,1)S(1)}, u32[]{:S(2)}, u32[]{:S(2)}) async-start(bf16[16,4,8,1024]{3,2,1,0:T(8,128)(2,1)} %spread.1), calls=%async_computation | async-start | bytes 2097152 | tf_op jit(solution)/shard_map/all_to_all | solution.py:306
  33.9 6.5 %copy-start = (bf16[1,2,256,1024]{3,2,1,0:T(8,128)(2,1)S(1)}, bf16[1,2,256,1024]{3,2,1,0:T(8,128)(2,1)}, u32[]{:S(2)}) copy-start(bf16[1,2,256,1024]{3,2,1,0:T(8,128)(2,1)} %param.9) | copy-start | bytes 3145732
  33.9 6.5 %copy-start.1 = (s32[7,256]{1,0:T(8,128)S(1)}, s32[7,256]{1,0:T(8,128)}, u32[]{:S(2)}) copy-start(s32[7,256]{1,0:T(8,128)} %nb_mid_ref.3) | copy-start | bytes 21508
  33.9 6.5 %copy-start.2 = (s32[1024]{0:T(1024)S(1)}, s32[1024]{0:T(1024)}, u32[]{:S(2)}) copy-start(s32[1024]{0:T(1024)} %param.15) | copy-start | bytes 12292
  33.9 6.5 %copy-start.3 = (s32[256]{0:T(256)S(1)}, s32[256]{0:T(256)}, u32[]{:S(2)}) copy-start(s32[256]{0:T(256)} %param.16) | copy-start | bytes 3076
  37.8 2.7 %collective-permute-start.3 = (bf16[16,4,8,1024]{3,2,1,0:T(8,128)(2,1)S(1)}, bf16[16,4,8,1024]{3,2,1,0:T(8,128)(2,1)S(1)}, u32[]{:S(2)}, u32[]{:S(2)}) collective-permute-start(bf16[16,4,8,1024]{3,2,1,0:T(8,128)(2,1)S(1)} %after.1.mine_ref), channel_id=1, source_target_pairs={{0,1},{1,0},{2,3},{3,2},{4,5},{5,4},{6,7},{7,6},{8,9},{9,8},{10,11... | collective-permute-start | bytes 3145736 | tf_op jit(solution)/shard_map/ppermute | solution.py:290
  40.5 9.8 %copy-start.6 = (f32[1,69,64]{1,2,0:T(8,128)S(1)}, f32[1,69,64]{1,2,0:T(8,128)}, u32[]{:S(2)}) copy-start(f32[1,69,64]{1,2,0:T(8,128)} %param.17) | copy-start | bytes 52996
  49.2 4.0 %collective-permute-start.4 = (f32[72,128]{1,0:T(8,128)S(1)}, f32[72,128]{1,0:T(8,128)S(1)}, u32[]{:S(2)}, u32[]{:S(2)}) collective-permute-start(f32[72,128]{1,0:T(8,128)S(1)} %get-tuple-element.11.own_ref), channel_id=1, source_target_pairs={{0,128},{128,0},{1,129},{129,1},{2,130},{130,2},{3,131},{131,3},{4... | collective-permute-start | bytes 110600 | tf_op jit(solution)/shard_map/ppermute | solution.py:290
  53.2 5.6 %collective-permute-start.7 = (f32[2,72,128]{2,1,0:T(8,128)S(1)}, f32[2,72,128]{2,1,0:T(8,128)S(1)}, u32[]{:S(2)}, u32[]{:S(2)}) collective-permute-start(f32[2,72,128]{2,1,0:T(8,128)S(1)} %pad_maximum_fusion.cohort0_ref), channel_id=1, source_target_pairs={{0,96},{32,0},{64,32},{96,64},{1,97},{33,1},{65,33},{97,65},{2,98}... | collective-permute-start | bytes 221192 | tf_op jit(solution)/shard_map/ppermute | solution.py:290
  53.7 6.2 %collective-permute-start.6 = (f32[2,72,128]{2,1,0:T(8,128)S(1)}, f32[2,72,128]{2,1,0:T(8,128)S(1)}, u32[]{:S(2)}, u32[]{:S(2)}) collective-permute-start(f32[2,72,128]{2,1,0:T(8,128)S(1)} %pad_maximum_fusion.cohort0_ref), channel_id=1, source_target_pairs={{0,64},{32,96},{64,0},{96,32},{1,65},{33,97},{65,1},{97,33},{2,66}... | collective-permute-start | bytes 221192 | tf_op jit(solution)/shard_map/ppermute | solution.py:290
  56.7 4.4 %collective-permute-start.5 = (f32[2,72,128]{2,1,0:T(8,128)S(1)}, f32[2,72,128]{2,1,0:T(8,128)S(1)}, u32[]{:S(2)}, u32[]{:S(2)}) collective-permute-start(f32[2,72,128]{2,1,0:T(8,128)S(1)} %pad_maximum_fusion.cohort0_ref), channel_id=1, source_target_pairs={{0,32},{32,64},{64,96},{96,0},{1,33},{33,65},{65,97},{97,1},{2,34}... | collective-permute-start | bytes 221192 | tf_op jit(solution)/shard_map/ppermute | solution.py:290
  61.0 1.2 %copy-start.4 = (bf16[256,1920]{1,0:T(8,128)(2,1)S(1)}, bf16[256,1920]{1,0:T(8,128)(2,1)}, u32[]{:S(2)}) copy-start(bf16[256,1920]{1,0:T(8,128)(2,1)} %get-tuple-element.13.w_hbm) | copy-start | bytes 2949124
  62.2 1.0 copy-start.5
  71.4 2.7 %collective-permute-start.8 = (bf16[4,4,4,8,1024]{4,3,2,1,0:T(8,128)(2,1)S(1)}, bf16[4,4,4,8,1024]{4,3,2,1,0:T(8,128)(2,1)S(1)}, u32[]{:S(2)}, u32[]{:S(2)}) collective-permute-start(bf16[4,4,4,8,1024]{4,3,2,1,0:T(8,128)(2,1)S(1)} %get-tuple-element.18), channel_id=1, source_target_pairs={{0,1},{1,0},{2,3},{3,2},{4,5},{5,4},{6,7},{7,6},{8,9},{9,8},{10,11... | collective-permute-start | bytes 3145736 | tf_op jit(solution)/shard_map/ppermute | solution.py:290
  109.5 5.0 %collective-permute-start.9 = (bf16[8,1024]{1,0:T(8,128)(2,1)S(1)}, bf16[8,1024]{1,0:T(8,128)(2,1)S(1)}, u32[]{:S(2)}, u32[]{:S(2)}) collective-permute-start(bf16[8,1024]{1,0:T(8,128)(2,1)S(1)} %reduce_sum.25), channel_id=1, source_target_pairs={{0,96},{32,0},{64,32},{96,64},{1,97},{33,1},{65,33},{97,65},{2,98}... | collective-permute-start | bytes 49160 | tf_op jit(solution)/shard_map/ppermute | solution.py:290
  110.1 8.0 %collective-permute-start.11 = (bf16[8,1024]{1,0:T(8,128)(2,1)S(1)}, bf16[8,1024]{1,0:T(8,128)(2,1)S(1)}, u32[]{:S(2)}, u32[]{:S(2)}) collective-permute-start(bf16[8,1024]{1,0:T(8,128)(2,1)S(1)} %reduce_sum.25), channel_id=1, source_target_pairs={{0,32},{32,64},{64,96},{96,0},{1,33},{33,65},{65,97},{97,1},{2,34}... | collective-permute-start | bytes 49160 | tf_op jit(solution)/shard_map/ppermute | solution.py:290
  112.8 5.2 %collective-permute-start.10 = (bf16[8,1024]{1,0:T(8,128)(2,1)S(1)}, bf16[8,1024]{1,0:T(8,128)(2,1)S(1)}, u32[]{:S(2)}, u32[]{:S(2)}) collective-permute-start(bf16[8,1024]{1,0:T(8,128)(2,1)S(1)} %reduce_sum.25), channel_id=1, source_target_pairs={{0,64},{32,96},{64,0},{96,32},{1,65},{33,97},{65,1},{97,33},{2,66}... | collective-permute-start | bytes 49160 | tf_op jit(solution)/shard_map/ppermute | solution.py:290

commit v4 on v3

--- a/solution.py
+++ b/solution.py
@@ -28,6 +28,9 @@
 HEAD_AT = 2 * SLOTS * CHANNELS
 WIDTH = 4096
 MIB = 1024 * 1024
+TILES_MIB = 24
+SAVED_ROWS = 8192
+MID_AT, W_AT, SLOPE1_AT, SLOPE2_AT = 0, 3584, 5632, 7680
 
 f32 = jnp.float32
 bf16 = jnp.bfloat16
@@ -66,8 +69,8 @@
             pl.BlockSpec((SLOTS, CELLS_IN), lambda j: (0, 0)),
         ],
         out_specs=pl.BlockSpec((LOCAL, 1, CHANNELS, CELLS_IN), lambda j: (0, j, 0, 0)),
-        out_shape=jax.ShapeDtypeStruct((LOCAL, SLOTS - 1, CHANNELS, CELLS_IN), bf16),
-        compiler_params=pltpu.CompilerParams(vmem_limit_bytes=56 * MIB),
+        out_shape=pltpu.HBM((LOCAL, SLOTS - 1, CHANNELS, CELLS_IN), bf16),
+        compiler_params=pltpu.CompilerParams(vmem_limit_bytes=TILES_MIB * MIB),
         cost_estimate=pl.CostEstimate(flops=6_500_000_000, bytes_accessed=8_000_000, transcendentals=0),
         name="fine_tiles",
     )(x0, nb)
@@ -75,8 +78,8 @@
 
 def forward_kernel(
     place_ref, mine_ref, other_ref, x_ref, parents_ref, nb_mid_ref, parents_mid_ref, tiles_hbm,
-    x2_ref, pred_ref, slope1_hbm, w_hbm, tiles_mid_hbm, slope2_hbm,
-    tiles_ref, w_ref, slope1_ref, tiles_mid_ref, slope2_ref, in_sem, out_sem,
+    x2_ref, pred_ref, saved_hbm,
+    tiles_ref, w_ref, saved_ref, in_sem, out_sem,
 ):
     loads = [pltpu.make_async_copy(tiles_hbm.at[m], tiles_ref.at[m], in_sem.at[m]) for m in range(LOCAL)]
     for load in loads:
@@ -89,8 +92,19 @@
                 pair = jnp.concatenate([jnp.where(first, mine, other), jnp.where(first, other, mine)], 0)
                 row = pl.multiple_of((lax.rem(z - back + 4, 4) * 4 + y) * 16, 16)
                 w_ref[pl.ds(row, 16), x * QUARTER : (x + 1) * QUARTER] = pair.astype(bf16)
-    stores = [pltpu.make_async_copy(w_ref.at[:, SECOND_AT : HEAD_AT + 128], w_hbm, out_sem.at[0])]
-    stores[0].start()
+    saved_ref[W_AT + SECOND_AT : SLOPE1_AT, 128:256] = jnp.zeros((CHANNELS, 128), bf16)
+    saved_ref[W_AT + SECOND_AT : SLOPE1_AT, 0:128] = w_ref[:, HEAD_AT : HEAD_AT + 128]
+    for j in range(SLOTS):
+        at = SECOND_AT + j * CHANNELS
+        saved_ref[W_AT + j * CHANNELS : W_AT + (j + 1) * CHANNELS] = w_ref[:, at : at + CHANNELS]
+    stores = []
+
+    def save(begin, end):
+        rows = slice(begin, end)
+        stores.append(pltpu.make_async_copy(saved_ref.at[rows], saved_hbm.at[rows], out_sem.at[len(stores)]))
+        stores[-1].start()
+
+    save(W_AT, SLOPE1_AT)
     unpool = one_hot(parents_ref[...], CELLS_MID)
     x1 = []
     for m in range(LOCAL):
@@ -102,29 +116,31 @@
             for j in range(1, SLOTS):
                 a1 = a1 + dot(w_ref[:, j * CHANNELS : (j + 1) * CHANNELS], tiles_ref[m, j - 1, :, cells])
             gate = jax.nn.sigmoid(a1)
-            slope1_ref[m, :, cells] = (gate * (1.0 + a1 * (1.0 - gate))).astype(bf16)
+            slope1 = (gate * (1.0 + a1 * (1.0 - gate))).astype(bf16)
+            for half in range(2):
+                row = SLOPE1_AT + m * CELLS_IN + at + half * 256
+                saved_ref[row : row + 256] = slope1[:, half * 256 : (half + 1) * 256]
             h1 = (x_ref[m, :, cells].astype(f32) + a1 * gate).astype(bf16)
             pooled = pooled + dot_bt(h1, unpool[:, cells])
-        stores.append(pltpu.make_async_copy(slope1_ref.at[m], slope1_hbm.at[m], out_sem.at[1 + m]))
-        stores[-1].start()
+        save(SLOPE1_AT + m * CELLS_IN, SLOPE1_AT + (m + 1) * CELLS_IN)
         x1.append((pooled * 0.25).astype(bf16))
-        tiles_mid_ref[m, 0:CHANNELS] = x1[m]
+        saved_ref[m * SECOND_AT : m * SECOND_AT + CHANNELS] = x1[m]
     both = jnp.concatenate(x1, 0)
     for j in range(1, SLOTS):
         tile = dot(both, one_hot(nb_mid_ref[j : j + 1, :], CELLS_MID)).astype(bf16)
         for m in range(LOCAL):
-            tiles_mid_ref[m, j * CHANNELS : (j + 1) * CHANNELS] = tile[m * CHANNELS : (m + 1) * CHANNELS]
-    stores.append(pltpu.make_async_copy(tiles_mid_ref, tiles_mid_hbm, out_sem.at[3]))
-    stores[-1].start()
+            row = m * SECOND_AT + j * CHANNELS
+            saved_ref[row : row + CHANNELS] = tile[m * CHANNELS : (m + 1) * CHANNELS]
+    save(MID_AT, W_AT)
     pool = one_hot(parents_mid_ref[...], CELLS_OUT)
     for m in range(LOCAL):
-        a2 = dot(w_ref[:, SECOND_AT:HEAD_AT], tiles_mid_ref[m])
+        a2 = dot(w_ref[:, SECOND_AT:HEAD_AT], saved_ref[m * SECOND_AT : (m + 1) * SECOND_AT])
         gate2 = jax.nn.sigmoid(a2)
-        slope2_ref[m] = gate2 * (1.0 + a2 * (1.0 - gate2))
+        row = SLOPE2_AT + m * CHANNELS
+        saved_ref[row : row + CHANNELS] = (gate2 * (1.0 + a2 * (1.0 - gate2))).astype(bf16)
         h2 = (x1[m].astype(f32) + a2 * gate2).astype(bf16)
         x2_ref[:, m * CELLS_OUT : (m + 1) * CELLS_OUT] = (dot_bt(h2, pool) * 0.25).astype(bf16)
-    stores.append(pltpu.make_async_copy(slope2_ref, slope2_hbm, out_sem.at[4]))
-    stores[-1].start()
+    save(SLOPE2_AT, SAVED_ROWS)
     pred = dot_at(w_ref[:, HEAD_AT : HEAD_AT + 128], x2_ref[...])
     pred_ref[...] = pred[0:FIELD_ROWS]
     for store in stores:
@@ -168,28 +184,22 @@
 HBM = pl.BlockSpec(memory_space=pltpu.HBM)
 SMEM = pl.BlockSpec(memory_space=pltpu.SMEM)
 TILES = (LOCAL, SLOTS - 1, CHANNELS, CELLS_IN)
-BACK_W = SECOND_AT + 128
 
 
 def forward(place, mine, other, x0, tiles, parents_fine, nb_mid, parents_mid):
     return pl.pallas_call(
         forward_kernel,
         in_specs=[SMEM, VMEM, VMEM, VMEM, VMEM, VMEM, VMEM, HBM],
-        out_specs=[VMEM, VMEM, HBM, HBM, HBM, HBM],
+        out_specs=[VMEM, VMEM, HBM],
         out_shape=[
             jax.ShapeDtypeStruct((CHANNELS, LOCAL * CELLS_OUT), bf16),
             jax.ShapeDtypeStruct((FIELD_ROWS, LOCAL * CELLS_OUT), f32),
-            pltpu.HBM((LOCAL, CHANNELS, CELLS_IN), bf16),
-            pltpu.HBM((CHANNELS, BACK_W), bf16),
-            pltpu.HBM((LOCAL, SECOND_AT, CELLS_MID), bf16),
-            pltpu.HBM((LOCAL, CHANNELS, CELLS_MID), f32),
+            pltpu.HBM((SAVED_ROWS, CELLS_MID), bf16),
         ],
         scratch_shapes=[
             pltpu.VMEM(TILES, bf16),
             pltpu.VMEM((CHANNELS, WIDTH), bf16),
-            pltpu.VMEM((LOCAL, CHANNELS, CELLS_IN), bf16),
-            pltpu.VMEM((LOCAL, SECOND_AT, CELLS_MID), bf16),
-            pltpu.VMEM((LOCAL, CHANNELS, CELLS_MID), f32),
+            pltpu.VMEM((SAVED_ROWS, CELLS_MID), bf16),
             pltpu.SemaphoreType.DMA((LOCAL,)),
             pltpu.SemaphoreType.DMA((5,)),
         ],
@@ -205,11 +215,11 @@
 
 def backward_kernel(
     place_ref, cohort0_ref, cohort1_ref, cohort2_ref, cohort3_ref, own_ref, obs_ref, x2_ref,
-    parents_ref, nb_mid_ref, parents_mid_ref, w_hbm, tiles_mid_hbm, slope2_hbm, slope1_hbm, x_hbm, tiles_hbm,
+    parents_ref, nb_mid_ref, parents_mid_ref, saved_hbm, x_hbm, tiles_hbm,
     kept_ref, sent_ref,
-    w_ref, tiles_mid_ref, slope2_ref, slope1_ref, x_ref, tiles_ref, g1_ref, sem,
+    saved_ref, x_ref, tiles_ref, g1_ref, sem,
 ):
-    moves = ((w_hbm, w_ref), (slope2_hbm, slope2_ref), (tiles_mid_hbm, tiles_mid_ref), (slope1_hbm, slope1_ref), (x_hbm, x_ref), (tiles_hbm, tiles_ref))
+    moves = ((saved_hbm, saved_ref), (x_hbm, x_ref), (tiles_hbm, tiles_ref))
     loads = [pltpu.make_async_copy(source, here, sem.at[i]) for i, (source, here) in enumerate(moves)]
     for load in loads:
         load.start()
@@ -236,27 +246,29 @@
     put(3, 640, 384, jnp.zeros((CHANNELS, 384), f32))
     pool = one_hot(parents_mid_ref[...], CELLS_OUT)
     wide = [dot(slope[:, m * CELLS_OUT : (m + 1) * CELLS_OUT], pool).astype(bf16) for m in range(LOCAL)]
-    for load in loads[:4]:
-        load.wait()
-    head_t = w_ref[:, SECOND_AT:BACK_W]
+    loads[0].wait()
+    head_t = saved_ref[W_AT + SECOND_AT : SLOPE1_AT, 0:128]
     dh2 = [dot(head_t, wide[m]) * 0.25 for m in range(LOCAL)]
-    g2 = [(dh2[m] * slope2_ref[m]).astype(bf16) for m in range(LOCAL)]
+    slope2 = saved_ref[SLOPE2_AT:SAVED_ROWS].astype(f32)
+    g2 = [(dh2[m] * slope2[m * CHANNELS : (m + 1) * CHANNELS]).astype(bf16) for m in range(LOCAL)]
     both = jnp.concatenate(g2, 0)
-    back = [dh2[m] + dot_at(w_ref[:, 0:CHANNELS], g2[m]) for m in range(LOCAL)]
+    back = [dh2[m] + dot_at(saved_ref[W_AT : W_AT + CHANNELS], g2[m]) for m in range(LOCAL)]
     for q in range(1, SLOTS):
         spread_back = dot_bt(both, one_hot(nb_mid_ref[q : q + 1, :], CELLS_MID)).astype(bf16)
-        weight = w_ref[:, q * CHANNELS : (q + 1) * CHANNELS]
+        weight = saved_ref[W_AT + q * CHANNELS : W_AT + (q + 1) * CHANNELS]
         for m in range(LOCAL):
             back[m] = back[m] + dot_at(weight, spread_back[m * CHANNELS : (m + 1) * CHANNELS])
     unpool = one_hot(parents_ref[...], CELLS_MID)
     for m in range(LOCAL):
         dh1 = dot((back[m] * 0.25).astype(bf16), unpool)
-        g1_ref[m] = (dh1 * slope1_ref[m].astype(f32)).astype(bf16)
-    for load in loads[4:]:
+        for at in range(0, CELLS_IN, 256):
+            slope1 = saved_ref[SLOPE1_AT + m * CELLS_IN + at : SLOPE1_AT + m * CELLS_IN + at + 256].astype(f32)
+            g1_ref[m, :, at : at + 256] = (dh1[:, at : at + 256] * slope1).astype(bf16)
+    for load in loads[1:]:
         load.wait()
     for q in range(SLOTS):
-        rows = slice(q * CHANNELS, (q + 1) * CHANNELS)
-        grad = dot_bt(g2[0], tiles_mid_ref[0, rows]) + dot_bt(g2[1], tiles_mid_ref[1, rows])
+        row0, row1 = q * CHANNELS, SECOND_AT + q * CHANNELS
+        grad = dot_bt(g2[0], saved_ref[row0 : row0 + CHANNELS]) + dot_bt(g2[1], saved_ref[row1 : row1 + CHANNELS])
         put((SLOTS + q) // 4, (SLOTS + q) % 4 * 256, 256, grad)
     put(0, 0, 256, dot_bt(g1_ref[0], x_ref[0]) + dot_bt(g1_ref[1], x_ref[1]))
     for j in range(1, SLOTS):
@@ -264,26 +276,23 @@
         put(j // 4, j % 4 * 256, 256, grad)
 
 
-def backward(place, cohort, own, obs, w, tiles_mid, slope2, x2, slope1, x0, tiles, parents_fine, nb_mid, parents_mid):
+def backward(place, cohort, own, obs, x2, saved, x0, tiles, parents_fine, nb_mid, parents_mid):
     return pl.pallas_call(
         backward_kernel,
-        in_specs=[SMEM] + [VMEM] * 10 + [HBM] * 6,
+        in_specs=[SMEM] + [VMEM] * 10 + [HBM] * 3,
         out_specs=[VMEM] * 2,
         out_shape=[jax.ShapeDtypeStruct((4, 4, 4, 8, QUARTER), bf16)] * 2,
         scratch_shapes=[
-            pltpu.VMEM((CHANNELS, BACK_W), bf16),
-            pltpu.VMEM((LOCAL, SECOND_AT, CELLS_MID), bf16),
-            pltpu.VMEM((LOCAL, CHANNELS, CELLS_MID), f32),
-            pltpu.VMEM((LOCAL, CHANNELS, CELLS_IN), bf16),
+            pltpu.VMEM((SAVED_ROWS, CELLS_MID), bf16),
             pltpu.VMEM((LOCAL, CHANNELS, CELLS_IN), bf16),
             pltpu.VMEM(TILES, bf16),
             pltpu.VMEM((LOCAL, CHANNELS, CELLS_IN), bf16),
-            pltpu.SemaphoreType.DMA((6,)),
+            pltpu.SemaphoreType.DMA((3,)),
         ],
         compiler_params=pltpu.CompilerParams(vmem_limit_bytes=50 * MIB),
         cost_estimate=pl.CostEstimate(flops=4_000_000_000, bytes_accessed=16_000_000, transcendentals=200_000),
         name="backward",
-    )(place, *cohort, own, obs, x2, parents_fine, nb_mid, parents_mid, w, tiles_mid, slope2, slope1, x0, tiles)
+    )(place, *cohort, own, obs, x2, parents_fine, nb_mid, parents_mid, saved, x0, tiles)
 
 
 def shift(v, axis, n, by):
@@ -314,9 +323,33 @@
     column = jnp.broadcast_to(total[:, None], (4, 2, 8, QUARTER)).reshape(8, 8, QUARTER)
     column = lax.all_to_all(column, ("z_hi", "z_lo"), 0, 0)
     total = jnp.sum(column.astype(f32), 0).astype(bf16)
-    back = [total] + [shift(total, "x", 4, s) for s in (1, 2, 3)]
-    ring = jnp.stack([back[i] for i in (3, 2, 1, 0, 3, 2, 1)])
-    return lax.dynamic_slice_in_dim(ring, 3 - x, 4, 0).astype(f32).transpose(1, 0, 2).reshape(8, WIDTH)
+    return finish(x.astype(jnp.int32).reshape(1), [total] + [shift(total, "x", 4, s) for s in (1, 2, 3)])
+
+
+def finish_kernel(x_ref, own_ref, back1_ref, back2_ref, back3_ref, first_ref, second_ref, head_ref, slots_ref):
+    for back, source in enumerate((own_ref, back1_ref, back2_ref, back3_ref)):
+        at = lax.rem(x_ref[0] - back + 4, 4) * 4
+        for slot in range(4):
+            slots_ref[at + slot] = source[:, slot * CHANNELS : (slot + 1) * CHANNELS].astype(f32)
+    first_ref[...] = slots_ref[0:SLOTS]
+    second_ref[...] = slots_ref[SLOTS : 2 * SLOTS]
+    head_ref[...] = slots_ref[2 * SLOTS, :, 0:FIELDS]
+
+
+def finish(x, quarters):
+    return pl.pallas_call(
+        finish_kernel,
+        in_specs=[SMEM] + [VMEM] * 4,
+        out_specs=[VMEM] * 3,
+        out_shape=[
+            jax.ShapeDtypeStruct((SLOTS, 8, CHANNELS), f32),
+            jax.ShapeDtypeStruct((SLOTS, 8, CHANNELS), f32),
+            jax.ShapeDtypeStruct((8, FIELDS), f32),
+        ],
+        scratch_shapes=[pltpu.VMEM((16, 8, CHANNELS), f32)],
+        compiler_params=pltpu.CompilerParams(vmem_limit_bytes=16 * MIB),
+        name="finish",
+    )(x, *quarters)
 
 
 def per_device(
@@ -333,20 +366,14 @@
 
     tiles = fine_tiles(x0.reshape(LOCAL * CHANNELS, CELLS_IN), neighbours_fine)
     mine, other = gather_weights(weight_first, weight_second, weight_head, x, tiles)
-    x2, pred, slope1, w, tiles_mid, slope2 = forward(
+    x2, pred, saved = forward(
         place, mine, other, x0, tiles, parents_fine, neighbours_mid, parents_mid
     )
     pair = jnp.stack([pred, shift(pred, "z_lo", 2, 1)])
     cohort = [pair] + [shift(pair, "x", 4, s) for s in (1, 2, 3)]
-    kept, sent = backward(
-        place, cohort, pred, truth, w, tiles_mid, slope2, x2, slope1, x0, tiles, parents_fine, neighbours_mid, parents_mid
-    )
-    rows = reduce_gradients(kept, sent, x)
-    return (
-        rows[:, :SECOND_AT].reshape(8, SLOTS, CHANNELS).transpose(1, 0, 2),
-        rows[:, SECOND_AT:HEAD_AT].reshape(8, SLOTS, CHANNELS).transpose(1, 0, 2),
-        rows[:, HEAD_AT : HEAD_AT + FIELDS].T,
-    )
+    kept, sent = backward(place, cohort, pred, truth, x2, saved, x0, tiles, parents_fine, neighbours_mid, parents_mid)
+    grad_first, grad_second, grad_head = reduce_gradients(kept, sent, x)
+    return grad_first, grad_second, grad_head.T
 
 
 def solution(mesh):

time: 120 us -> 115 us (0.958)
  local copies, waits for them, and re-layouts: 4.49 us -> 1.07 us
    unnamed x21 -> x13, local copies, waits for them, and re-layouts: 2.37 us -> 0.11 us
    ppermute x12, waiting for transfers between devices: 20.4 us -> 19 us  [shift(): return lax.ppermute(v, axis, [(i, (i + by) % n) for i in range(n)])]
    pallas_call x1, Pallas kernels: 9.93 us -> 8.67 us  [fine_tiles(): pl.pallas_call(tiles_kernel, grid=(SLOTS - 1,), in_specs=[pl.BlockSpec((L...]
    all_to_all x1, waiting for transfers between devices: 3.85 us -> 5.11 us  [gather_weights(): plane = after(lax.all_to_all(column, ('x', 'y'), 0, 0), tiles)]
    pallas_call x1 -> x2, Pallas kernels: 8.07 us -> 8.6 us  [the longest x1 7.93 us: backward(): pl.pallas_call(backward_kernel, in_specs=[SMEM] + [VMEM] * 10 + [HBM] * 3...]
  transfers between devices with their start and end apart: 13 -> 13, of which waited for: 10 -> 11; matrix products, arithmetic and copies ran while one was open for 0% -> 0% of each run, Pallas kernels for 8% -> 8%
where the time goes in v4:
time: 115 us
  blocking collectives  34.7 us (30%)
  starting transfers between devices  26.8 us (23%)
  Pallas kernels  26.8 us (23%)
  waiting for transfers between devices  24.1 us (21%)
    all_to_all x1, blocking collectives, reduce_gradients(): plane = lax.all_to_all(total.reshape(16, 4, 8, QUARTER), ('x', 'y'), 0, 0)  20.7 us
    ppermute x12, starting transfers between devices, shift(): return lax.ppermute(v, axis, [(i, (i + by) % n) for i in range(n)])  19.4 us
    ppermute x12, waiting for transfers between devices, shift(): return lax.ppermute(v, axis, [(i, (i + by) % n) for i in range(n)])  19 us
    all_to_all x1, blocking collectives, reduce_gradients(): column = lax.all_to_all(column, ('z_hi', 'z_lo'), 0, 0)  14 us
    pallas_call x1, Pallas kernels, fine_tiles(): pl.pallas_call(tiles_kernel, grid=(SLOTS - 1,), in_specs=[pl.BlockSpec((L...  8.67 us
    pallas_call x1, Pallas kernels, forward(): pl.pallas_call(forward_kernel, in_specs=[SMEM, VMEM, VMEM, VMEM, VMEM, VM...  8.43 us
    pallas_call x1, Pallas kernels, backward(): pl.pallas_call(backward_kernel, in_specs=[SMEM] + [VMEM] * 10 + [HBM] * 3...  7.93 us
    all_to_all x1, starting transfers between devices, gather_weights(): plane = after(lax.all_to_all(column, ('x', 'y'), 0, 0), tiles)  7.43 us
  transfers between devices with their start and end apart: 13, of which 11 were waited for; matrix products, arithmetic and copies ran while one was open for 0% of the time, Pallas kernels for 8%

profile of v4, /device:TPU:6, one launch (start us, length us, event | category | flops | bytes accessed | tf_op | source)
XLA Modules:
  0.0 115.1 jit_solution(7565141336045411094)
XLA Ops:
  0.7 0.9 concatenate.6
  1.6 6.4 %collective-permute-start.2 = (bf16[8,1024]{1,0:T(8,128)(2,1)S(1)}, bf16[8,1024]{1,0:T(8,128)(2,1)S(1)}, u32[]{:S(2)}, u32[]{:S(2)}) collective-permute-start(bf16[8,1024]{1,0:T(8,128)(2,1)S(1)} %constant_dynamic-slice_fusion.own_ref), channel_id=1, source_target_pairs={{0,24},{8,0},{16,8},{24,16},{1,25},{9,1},{17,9},{25,17},{2,26},{10... | collective-permute-start | bytes 49160 | tf_op jit(solution)/shard_map/ppermute | solution.py:299
  8.0 1.0 collective-permute-start.1
  9.0 2.8 %collective-permute-start = (bf16[8,1024]{1,0:T(8,128)(2,1)S(1)}, bf16[8,1024]{1,0:T(8,128)(2,1)S(1)}, u32[]{:S(2)}, u32[]{:S(2)}) collective-permute-start(bf16[8,1024]{1,0:T(8,128)(2,1)S(1)} %constant_dynamic-slice_fusion.own_ref), channel_id=1, source_target_pairs={{0,8},{8,16},{16,24},{24,0},{1,9},{9,17},{17,25},{25,1},{2,10},{10... | collective-permute-start | bytes 49160 | tf_op jit(solution)/shard_map/ppermute | solution.py:299
  11.8 3.8 %collective-permute-done.1.back2_ref = bf16[8,1024]{1,0:T(8,128)(2,1)S(1)} collective-permute-done((bf16[8,1024]{1,0:T(8,128)(2,1)S(1)}, bf16[8,1024]{1,0:T(8,128)(2,1)S(1)}, u32[]{:S(2)}, u32[]{:S(2)}) %collective-permute-start.1) | collective-permute-done | bytes 16416 | tf_op jit(solution)/shard_map/ppermute | solution.py:299
  15.6 1.1 spread.1
  16.7 7.4 %all-to-all-start = ((bf16[16,4,8,1024]{3,2,1,0:T(8,128)(2,1)}), bf16[16,4,8,1024]{3,2,1,0:T(8,128)(2,1)S(1)}, u32[]{:S(2)}, u32[]{:S(2)}) async-start(bf16[16,4,8,1024]{3,2,1,0:T(8,128)(2,1)} %spread.1), calls=%async_computation | async-start | bytes 2097152 | tf_op jit(solution)/shard_map/all_to_all | solution.py:315
  24.1 8.7 %fine_tiles.1.first_ref.tiles_hbm = bf16[2,6,256,1024]{3,2,1,0:T(8,128)(2,1)} custom-call(bf16[512,1024]{1,0:T(8,128)(2,1)S(1)} %bitcast.21, s32[7,1024]{1,0:T(8,128)S(1)} %copy-done.1), custom_call_target="tpu_custom_call" | custom-call | flops 6499999744 | bytes 8000000 | tf_op jit(solution)/shard_map/fine_tiles/pallas_call | solution.py:64
  32.8 5.1 %all-to-all-done.value_ref = bf16[16,4,8,1024]{3,2,1,0:T(8,128)(2,1)S(1)} async-done(((bf16[16,4,8,1024]{3,2,1,0:T(8,128)(2,1)}), bf16[16,4,8,1024]{3,2,1,0:T(8,128)(2,1)S(1)}, u32[]{:S(2)}, u32[]{:S(2)}) %all-to-all-start) | async-done | bytes 1048608 | tf_op jit(solution)/shard_map/all_to_all | solution.py:315
  38.0 2.6 %collective-permute-done.3.other_ref = bf16[16,4,8,1024]{3,2,1,0:T(8,128)(2,1)S(1)} collective-permute-done((bf16[16,4,8,1024]{3,2,1,0:T(8,128)(2,1)S(1)}, bf16[16,4,8,1024]{3,2,1,0:T(8,128)(2,1)S(1)}, u32[]{:S(2)}, u32[]{:S(2)}) %collective-permute-start.3) | collective-permute-done | bytes 1048608 | tf_op jit(solution)/shard_map/ppermute | solution.py:299
  40.6 8.4 %forward.1 = (bf16[256,128]{1,0:T(8,128)(2,1)S(1)}, f32[72,128]{1,0:T(8,128)S(1)}, bf16[8192,256]{1,0:T(8,128)(2,1)}) custom-call(s32[2]{0:T(128)S(1)} %pad_add_fusion.place_ref, bf16[16,4,8,1024]{3,2,1,0:T(8,128)(2,1)S(1)} %after.1.mine_ref, bf16[16,4,8,1024]{3,2,1,0:T(8,128)(2,1)S(1)} %collective-permute-done.3.other_ref, ...), custom_call_target="tpu_custom_call" | custom-call | flops 3200000000 | bytes 14000000 | tf_op jit(solution)/shard_map/forward/pallas_call | solution.py:190
  49.0 1.1 collective-permute-start.4
  50.3 2.8 %collective-permute-done.4 = f32[72,128]{1,0:T(8,128)S(1)} collective-permute-done((f32[72,128]{1,0:T(8,128)S(1)}, f32[72,128]{1,0:T(8,128)S(1)}, u32[]{:S(2)}, u32[]{:S(2)}) %collective-permute-start.4) | collective-permute-done | bytes 36896 | tf_op jit(solution)/shard_map/ppermute | solution.py:299
  53.1 0.4 collective-permute-start.7
  53.5 3.0 %collective-permute-start.6 = (f32[2,72,128]{2,1,0:T(8,128)S(1)}, f32[2,72,128]{2,1,0:T(8,128)S(1)}, u32[]{:S(2)}, u32[]{:S(2)}) collective-permute-start(f32[2,72,128]{2,1,0:T(8,128)S(1)} %pad_maximum_fusion.cohort0_ref), channel_id=1, source_target_pairs={{0,64},{32,96},{64,0},{96,32},{1,65},{33,97},{65,1},{97,33},{2,66}... | collective-permute-start | bytes 221192 | tf_op jit(solution)/shard_map/ppermute | solution.py:299
  56.6 0.6 collective-permute-start.5
  57.3 1.4 %collective-permute-done.7.cohort3_ref = f32[2,72,128]{2,1,0:T(8,128)S(1)} collective-permute-done((f32[2,72,128]{2,1,0:T(8,128)S(1)}, f32[2,72,128]{2,1,0:T(8,128)S(1)}, u32[]{:S(2)}, u32[]{:S(2)}) %collective-permute-start.7) | collective-permute-done | bytes 73760 | tf_op jit(solution)/shard_map/ppermute | solution.py:299
  58.7 1.0 collective-permute-done.6.cohort2_ref
  59.7 1.2 %collective-permute-done.5.cohort1_ref = f32[2,72,128]{2,1,0:T(8,128)S(1)} collective-permute-done((f32[2,72,128]{2,1,0:T(8,128)S(1)}, f32[2,72,128]{2,1,0:T(8,128)S(1)}, u32[]{:S(2)}, u32[]{:S(2)}) %collective-permute-start.5) | collective-permute-done | bytes 73760 | tf_op jit(solution)/shard_map/ppermute | solution.py:299
  60.9 7.9 %backward.1 = (bf16[4,4,4,8,1024]{4,3,2,1,0:T(8,128)(2,1)S(1)}, bf16[4,4,4,8,1024]{4,3,2,1,0:T(8,128)(2,1)S(1)}) custom-call(s32[2]{0:T(128)S(1)} %pad_add_fusion.place_ref, f32[2,72,128]{2,1,0:T(8,128)S(1)} %pad_maximum_fusion.cohort0_ref, f32[2,72,128]{2,1,0:T(8,128)S(1)} %collective-permute-done.5.cohort1_ref, ...), custom_call_target="tpu_custom_call" | custom-call | flops 4000000000 | bytes 16000000 | tf_op jit(solution)/shard_map/backward/pallas_call | solution.py:280
  69.0 2.6 %collective-permute-done.8 = bf16[4,4,4,8,1024]{4,3,2,1,0:T(8,128)(2,1)S(1)} collective-permute-done((bf16[4,4,4,8,1024]{4,3,2,1,0:T(8,128)(2,1)S(1)}, bf16[4,4,4,8,1024]{4,3,2,1,0:T(8,128)(2,1)S(1)}, u32[]{:S(2)}, u32[]{:S(2)}) %collective-permute-start.8) | collective-permute-done | bytes 1048608 | tf_op jit(solution)/shard_map/ppermute | solution.py:299
  71.6 0.4 add_convert_fusion
  72.0 20.7 %all_to_all.15 = bf16[16,4,8,1024]{3,2,1,0:T(8,128)(2,1)S(1)} all-to-all(bf16[16,4,8,1024]{3,2,1,0:T(8,128)(2,1)S(1)} %bitcast.28), channel_id=1, replica_groups=mesh['z_lo'=2,'x'=4,'z_hi'=4,'y'=4,'core'=2] {'x','y'}, dimensions={0} | all-to-all | bytes 2097152 | tf_op jit(solution)/shard_map/all_to_all | solution.py:321
  92.8 0.2 reduce_sum.24
  93.0 14.0 %all_to_all.16 = bf16[8,8,1024]{2,1,0:T(8,128)(2,1)S(1)} all-to-all(bf16[8,8,1024]{2,1,0:T(8,128)(2,1)S(1)} %bitcast.29), channel_id=1, replica_groups=mesh['z_lo'=2,'x'=4,'z_hi'=4,'y'=4,'core'=2] {'z_hi','z_lo'}, dimensions={0} | all-to-all | bytes 262144 | tf_op jit(solution)/shard_map/all_to_all | solution.py:324
  107.0 0.6 collective-permute-start.11
  107.6 3.1 %collective-permute-start.10 = (bf16[8,1024]{1,0:T(8,128)(2,1)S(1)}, bf16[8,1024]{1,0:T(8,128)(2,1)S(1)}, u32[]{:S(2)}, u32[]{:S(2)}) collective-permute-start(bf16[8,1024]{1,0:T(8,128)(2,1)S(1)} %reduce_sum.25.own_ref), channel_id=1, source_target_pairs={{0,64},{32,96},{64,0},{96,32},{1,65},{33,97},{65,1},{97,33},{2,66}... | collective-permute-start | bytes 49160 | tf_op jit(solution)/shard_map/ppermute | solution.py:299
  110.7 0.2 collective-permute-start.9
  110.9 1.1 collective-permute-done.11.back3_ref
  112.0 0.8 collective-permute-done.10.back2_ref
  112.8 1.6 %collective-permute-done.9.back1_ref = bf16[8,1024]{1,0:T(8,128)(2,1)S(1)} collective-permute-done((bf16[8,1024]{1,0:T(8,128)(2,1)S(1)}, bf16[8,1024]{1,0:T(8,128)(2,1)S(1)}, u32[]{:S(2)}, u32[]{:S(2)}) %collective-permute-start.9) | collective-permute-done | bytes 16416 | tf_op jit(solution)/shard_map/ppermute | solution.py:299
  114.4 0.7 finish.1
  (26 shorter events, 0.4 us)
Async XLA Ops:
  0.6 23.5 %copy-start = (bf16[1,2,256,1024]{3,2,1,0:T(8,128)(2,1)S(1)}, bf16[1,2,256,1024]{3,2,1,0:T(8,128)(2,1)}, u32[]{:S(2)}) copy-start(bf16[1,2,256,1024]{3,2,1,0:T(8,128)(2,1)} %param.9) | copy-start | bytes 3145732
  0.6 23.5 %copy-start.1 = (s32[7,1024]{1,0:T(8,128)S(1)}, s32[7,1024]{1,0:T(8,128)}, u32[]{:S(2)}) copy-start(s32[7,1024]{1,0:T(8,128)} %nb_ref.1) | copy-start | bytes 86020
  1.6 10.2 %collective-permute-start.2 = (bf16[8,1024]{1,0:T(8,128)(2,1)S(1)}, bf16[8,1024]{1,0:T(8,128)(2,1)S(1)}, u32[]{:S(2)}, u32[]{:S(2)}) collective-permute-start(bf16[8,1024]{1,0:T(8,128)(2,1)S(1)} %constant_dynamic-slice_fusion.own_ref), channel_id=1, source_target_pairs={{0,24},{8,0},{16,8},{24,16},{1,25},{9,1},{17,9},{25,17},{2,26},{10... | collective-permute-start | bytes 49160 | tf_op jit(solution)/shard_map/ppermute | solution.py:299
  8.0 7.6 %collective-permute-start.1 = (bf16[8,1024]{1,0:T(8,128)(2,1)S(1)}, bf16[8,1024]{1,0:T(8,128)(2,1)S(1)}, u32[]{:S(2)}, u32[]{:S(2)}) collective-permute-start(bf16[8,1024]{1,0:T(8,128)(2,1)S(1)} %constant_dynamic-slice_fusion.own_ref), channel_id=1, source_target_pairs={{0,16},{8,24},{16,0},{24,8},{1,17},{9,25},{17,1},{25,9},{2,18},{10... | collective-permute-start | bytes 49160 | tf_op jit(solution)/shard_map/ppermute | solution.py:299
  9.0 6.7 %collective-permute-start = (bf16[8,1024]{1,0:T(8,128)(2,1)S(1)}, bf16[8,1024]{1,0:T(8,128)(2,1)S(1)}, u32[]{:S(2)}, u32[]{:S(2)}) collective-permute-start(bf16[8,1024]{1,0:T(8,128)(2,1)S(1)} %constant_dynamic-slice_fusion.own_ref), channel_id=1, source_target_pairs={{0,8},{8,16},{16,24},{24,0},{1,9},{9,17},{17,25},{25,1},{2,10},{10... | collective-permute-start | bytes 49160 | tf_op jit(solution)/shard_map/ppermute | solution.py:299
  16.7 21.2 %all-to-all-start = ((bf16[16,4,8,1024]{3,2,1,0:T(8,128)(2,1)}), bf16[16,4,8,1024]{3,2,1,0:T(8,128)(2,1)S(1)}, u32[]{:S(2)}, u32[]{:S(2)}) async-start(bf16[16,4,8,1024]{3,2,1,0:T(8,128)(2,1)} %spread.1), calls=%async_computation | async-start | bytes 2097152 | tf_op jit(solution)/shard_map/all_to_all | solution.py:315
  32.8 7.8 %copy-start.2 = (s32[7,256]{1,0:T(8,128)S(1)}, s32[7,256]{1,0:T(8,128)}, u32[]{:S(2)}) copy-start(s32[7,256]{1,0:T(8,128)} %nb_mid_ref.3) | copy-start | bytes 21508
  32.8 7.8 %copy-start.3 = (s32[1024]{0:T(1024)S(1)}, s32[1024]{0:T(1024)}, u32[]{:S(2)}) copy-start(s32[1024]{0:T(1024)} %param.15) | copy-start | bytes 12292
  32.8 7.8 %copy-start.4 = (s32[256]{0:T(256)S(1)}, s32[256]{0:T(256)}, u32[]{:S(2)}) copy-start(s32[256]{0:T(256)} %param.16) | copy-start | bytes 3076
  37.9 2.7 %collective-permute-start.3 = (bf16[16,4,8,1024]{3,2,1,0:T(8,128)(2,1)S(1)}, bf16[16,4,8,1024]{3,2,1,0:T(8,128)(2,1)S(1)}, u32[]{:S(2)}, u32[]{:S(2)}) collective-permute-start(bf16[16,4,8,1024]{3,2,1,0:T(8,128)(2,1)S(1)} %after.1.mine_ref), channel_id=1, source_target_pairs={{0,1},{1,0},{2,3},{3,2},{4,5},{5,4},{6,7},{7,6},{8,9},{9,8},{10,11... | collective-permute-start | bytes 3145736 | tf_op jit(solution)/shard_map/ppermute | solution.py:299
  40.6 9.6 %copy-start.5 = (f32[1,69,64]{1,2,0:T(8,128)S(1)}, f32[1,69,64]{1,2,0:T(8,128)}, u32[]{:S(2)}) copy-start(f32[1,69,64]{1,2,0:T(8,128)} %param.17) | copy-start | bytes 52996
  49.0 4.0 %collective-permute-start.4 = (f32[72,128]{1,0:T(8,128)S(1)}, f32[72,128]{1,0:T(8,128)S(1)}, u32[]{:S(2)}, u32[]{:S(2)}) collective-permute-start(f32[72,128]{1,0:T(8,128)S(1)} %get-tuple-element.11.own_ref), channel_id=1, source_target_pairs={{0,128},{128,0},{1,129},{129,1},{2,130},{130,2},{3,131},{131,3},{4... | collective-permute-start | bytes 110600 | tf_op jit(solution)/shard_map/ppermute | solution.py:299
  53.1 5.6 %collective-permute-start.7 = (f32[2,72,128]{2,1,0:T(8,128)S(1)}, f32[2,72,128]{2,1,0:T(8,128)S(1)}, u32[]{:S(2)}, u32[]{:S(2)}) collective-permute-start(f32[2,72,128]{2,1,0:T(8,128)S(1)} %pad_maximum_fusion.cohort0_ref), channel_id=1, source_target_pairs={{0,96},{32,0},{64,32},{96,64},{1,97},{33,1},{65,33},{97,65},{2,98}... | collective-permute-start | bytes 221192 | tf_op jit(solution)/shard_map/ppermute | solution.py:299
  53.5 6.2 %collective-permute-start.6 = (f32[2,72,128]{2,1,0:T(8,128)S(1)}, f32[2,72,128]{2,1,0:T(8,128)S(1)}, u32[]{:S(2)}, u32[]{:S(2)}) collective-permute-start(f32[2,72,128]{2,1,0:T(8,128)S(1)} %pad_maximum_fusion.cohort0_ref), channel_id=1, source_target_pairs={{0,64},{32,96},{64,0},{96,32},{1,65},{33,97},{65,1},{97,33},{2,66}... | collective-permute-start | bytes 221192 | tf_op jit(solution)/shard_map/ppermute | solution.py:299
  56.6 4.4 %collective-permute-start.5 = (f32[2,72,128]{2,1,0:T(8,128)S(1)}, f32[2,72,128]{2,1,0:T(8,128)S(1)}, u32[]{:S(2)}, u32[]{:S(2)}) collective-permute-start(f32[2,72,128]{2,1,0:T(8,128)S(1)} %pad_maximum_fusion.cohort0_ref), channel_id=1, source_target_pairs={{0,32},{32,64},{64,96},{96,0},{1,33},{33,65},{65,97},{97,1},{2,34}... | collective-permute-start | bytes 221192 | tf_op jit(solution)/shard_map/ppermute | solution.py:299
  68.9 2.7 %collective-permute-start.8 = (bf16[4,4,4,8,1024]{4,3,2,1,0:T(8,128)(2,1)S(1)}, bf16[4,4,4,8,1024]{4,3,2,1,0:T(8,128)(2,1)S(1)}, u32[]{:S(2)}, u32[]{:S(2)}) collective-permute-start(bf16[4,4,4,8,1024]{4,3,2,1,0:T(8,128)(2,1)S(1)} %get-tuple-element.15), channel_id=1, source_target_pairs={{0,1},{1,0},{2,3},{3,2},{4,5},{5,4},{6,7},{7,6},{8,9},{9,8},{10,11... | collective-permute-start | bytes 3145736 | tf_op jit(solution)/shard_map/ppermute | solution.py:299
  107.0 5.0 %collective-permute-start.11 = (bf16[8,1024]{1,0:T(8,128)(2,1)S(1)}, bf16[8,1024]{1,0:T(8,128)(2,1)S(1)}, u32[]{:S(2)}, u32[]{:S(2)}) collective-permute-start(bf16[8,1024]{1,0:T(8,128)(2,1)S(1)} %reduce_sum.25.own_ref), channel_id=1, source_target_pairs={{0,96},{32,0},{64,32},{96,64},{1,97},{33,1},{65,33},{97,65},{2,98}... | collective-permute-start | bytes 49160 | tf_op jit(solution)/shard_map/ppermute | solution.py:299
  107.6 5.2 %collective-permute-start.10 = (bf16[8,1024]{1,0:T(8,128)(2,1)S(1)}, bf16[8,1024]{1,0:T(8,128)(2,1)S(1)}, u32[]{:S(2)}, u32[]{:S(2)}) collective-permute-start(bf16[8,1024]{1,0:T(8,128)(2,1)S(1)} %reduce_sum.25.own_ref), channel_id=1, source_target_pairs={{0,64},{32,96},{64,0},{96,32},{1,65},{33,97},{65,1},{97,33},{2,66}... | collective-permute-start | bytes 49160 | tf_op jit(solution)/shard_map/ppermute | solution.py:299
  110.7 3.7 %collective-permute-start.9 = (bf16[8,1024]{1,0:T(8,128)(2,1)S(1)}, bf16[8,1024]{1,0:T(8,128)(2,1)S(1)}, u32[]{:S(2)}, u32[]{:S(2)}) collective-permute-start(bf16[8,1024]{1,0:T(8,128)(2,1)S(1)} %reduce_sum.25.own_ref), channel_id=1, source_target_pairs={{0,32},{32,64},{64,96},{96,0},{1,33},{33,65},{65,97},{97,1},{2,34}... | collective-permute-start | bytes 49160 | tf_op jit(solution)/shard_map/ppermute | solution.py:299

commit v5 on v4

--- a/solution.py
+++ b/solution.py
@@ -26,11 +26,13 @@
 NORM = MEMBERS / math.sqrt(SAMPLES * CELLS_OUT)
 SECOND_AT = SLOTS * CHANNELS
 HEAD_AT = 2 * SLOTS * CHANNELS
-WIDTH = 4096
+PART = 896
+SHARE = 32
+WIDTH = HEAD_AT + 128
 MIB = 1024 * 1024
 TILES_MIB = 24
 SAVED_ROWS = 8192
-MID_AT, W_AT, SLOPE1_AT, SLOPE2_AT = 0, 3584, 5632, 7680
+MID_AT, SLOPE1_AT, W_AT, SLOPE2_AT = 0, 3584, 5632, 7680
 
 f32 = jnp.float32
 bf16 = jnp.bfloat16
@@ -79,21 +81,32 @@
 def forward_kernel(
     place_ref, mine_ref, other_ref, x_ref, parents_ref, nb_mid_ref, parents_mid_ref, tiles_hbm,
     x2_ref, pred_ref, saved_hbm,
-    tiles_ref, w_ref, saved_ref, in_sem, out_sem,
+    tiles_ref, w_ref, saved_ref, select_ref, in_sem, out_sem,
 ):
     loads = [pltpu.make_async_copy(tiles_hbm.at[m], tiles_ref.at[m], in_sem.at[m]) for m in range(LOCAL)]
     for load in loads:
         load.start()
     first, z = place_ref[0] == 0, place_ref[1]
-    for x in range(4):
-        for y in range(4):
+    group = lane_group(16)
+
+    def both_rows(block, lanes):
+        mine, other = mine_ref[block, :, lanes].astype(f32), other_ref[block, :, lanes].astype(f32)
+        return jnp.concatenate([jnp.where(first, mine, other), jnp.where(first, other, mine)], 0)
+
+    for y in range(4):
+        rows = [pl.ds(pl.multiple_of((lax.rem(z - back + 4, 4) * 4 + y) * 16, 16), 16) for back in range(4)]
+        for x in range(4):
             for back in range(4):
-                mine, other = mine_ref[x * 4 + y, back].astype(f32), other_ref[x * 4 + y, back].astype(f32)
-                pair = jnp.concatenate([jnp.where(first, mine, other), jnp.where(first, other, mine)], 0)
-                row = pl.multiple_of((lax.rem(z - back + 4, 4) * 4 + y) * 16, 16)
-                w_ref[pl.ds(row, 16), x * QUARTER : (x + 1) * QUARTER] = pair.astype(bf16)
-    saved_ref[W_AT + SECOND_AT : SLOPE1_AT, 128:256] = jnp.zeros((CHANNELS, 128), bf16)
-    saved_ref[W_AT + SECOND_AT : SLOPE1_AT, 0:128] = w_ref[:, HEAD_AT : HEAD_AT + 128]
+                part = both_rows(x * 4 + y, slice(back * PART, (back + 1) * PART))
+                w_ref[rows[back], x * PART : (x + 1) * PART] = part.astype(bf16)
+        shares = [both_rows(x * 4 + y, slice(HEAD_AT, WIDTH)) for x in range(4)]
+        for back in range(4):
+            head = jnp.zeros((16, 128), f32)
+            for x in range(4):
+                head = jnp.where(group == x, pltpu.roll(shares[x], (x - back) % 4 * SHARE, 1), head)
+            w_ref[rows[back], HEAD_AT:WIDTH] = head.astype(bf16)
+    saved_ref[W_AT + SECOND_AT : SLOPE2_AT, 128:256] = jnp.zeros((CHANNELS, 128), bf16)
+    saved_ref[W_AT + SECOND_AT : SLOPE2_AT, 0:128] = w_ref[:, HEAD_AT : HEAD_AT + 128]
     for j in range(SLOTS):
         at = SECOND_AT + j * CHANNELS
         saved_ref[W_AT + j * CHANNELS : W_AT + (j + 1) * CHANNELS] = w_ref[:, at : at + CHANNELS]
@@ -104,8 +117,10 @@
         stores.append(pltpu.make_async_copy(saved_ref.at[rows], saved_hbm.at[rows], out_sem.at[len(stores)]))
         stores[-1].start()
 
-    save(W_AT, SLOPE1_AT)
+    save(W_AT, SLOPE2_AT)
     unpool = one_hot(parents_ref[...], CELLS_MID)
+    for j in range(1, SLOTS):
+        select_ref[j - 1] = one_hot(nb_mid_ref[j : j + 1, :], CELLS_MID)
     x1 = []
     for m in range(LOCAL):
         loads[m].wait()
@@ -127,11 +142,11 @@
         saved_ref[m * SECOND_AT : m * SECOND_AT + CHANNELS] = x1[m]
     both = jnp.concatenate(x1, 0)
     for j in range(1, SLOTS):
-        tile = dot(both, one_hot(nb_mid_ref[j : j + 1, :], CELLS_MID)).astype(bf16)
+        tile = dot(both, select_ref[j - 1]).astype(bf16)
         for m in range(LOCAL):
             row = m * SECOND_AT + j * CHANNELS
             saved_ref[row : row + CHANNELS] = tile[m * CHANNELS : (m + 1) * CHANNELS]
-    save(MID_AT, W_AT)
+    save(MID_AT, SLOPE1_AT)
     pool = one_hot(parents_mid_ref[...], CELLS_OUT)
     for m in range(LOCAL):
         a2 = dot(w_ref[:, SECOND_AT:HEAD_AT], saved_ref[m * SECOND_AT : (m + 1) * SECOND_AT])
@@ -147,10 +162,20 @@
         store.wait()
 
 
+def lane_group(rows):
+    return lax.div(lax.broadcasted_iota(jnp.int32, (rows, 128), 1), SHARE)
+
+
 def spread_kernel(own_ref, back1_ref, back2_ref, back3_ref, out_ref):
+    sources = (own_ref, back1_ref, back2_ref, back3_ref)
+    head = own_ref[:, PART:QUARTER].astype(f32)
+    for back in range(1, 4):
+        head = head + pltpu.roll(sources[back][:, PART:QUARTER].astype(f32), back * SHARE, 1)
+    head = head.astype(bf16)
     for block in range(16):
-        for back, source in enumerate((own_ref, back1_ref, back2_ref, back3_ref)):
-            out_ref[block, back] = source[...]
+        for back in range(4):
+            out_ref[block, :, back * PART : (back + 1) * PART] = sources[back][:, 0:PART]
+        out_ref[block, :, HEAD_AT:WIDTH] = head
 
 
 def spread(pieces):
@@ -158,7 +183,7 @@
         spread_kernel,
         in_specs=[pl.BlockSpec(memory_space=pltpu.VMEM)] * 4,
         out_specs=pl.BlockSpec(memory_space=pltpu.VMEM),
-        out_shape=jax.ShapeDtypeStruct((16, 4, 8, QUARTER), bf16),
+        out_shape=jax.ShapeDtypeStruct((16, 8, WIDTH), bf16),
         compiler_params=pltpu.CompilerParams(vmem_limit_bytes=8 * MIB),
         name="spread",
     )(*pieces)
@@ -200,6 +225,7 @@
             pltpu.VMEM(TILES, bf16),
             pltpu.VMEM((CHANNELS, WIDTH), bf16),
             pltpu.VMEM((SAVED_ROWS, CELLS_MID), bf16),
+            pltpu.VMEM((SLOTS - 1, CELLS_MID, CELLS_MID), bf16),
             pltpu.SemaphoreType.DMA((LOCAL,)),
             pltpu.SemaphoreType.DMA((5,)),
         ],
@@ -217,21 +243,41 @@
     place_ref, cohort0_ref, cohort1_ref, cohort2_ref, cohort3_ref, own_ref, obs_ref, x2_ref,
     parents_ref, nb_mid_ref, parents_mid_ref, saved_hbm, x_hbm, tiles_hbm,
     kept_ref, sent_ref,
-    saved_ref, x_ref, tiles_ref, g1_ref, sem,
+    saved_ref, x_ref, tiles_ref, g1_ref, select_ref, unpool_ref, sem,
 ):
-    moves = ((saved_hbm, saved_ref), (x_hbm, x_ref), (tiles_hbm, tiles_ref))
+    early, late = pl.ds(W_AT, SAVED_ROWS - W_AT), pl.ds(0, W_AT)
+    moves = (
+        (saved_hbm.at[early], saved_ref.at[early]), (saved_hbm.at[late], saved_ref.at[late]), (x_hbm, x_ref), (tiles_hbm, tiles_ref)
+    )
     loads = [pltpu.make_async_copy(source, here, sem.at[i]) for i, (source, here) in enumerate(moves)]
     for load in loads:
         load.start()
     first = place_ref[0] == 0
 
-    def put(quarter, at, lanes, value):
-        for z in range(4):
+    def put_rows(quarter, y, lanes, value0, value1):
+        kept_ref[quarter, y, :, lanes] = jnp.where(first, value0, value1).astype(bf16)
+        sent_ref[quarter, y, :, lanes] = jnp.where(first, value1, value0).astype(bf16)
+
+    def put(piece, value):
+        at = piece * 256
+        cuts = [0, 128, 256] if at // PART != (at + 128) // PART else [0, 256]
+        for begin, end in zip(cuts[:-1], cuts[1:]):
+            quarter, offset = (at + begin) // PART, (at + begin) % PART
+            for z in range(4):
+                lanes = slice(z * PART + offset, z * PART + offset + end - begin)
+                for y in range(4):
+                    row = (z * 4 + y) * 16
+                    put_rows(quarter, y, lanes, value[row : row + 8, begin:end], value[row + 8 : row + 16, begin:end])
+
+    def put_head(value):
+        group = lane_group(16)
+        for quarter in range(4):
             for y in range(4):
-                row = (z * 4 + y) * 16
-                low, high = value[row : row + 8], value[row + 8 : row + 16]
-                kept_ref[quarter, y, z, :, at : at + lanes] = jnp.where(first, low, high).astype(bf16)
-                sent_ref[quarter, y, z, :, at : at + lanes] = jnp.where(first, high, low).astype(bf16)
+                packed = jnp.zeros((16, 128), f32)
+                for z in range(4):
+                    row = (z * 4 + y) * 16
+                    packed = jnp.where(group == z, pltpu.roll(value[row : row + 16], (z - quarter) % 4 * SHARE, 1), packed)
+                put_rows(quarter, y, slice(HEAD_AT, WIDTH), packed[0:8], packed[8:16])
 
     own = own_ref[...]
     spread = jnp.zeros_like(own)
@@ -242,38 +288,40 @@
     skill = sign_smooth(own - obs_ref[...])
     slope = NORM * (skill / MEMBERS - spread / (MEMBERS * (MEMBERS - 1)))
     slope = jnp.concatenate([slope, jnp.zeros((128 - FIELD_ROWS, 128), f32)], 0).astype(bf16)
-    put(3, 512, 128, dot_bt(x2_ref[...], slope))
-    put(3, 640, 384, jnp.zeros((CHANNELS, 384), f32))
+    put_head(dot_bt(x2_ref[...], slope))
     pool = one_hot(parents_mid_ref[...], CELLS_OUT)
     wide = [dot(slope[:, m * CELLS_OUT : (m + 1) * CELLS_OUT], pool).astype(bf16) for m in range(LOCAL)]
+    for j in range(1, SLOTS):
+        select_ref[j - 1] = one_hot(nb_mid_ref[j : j + 1, :], CELLS_MID)
+    unpool_ref[...] = one_hot(parents_ref[...], CELLS_MID)
     loads[0].wait()
-    head_t = saved_ref[W_AT + SECOND_AT : SLOPE1_AT, 0:128]
+    head_t = saved_ref[W_AT + SECOND_AT : SLOPE2_AT, 0:128]
     dh2 = [dot(head_t, wide[m]) * 0.25 for m in range(LOCAL)]
     slope2 = saved_ref[SLOPE2_AT:SAVED_ROWS].astype(f32)
     g2 = [(dh2[m] * slope2[m * CHANNELS : (m + 1) * CHANNELS]).astype(bf16) for m in range(LOCAL)]
     both = jnp.concatenate(g2, 0)
     back = [dh2[m] + dot_at(saved_ref[W_AT : W_AT + CHANNELS], g2[m]) for m in range(LOCAL)]
     for q in range(1, SLOTS):
-        spread_back = dot_bt(both, one_hot(nb_mid_ref[q : q + 1, :], CELLS_MID)).astype(bf16)
+        spread_back = dot_bt(both, select_ref[q - 1]).astype(bf16)
         weight = saved_ref[W_AT + q * CHANNELS : W_AT + (q + 1) * CHANNELS]
         for m in range(LOCAL):
             back[m] = back[m] + dot_at(weight, spread_back[m * CHANNELS : (m + 1) * CHANNELS])
-    unpool = one_hot(parents_ref[...], CELLS_MID)
+    loads[1].wait()
     for m in range(LOCAL):
-        dh1 = dot((back[m] * 0.25).astype(bf16), unpool)
+        dh1 = dot((back[m] * 0.25).astype(bf16), unpool_ref[...])
         for at in range(0, CELLS_IN, 256):
             slope1 = saved_ref[SLOPE1_AT + m * CELLS_IN + at : SLOPE1_AT + m * CELLS_IN + at + 256].astype(f32)
             g1_ref[m, :, at : at + 256] = (dh1[:, at : at + 256] * slope1).astype(bf16)
-    for load in loads[1:]:
+    for load in loads[2:]:
         load.wait()
     for q in range(SLOTS):
         row0, row1 = q * CHANNELS, SECOND_AT + q * CHANNELS
         grad = dot_bt(g2[0], saved_ref[row0 : row0 + CHANNELS]) + dot_bt(g2[1], saved_ref[row1 : row1 + CHANNELS])
-        put((SLOTS + q) // 4, (SLOTS + q) % 4 * 256, 256, grad)
-    put(0, 0, 256, dot_bt(g1_ref[0], x_ref[0]) + dot_bt(g1_ref[1], x_ref[1]))
+        put(SLOTS + q, grad)
+    put(0, dot_bt(g1_ref[0], x_ref[0]) + dot_bt(g1_ref[1], x_ref[1]))
     for j in range(1, SLOTS):
         grad = dot_bt(g1_ref[0], tiles_ref[0, j - 1]) + dot_bt(g1_ref[1], tiles_ref[1, j - 1])
-        put(j // 4, j % 4 * 256, 256, grad)
+        put(j, grad)
 
 
 def backward(place, cohort, own, obs, x2, saved, x0, tiles, parents_fine, nb_mid, parents_mid):
@@ -281,13 +329,15 @@
         backward_kernel,
         in_specs=[SMEM] + [VMEM] * 10 + [HBM] * 3,
         out_specs=[VMEM] * 2,
-        out_shape=[jax.ShapeDtypeStruct((4, 4, 4, 8, QUARTER), bf16)] * 2,
+        out_shape=[jax.ShapeDtypeStruct((4, 4, 8, WIDTH), bf16)] * 2,
         scratch_shapes=[
             pltpu.VMEM((SAVED_ROWS, CELLS_MID), bf16),
             pltpu.VMEM((LOCAL, CHANNELS, CELLS_IN), bf16),
             pltpu.VMEM(TILES, bf16),
             pltpu.VMEM((LOCAL, CHANNELS, CELLS_IN), bf16),
-            pltpu.SemaphoreType.DMA((3,)),
+            pltpu.VMEM((SLOTS - 1, CELLS_MID, CELLS_MID), bf16),
+            pltpu.VMEM((CELLS_MID, CELLS_IN), bf16),
+            pltpu.SemaphoreType.DMA((4,)),
         ],
         compiler_params=pltpu.CompilerParams(vmem_limit_bytes=50 * MIB),
         cost_estimate=pl.CostEstimate(flops=4_000_000_000, bytes_accessed=16_000_000, transcendentals=200_000),
@@ -310,30 +360,62 @@
         ],
         1,
     )
-    mine = lax.dynamic_slice_in_dim(flat, x * QUARTER, QUARTER, 1)
+    mine = jnp.concatenate(
+        [
+            lax.dynamic_slice_in_dim(flat, x * PART, PART, 1),
+            lax.dynamic_slice_in_dim(flat, HEAD_AT + x * SHARE, SHARE, 1),
+            jnp.zeros((rows, QUARTER - PART - SHARE), bf16),
+        ],
+        1,
+    )
     column = spread([mine] + [shift(mine, "z_hi", 4, s) for s in (1, 2, 3)])
     plane = after(lax.all_to_all(column, ("x", "y"), 0, 0), tiles)
     return plane, shift(plane, "core", 2, 1)
 
 
+def fold_kernel(plane_ref, out_ref):
+    total = plane_ref[0].astype(f32)
+    for block in range(1, 16):
+        total = total + plane_ref[block].astype(f32)
+    head, group = total[:, HEAD_AT:WIDTH], lane_group(8)
+    for z in range(4):
+        share = jnp.where(group == 0, pltpu.roll(head, -z % 4 * SHARE, 1), 0.0).astype(bf16)
+        for low in range(2):
+            out_ref[z * 2 + low, :, 0:PART] = total[:, z * PART : (z + 1) * PART].astype(bf16)
+            out_ref[z * 2 + low, :, PART:QUARTER] = share
+
+
+def fold(plane):
+    return pl.pallas_call(
+        fold_kernel,
+        in_specs=[VMEM],
+        out_specs=VMEM,
+        out_shape=jax.ShapeDtypeStruct((8, 8, QUARTER), bf16),
+        compiler_params=pltpu.CompilerParams(vmem_limit_bytes=8 * MIB),
+        name="fold",
+    )(plane)
+
+
 def reduce_gradients(kept, sent, x):
     total = (kept.astype(f32) + shift(sent, "core", 2, 1).astype(f32)).astype(bf16)
-    plane = lax.all_to_all(total.reshape(16, 4, 8, QUARTER), ("x", "y"), 0, 0)
-    total = jnp.sum(plane.astype(f32), 0).astype(bf16)
-    column = jnp.broadcast_to(total[:, None], (4, 2, 8, QUARTER)).reshape(8, 8, QUARTER)
+    column = fold(lax.all_to_all(total.reshape(16, 8, WIDTH), ("x", "y"), 0, 0))
     column = lax.all_to_all(column, ("z_hi", "z_lo"), 0, 0)
     total = jnp.sum(column.astype(f32), 0).astype(bf16)
     return finish(x.astype(jnp.int32).reshape(1), [total] + [shift(total, "x", 4, s) for s in (1, 2, 3)])
 
 
-def finish_kernel(x_ref, own_ref, back1_ref, back2_ref, back3_ref, first_ref, second_ref, head_ref, slots_ref):
+def finish_kernel(x_ref, own_ref, back1_ref, back2_ref, back3_ref, first_ref, second_ref, head_ref, flat_ref, heads_ref):
     for back, source in enumerate((own_ref, back1_ref, back2_ref, back3_ref)):
-        at = lax.rem(x_ref[0] - back + 4, 4) * 4
-        for slot in range(4):
-            slots_ref[at + slot] = source[:, slot * CHANNELS : (slot + 1) * CHANNELS].astype(f32)
-    first_ref[...] = slots_ref[0:SLOTS]
-    second_ref[...] = slots_ref[SLOTS : 2 * SLOTS]
-    head_ref[...] = slots_ref[2 * SLOTS, :, 0:FIELDS]
+        quarter = lax.rem(x_ref[0] - back + 4, 4)
+        flat_ref[:, pl.ds(pl.multiple_of(quarter * PART, 128), PART)] = source[:, 0:PART].astype(f32)
+        heads_ref[quarter] = source[:, PART:QUARTER].astype(f32)
+    for j in range(SLOTS):
+        first_ref[j] = flat_ref[:, j * CHANNELS : (j + 1) * CHANNELS]
+        second_ref[j] = flat_ref[:, SECOND_AT + j * CHANNELS : SECOND_AT + (j + 1) * CHANNELS]
+    head = heads_ref[0]
+    for x in range(1, 4):
+        head = head + pltpu.roll(heads_ref[x], x * SHARE, 1)
+    head_ref[...] = head[:, 0:FIELDS]
 
 
 def finish(x, quarters):
@@ -346,7 +428,7 @@
             jax.ShapeDtypeStruct((SLOTS, 8, CHANNELS), f32),
             jax.ShapeDtypeStruct((8, FIELDS), f32),
         ],
-        scratch_shapes=[pltpu.VMEM((16, 8, CHANNELS), f32)],
+        scratch_shapes=[pltpu.VMEM((8, HEAD_AT), f32), pltpu.VMEM((4, 8, 128), f32)],
         compiler_params=pltpu.CompilerParams(vmem_limit_bytes=16 * MIB),
         name="finish",
     )(x, *quarters)

time: 115 us -> 112 us (0.974)
  waiting for transfers between devices: 24.1 us -> 22.6 us
  blocking collectives: 34.7 us -> 33.5 us
    all_to_all x1, blocking collectives: 20.7 us -> 19.6 us  [reduce_gradients(): column = fold(lax.all_to_all(total.reshape(16, 8, WIDTH), ('x', 'y'), 0, 0))]
where the time goes in v5:
time: 112 us
  blocking collectives  33.5 us (30%)
  starting transfers between devices  26.8 us (24%)
  Pallas kernels  26.6 us (24%)
  waiting for transfers between devices  22.6 us (20%)
  local copies, waits for them, and re-layouts  1.22 us (1%)
    all_to_all x1, blocking collectives, reduce_gradients(): column = fold(lax.all_to_all(total.reshape(16, 8, WIDTH), ('x', 'y'), 0, 0))  19.6 us
    ppermute x12, starting transfers between devices, shift(): return lax.ppermute(v, axis, [(i, (i + by) % n) for i in range(n)])  19.3 us
    ppermute x12, waiting for transfers between devices, shift(): return lax.ppermute(v, axis, [(i, (i + by) % n) for i in range(n)])  18.6 us
    all_to_all x1, blocking collectives, reduce_gradients(): column = lax.all_to_all(column, ('z_hi', 'z_lo'), 0, 0)  14 us
    pallas_call x1, Pallas kernels, fine_tiles(): pl.pallas_call(tiles_kernel, grid=(SLOTS - 1,), in_specs=[pl.BlockSpec((L...  8.68 us
    pallas_call x1, Pallas kernels, forward(): pl.pallas_call(forward_kernel, in_specs=[SMEM, VMEM, VMEM, VMEM, VMEM, VM...  8.55 us
    pallas_call x1, Pallas kernels, backward(): pl.pallas_call(backward_kernel, in_specs=[SMEM] + [VMEM] * 10 + [HBM] * 3...  7.45 us
    all_to_all x1, starting transfers between devices, gather_weights(): plane = after(lax.all_to_all(column, ('x', 'y'), 0, 0), tiles)  7.43 us
  transfers between devices with their start and end apart: 13, of which 11 were waited for; matrix products, arithmetic and copies ran while one was open for 0% of the time, Pallas kernels for 8%

profile of v5, /device:TPU:6, one launch (start us, length us, event | category | flops | bytes accessed | tf_op | source)
XLA Modules:
  0.0 111.8 jit_solution(535781825012585051)
XLA Ops:
  0.7 0.9 concatenate.9
  1.8 6.4 %collective-permute-start.2 = (bf16[8,1024]{1,0:T(8,128)(2,1)S(1)}, bf16[8,1024]{1,0:T(8,128)(2,1)S(1)}, u32[]{:S(2)}, u32[]{:S(2)}) collective-permute-start(bf16[8,1024]{1,0:T(8,128)(2,1)S(1)} %maximum_maximum_fusion.own_ref), channel_id=1, source_target_pairs={{0,24},{8,0},{16,8},{24,16},{1,25},{9,1},{17,9},{25,17},{2,26},{10... | collective-permute-start | bytes 49160 | tf_op jit(solution)/shard_map/ppermute | solution.py:349
  8.2 1.0 collective-permute-start.1
  9.1 2.8 %collective-permute-start = (bf16[8,1024]{1,0:T(8,128)(2,1)S(1)}, bf16[8,1024]{1,0:T(8,128)(2,1)S(1)}, u32[]{:S(2)}, u32[]{:S(2)}) collective-permute-start(bf16[8,1024]{1,0:T(8,128)(2,1)S(1)} %maximum_maximum_fusion.own_ref), channel_id=1, source_target_pairs={{0,8},{8,16},{16,24},{24,0},{1,9},{9,17},{17,25},{25,1},{2,10},{10... | collective-permute-start | bytes 49160 | tf_op jit(solution)/shard_map/ppermute | solution.py:349
  12.0 3.8 %collective-permute-done.1.back2_ref = bf16[8,1024]{1,0:T(8,128)(2,1)S(1)} collective-permute-done((bf16[8,1024]{1,0:T(8,128)(2,1)S(1)}, bf16[8,1024]{1,0:T(8,128)(2,1)S(1)}, u32[]{:S(2)}, u32[]{:S(2)}) %collective-permute-start.1) | collective-permute-done | bytes 16416 | tf_op jit(solution)/shard_map/ppermute | solution.py:349
  15.8 1.1 spread.1
  16.9 7.4 %all-to-all-start = ((bf16[16,8,3712]{2,1,0:T(8,128)(2,1)}), bf16[16,8,3712]{2,1,0:T(8,128)(2,1)S(1)}, u32[]{:S(2)}, u32[]{:S(2)}) async-start(bf16[16,8,3712]{2,1,0:T(8,128)(2,1)} %spread.1), calls=%async_computation | async-start | bytes 1900544 | tf_op jit(solution)/shard_map/all_to_all | solution.py:372
  24.3 8.7 %fine_tiles.1.first_ref.tiles_hbm = bf16[2,6,256,1024]{3,2,1,0:T(8,128)(2,1)} custom-call(bf16[512,1024]{1,0:T(8,128)(2,1)S(1)} %bitcast.20, s32[7,1024]{1,0:T(8,128)S(1)} %copy-done.1), custom_call_target="tpu_custom_call" | custom-call | flops 6499999744 | bytes 8000000 | tf_op jit(solution)/shard_map/fine_tiles/pallas_call | solution.py:66
  33.0 4.0 %all-to-all-done.value_ref = bf16[16,8,3712]{2,1,0:T(8,128)(2,1)S(1)} async-done(((bf16[16,8,3712]{2,1,0:T(8,128)(2,1)}), bf16[16,8,3712]{2,1,0:T(8,128)(2,1)S(1)}, u32[]{:S(2)}, u32[]{:S(2)}) %all-to-all-start) | async-done | bytes 950304 | tf_op jit(solution)/shard_map/all_to_all | solution.py:372
  37.0 2.4 %collective-permute-done.3.other_ref = bf16[16,8,3712]{2,1,0:T(8,128)(2,1)S(1)} collective-permute-done((bf16[16,8,3712]{2,1,0:T(8,128)(2,1)S(1)}, bf16[16,8,3712]{2,1,0:T(8,128)(2,1)S(1)}, u32[]{:S(2)}, u32[]{:S(2)}) %collective-permute-start.3) | collective-permute-done | bytes 950304 | tf_op jit(solution)/shard_map/ppermute | solution.py:349
  39.5 8.5 %forward.1 = (bf16[256,128]{1,0:T(8,128)(2,1)S(1)}, f32[72,128]{1,0:T(8,128)S(1)}, bf16[8192,256]{1,0:T(8,128)(2,1)}) custom-call(s32[2]{0:T(128)S(1)} %pad_add_fusion.place_ref, bf16[16,8,3712]{2,1,0:T(8,128)(2,1)S(1)} %after.1.mine_ref, bf16[16,8,3712]{2,1,0:T(8,128)(2,1)S(1)} %collective-permute-done.3.other_ref, bf16[2,256,1024]{2,1,0:T(8,128)(2,1)S(1)} %bitcast.21, ...), custom_call_target="tpu_custom_call" | custom-call | flops 3200000000 | bytes 14000000 | tf_op jit(solution)/shard_map/forward/pallas_call | solution.py:215
  48.1 1.1 collective-permute-start.4
  49.3 2.8 %collective-permute-done.4 = f32[72,128]{1,0:T(8,128)S(1)} collective-permute-done((f32[72,128]{1,0:T(8,128)S(1)}, f32[72,128]{1,0:T(8,128)S(1)}, u32[]{:S(2)}, u32[]{:S(2)}) %collective-permute-start.4) | collective-permute-done | bytes 36896 | tf_op jit(solution)/shard_map/ppermute | solution.py:349
  52.1 0.5 collective-permute-start.7
  52.6 3.0 %collective-permute-start.6 = (f32[2,72,128]{2,1,0:T(8,128)S(1)}, f32[2,72,128]{2,1,0:T(8,128)S(1)}, u32[]{:S(2)}, u32[]{:S(2)}) collective-permute-start(f32[2,72,128]{2,1,0:T(8,128)S(1)} %pad_maximum_fusion.cohort0_ref), channel_id=1, source_target_pairs={{0,64},{32,96},{64,0},{96,32},{1,65},{33,97},{65,1},{97,33},{2,66}... | collective-permute-start | bytes 221192 | tf_op jit(solution)/shard_map/ppermute | solution.py:349
  55.6 0.5 collective-permute-start.5
  56.2 1.5 %collective-permute-done.7.cohort3_ref = f32[2,72,128]{2,1,0:T(8,128)S(1)} collective-permute-done((f32[2,72,128]{2,1,0:T(8,128)S(1)}, f32[2,72,128]{2,1,0:T(8,128)S(1)}, u32[]{:S(2)}, u32[]{:S(2)}) %collective-permute-start.7) | collective-permute-done | bytes 73760 | tf_op jit(solution)/shard_map/ppermute | solution.py:349
  57.7 1.1 collective-permute-done.6.cohort2_ref
  58.7 1.2 %collective-permute-done.5.cohort1_ref = f32[2,72,128]{2,1,0:T(8,128)S(1)} collective-permute-done((f32[2,72,128]{2,1,0:T(8,128)S(1)}, f32[2,72,128]{2,1,0:T(8,128)S(1)}, u32[]{:S(2)}, u32[]{:S(2)}) %collective-permute-start.5) | collective-permute-done | bytes 73760 | tf_op jit(solution)/shard_map/ppermute | solution.py:349
  60.0 7.4 %backward.1 = (bf16[4,4,8,3712]{3,2,1,0:T(8,128)(2,1)S(1)}, bf16[4,4,8,3712]{3,2,1,0:T(8,128)(2,1)S(1)}) custom-call(s32[2]{0:T(128)S(1)} %pad_add_fusion.place_ref, f32[2,72,128]{2,1,0:T(8,128)S(1)} %pad_maximum_fusion.cohort0_ref, f32[2,72,128]{2,1,0:T(8,128)S(1)} %collective-permute-done.5.cohort1_ref, ...), custom_call_target="tpu_custom_call" | custom-call | flops 4000000000 | bytes 16000000 | tf_op jit(solution)/shard_map/backward/pallas_call | solution.py:328
  67.5 2.5 %collective-permute-done.8 = bf16[4,4,8,3712]{3,2,1,0:T(8,128)(2,1)S(1)} collective-permute-done((bf16[4,4,8,3712]{3,2,1,0:T(8,128)(2,1)S(1)}, bf16[4,4,8,3712]{3,2,1,0:T(8,128)(2,1)S(1)}, u32[]{:S(2)}, u32[]{:S(2)}) %collective-permute-start.8) | collective-permute-done | bytes 950304 | tf_op jit(solution)/shard_map/ppermute | solution.py:349
  70.0 0.2 add_convert_fusion
  70.3 19.6 %all_to_all.15.plane_ref = bf16[16,8,3712]{2,1,0:T(8,128)(2,1)S(1)} all-to-all(bf16[16,8,3712]{2,1,0:T(8,128)(2,1)S(1)} %bitcast.27), channel_id=1, replica_groups=mesh['z_lo'=2,'x'=4,'z_hi'=4,'y'=4,'core'=2] {'x','y'}, dimensions={0} | all-to-all | bytes 1900544 | tf_op jit(solution)/shard_map/all_to_all | solution.py:401
  89.8 0.2 fold.1
  90.0 14.0 %all_to_all.16 = bf16[8,8,1024]{2,1,0:T(8,128)(2,1)S(1)} all-to-all(bf16[8,8,1024]{2,1,0:T(8,128)(2,1)S(1)} %fold.1), channel_id=1, replica_groups=mesh['z_lo'=2,'x'=4,'z_hi'=4,'y'=4,'core'=2] {'z_hi','z_lo'}, dimensions={0} | all-to-all | bytes 262144 | tf_op jit(solution)/shard_map/all_to_all | solution.py:402
  104.0 0.5 collective-permute-start.11
  104.5 2.9 %collective-permute-start.10 = (bf16[8,1024]{1,0:T(8,128)(2,1)S(1)}, bf16[8,1024]{1,0:T(8,128)(2,1)S(1)}, u32[]{:S(2)}, u32[]{:S(2)}) collective-permute-start(bf16[8,1024]{1,0:T(8,128)(2,1)S(1)} %reduce_sum.12.own_ref), channel_id=1, source_target_pairs={{0,64},{32,96},{64,0},{96,32},{1,65},{33,97},{65,1},{97,33},{2,66}... | collective-permute-start | bytes 49160 | tf_op jit(solution)/shard_map/ppermute | solution.py:349
  107.4 0.6 collective-permute-start.9
  108.0 1.0 collective-permute-done.11.back3_ref
  109.0 0.7 collective-permute-done.10.back2_ref
  109.7 1.4 %collective-permute-done.9.back1_ref = bf16[8,1024]{1,0:T(8,128)(2,1)S(1)} collective-permute-done((bf16[8,1024]{1,0:T(8,128)(2,1)S(1)}, bf16[8,1024]{1,0:T(8,128)(2,1)S(1)}, u32[]{:S(2)}, u32[]{:S(2)}) %collective-permute-start.9) | collective-permute-done | bytes 16416 | tf_op jit(solution)/shard_map/ppermute | solution.py:349
  111.1 0.7 finish.1
  (29 shorter events, 0.6 us)
Async XLA Ops:
  0.6 23.7 %copy-start = (bf16[1,2,256,1024]{3,2,1,0:T(8,128)(2,1)S(1)}, bf16[1,2,256,1024]{3,2,1,0:T(8,128)(2,1)}, u32[]{:S(2)}) copy-start(bf16[1,2,256,1024]{3,2,1,0:T(8,128)(2,1)} %param.9) | copy-start | bytes 3145732
  0.6 23.7 %copy-start.1 = (s32[7,1024]{1,0:T(8,128)S(1)}, s32[7,1024]{1,0:T(8,128)}, u32[]{:S(2)}) copy-start(s32[7,1024]{1,0:T(8,128)} %nb_ref.1) | copy-start | bytes 86020
  1.8 10.2 %collective-permute-start.2 = (bf16[8,1024]{1,0:T(8,128)(2,1)S(1)}, bf16[8,1024]{1,0:T(8,128)(2,1)S(1)}, u32[]{:S(2)}, u32[]{:S(2)}) collective-permute-start(bf16[8,1024]{1,0:T(8,128)(2,1)S(1)} %maximum_maximum_fusion.own_ref), channel_id=1, source_target_pairs={{0,24},{8,0},{16,8},{24,16},{1,25},{9,1},{17,9},{25,17},{2,26},{10... | collective-permute-start | bytes 49160 | tf_op jit(solution)/shard_map/ppermute | solution.py:349
  8.2 7.6 %collective-permute-start.1 = (bf16[8,1024]{1,0:T(8,128)(2,1)S(1)}, bf16[8,1024]{1,0:T(8,128)(2,1)S(1)}, u32[]{:S(2)}, u32[]{:S(2)}) collective-permute-start(bf16[8,1024]{1,0:T(8,128)(2,1)S(1)} %maximum_maximum_fusion.own_ref), channel_id=1, source_target_pairs={{0,16},{8,24},{16,0},{24,8},{1,17},{9,25},{17,1},{25,9},{2,18},{10... | collective-permute-start | bytes 49160 | tf_op jit(solution)/shard_map/ppermute | solution.py:349
  9.1 6.7 %collective-permute-start = (bf16[8,1024]{1,0:T(8,128)(2,1)S(1)}, bf16[8,1024]{1,0:T(8,128)(2,1)S(1)}, u32[]{:S(2)}, u32[]{:S(2)}) collective-permute-start(bf16[8,1024]{1,0:T(8,128)(2,1)S(1)} %maximum_maximum_fusion.own_ref), channel_id=1, source_target_pairs={{0,8},{8,16},{16,24},{24,0},{1,9},{9,17},{17,25},{25,1},{2,10},{10... | collective-permute-start | bytes 49160 | tf_op jit(solution)/shard_map/ppermute | solution.py:349
  16.9 20.1 %all-to-all-start = ((bf16[16,8,3712]{2,1,0:T(8,128)(2,1)}), bf16[16,8,3712]{2,1,0:T(8,128)(2,1)S(1)}, u32[]{:S(2)}, u32[]{:S(2)}) async-start(bf16[16,8,3712]{2,1,0:T(8,128)(2,1)} %spread.1), calls=%async_computation | async-start | bytes 1900544 | tf_op jit(solution)/shard_map/all_to_all | solution.py:372
  33.0 6.5 %copy-start.2 = (s32[7,256]{1,0:T(8,128)S(1)}, s32[7,256]{1,0:T(8,128)}, u32[]{:S(2)}) copy-start(s32[7,256]{1,0:T(8,128)} %nb_mid_ref.3) | copy-start | bytes 21508
  33.0 6.5 %copy-start.3 = (s32[1024]{0:T(1024)S(1)}, s32[1024]{0:T(1024)}, u32[]{:S(2)}) copy-start(s32[1024]{0:T(1024)} %param.15) | copy-start | bytes 12292
  33.0 6.5 %copy-start.4 = (s32[256]{0:T(256)S(1)}, s32[256]{0:T(256)}, u32[]{:S(2)}) copy-start(s32[256]{0:T(256)} %param.16) | copy-start | bytes 3076
  37.0 2.5 %collective-permute-start.3 = (bf16[16,8,3712]{2,1,0:T(8,128)(2,1)S(1)}, bf16[16,8,3712]{2,1,0:T(8,128)(2,1)S(1)}, u32[]{:S(2)}, u32[]{:S(2)}) collective-permute-start(bf16[16,8,3712]{2,1,0:T(8,128)(2,1)S(1)} %after.1.mine_ref), channel_id=1, source_target_pairs={{0,1},{1,0},{2,3},{3,2},{4,5},{5,4},{6,7},{7,6},{8,9},{9,8},{10,11... | collective-permute-start | bytes 2850824 | tf_op jit(solution)/shard_map/ppermute | solution.py:349
  39.5 9.7 %copy-start.5 = (f32[1,69,64]{1,2,0:T(8,128)S(1)}, f32[1,69,64]{1,2,0:T(8,128)}, u32[]{:S(2)}) copy-start(f32[1,69,64]{1,2,0:T(8,128)} %param.17) | copy-start | bytes 52996
  48.1 4.0 %collective-permute-start.4 = (f32[72,128]{1,0:T(8,128)S(1)}, f32[72,128]{1,0:T(8,128)S(1)}, u32[]{:S(2)}, u32[]{:S(2)}) collective-permute-start(f32[72,128]{1,0:T(8,128)S(1)} %get-tuple-element.11.own_ref), channel_id=1, source_target_pairs={{0,128},{128,0},{1,129},{129,1},{2,130},{130,2},{3,131},{131,3},{4... | collective-permute-start | bytes 110600 | tf_op jit(solution)/shard_map/ppermute | solution.py:349
  52.1 5.6 %collective-permute-start.7 = (f32[2,72,128]{2,1,0:T(8,128)S(1)}, f32[2,72,128]{2,1,0:T(8,128)S(1)}, u32[]{:S(2)}, u32[]{:S(2)}) collective-permute-start(f32[2,72,128]{2,1,0:T(8,128)S(1)} %pad_maximum_fusion.cohort0_ref), channel_id=1, source_target_pairs={{0,96},{32,0},{64,32},{96,64},{1,97},{33,1},{65,33},{97,65},{2,98}... | collective-permute-start | bytes 221192 | tf_op jit(solution)/shard_map/ppermute | solution.py:349
  52.6 6.1 %collective-permute-start.6 = (f32[2,72,128]{2,1,0:T(8,128)S(1)}, f32[2,72,128]{2,1,0:T(8,128)S(1)}, u32[]{:S(2)}, u32[]{:S(2)}) collective-permute-start(f32[2,72,128]{2,1,0:T(8,128)S(1)} %pad_maximum_fusion.cohort0_ref), channel_id=1, source_target_pairs={{0,64},{32,96},{64,0},{96,32},{1,65},{33,97},{65,1},{97,33},{2,66}... | collective-permute-start | bytes 221192 | tf_op jit(solution)/shard_map/ppermute | solution.py:349
  55.6 4.4 %collective-permute-start.5 = (f32[2,72,128]{2,1,0:T(8,128)S(1)}, f32[2,72,128]{2,1,0:T(8,128)S(1)}, u32[]{:S(2)}, u32[]{:S(2)}) collective-permute-start(f32[2,72,128]{2,1,0:T(8,128)S(1)} %pad_maximum_fusion.cohort0_ref), channel_id=1, source_target_pairs={{0,32},{32,64},{64,96},{96,0},{1,33},{33,65},{65,97},{97,1},{2,34}... | collective-permute-start | bytes 221192 | tf_op jit(solution)/shard_map/ppermute | solution.py:349
  67.4 2.6 %collective-permute-start.8 = (bf16[4,4,8,3712]{3,2,1,0:T(8,128)(2,1)S(1)}, bf16[4,4,8,3712]{3,2,1,0:T(8,128)(2,1)S(1)}, u32[]{:S(2)}, u32[]{:S(2)}) collective-permute-start(bf16[4,4,8,3712]{3,2,1,0:T(8,128)(2,1)S(1)} %get-tuple-element.15), channel_id=1, source_target_pairs={{0,1},{1,0},{2,3},{3,2},{4,5},{5,4},{6,7},{7,6},{8,9},{9,8},{10,11... | collective-permute-start | bytes 2850824 | tf_op jit(solution)/shard_map/ppermute | solution.py:349
  104.0 5.0 %collective-permute-start.11 = (bf16[8,1024]{1,0:T(8,128)(2,1)S(1)}, bf16[8,1024]{1,0:T(8,128)(2,1)S(1)}, u32[]{:S(2)}, u32[]{:S(2)}) collective-permute-start(bf16[8,1024]{1,0:T(8,128)(2,1)S(1)} %reduce_sum.12.own_ref), channel_id=1, source_target_pairs={{0,96},{32,0},{64,32},{96,64},{1,97},{33,1},{65,33},{97,65},{2,98}... | collective-permute-start | bytes 49160 | tf_op jit(solution)/shard_map/ppermute | solution.py:349
  104.5 5.2 %collective-permute-start.10 = (bf16[8,1024]{1,0:T(8,128)(2,1)S(1)}, bf16[8,1024]{1,0:T(8,128)(2,1)S(1)}, u32[]{:S(2)}, u32[]{:S(2)}) collective-permute-start(bf16[8,1024]{1,0:T(8,128)(2,1)S(1)} %reduce_sum.12.own_ref), channel_id=1, source_target_pairs={{0,64},{32,96},{64,0},{96,32},{1,65},{33,97},{65,1},{97,33},{2,66}... | collective-permute-start | bytes 49160 | tf_op jit(solution)/shard_map/ppermute | solution.py:349
  107.4 3.7 %collective-permute-start.9 = (bf16[8,1024]{1,0:T(8,128)(2,1)S(1)}, bf16[8,1024]{1,0:T(8,128)(2,1)S(1)}, u32[]{:S(2)}, u32[]{:S(2)}) collective-permute-start(bf16[8,1024]{1,0:T(8,128)(2,1)S(1)} %reduce_sum.12.own_ref), channel_id=1, source_target_pairs={{0,32},{32,64},{64,96},{96,0},{1,33},{33,65},{65,97},{97,1},{2,34}... | collective-permute-start | bytes 49160 | tf_op jit(solution)/shard_map/ppermute | solution.py:349

commit v6 on v5

--- a/solution.py
+++ b/solution.py
@@ -80,7 +80,7 @@
 
 def forward_kernel(
     place_ref, mine_ref, other_ref, x_ref, parents_ref, nb_mid_ref, parents_mid_ref, tiles_hbm,
-    x2_ref, pred_ref, saved_hbm,
+    x2_ref, pred_ref, copies_ref, saved_hbm,
     tiles_ref, w_ref, saved_ref, select_ref, in_sem, out_sem,
 ):
     loads = [pltpu.make_async_copy(tiles_hbm.at[m], tiles_ref.at[m], in_sem.at[m]) for m in range(LOCAL)]
@@ -158,6 +158,8 @@
     save(SLOPE2_AT, SAVED_ROWS)
     pred = dot_at(w_ref[:, HEAD_AT : HEAD_AT + 128], x2_ref[...])
     pred_ref[...] = pred[0:FIELD_ROWS]
+    for peer in range(MEMBERS // LOCAL):
+        copies_ref[peer] = pred[0:FIELD_ROWS]
     for store in stores:
         store.wait()
 
@@ -215,10 +217,11 @@
     return pl.pallas_call(
         forward_kernel,
         in_specs=[SMEM, VMEM, VMEM, VMEM, VMEM, VMEM, VMEM, HBM],
-        out_specs=[VMEM, VMEM, HBM],
+        out_specs=[VMEM, VMEM, VMEM, HBM],
         out_shape=[
             jax.ShapeDtypeStruct((CHANNELS, LOCAL * CELLS_OUT), bf16),
             jax.ShapeDtypeStruct((FIELD_ROWS, LOCAL * CELLS_OUT), f32),
+            jax.ShapeDtypeStruct((MEMBERS // LOCAL, FIELD_ROWS, LOCAL * CELLS_OUT), f32),
             pltpu.HBM((SAVED_ROWS, CELLS_MID), bf16),
         ],
         scratch_shapes=[
@@ -240,7 +243,7 @@
 
 
 def backward_kernel(
-    place_ref, cohort0_ref, cohort1_ref, cohort2_ref, cohort3_ref, own_ref, obs_ref, x2_ref,
+    place_ref, cohort_ref, own_ref, obs_ref, x2_ref,
     parents_ref, nb_mid_ref, parents_mid_ref, saved_hbm, x_hbm, tiles_hbm,
     kept_ref, sent_ref,
     saved_ref, x_ref, tiles_ref, g1_ref, select_ref, unpool_ref, sem,
@@ -281,10 +284,9 @@
 
     own = own_ref[...]
     spread = jnp.zeros_like(own)
-    for pair_ref in (cohort0_ref, cohort1_ref, cohort2_ref, cohort3_ref):
-        for peer in range(2):
-            theirs = pair_ref[peer]
-            spread = spread + sign_smooth(own - theirs) + sign_smooth(own - pltpu.roll(theirs, CELLS_OUT, 1))
+    for peer in range(MEMBERS // LOCAL):
+        theirs = cohort_ref[peer]
+        spread = spread + sign_smooth(own - theirs) + sign_smooth(own - pltpu.roll(theirs, CELLS_OUT, 1))
     skill = sign_smooth(own - obs_ref[...])
     slope = NORM * (skill / MEMBERS - spread / (MEMBERS * (MEMBERS - 1)))
     slope = jnp.concatenate([slope, jnp.zeros((128 - FIELD_ROWS, 128), f32)], 0).astype(bf16)
@@ -327,7 +329,7 @@
 def backward(place, cohort, own, obs, x2, saved, x0, tiles, parents_fine, nb_mid, parents_mid):
     return pl.pallas_call(
         backward_kernel,
-        in_specs=[SMEM] + [VMEM] * 10 + [HBM] * 3,
+        in_specs=[SMEM] + [VMEM] * 7 + [HBM] * 3,
         out_specs=[VMEM] * 2,
         out_shape=[jax.ShapeDtypeStruct((4, 4, 8, WIDTH), bf16)] * 2,
         scratch_shapes=[
@@ -342,7 +344,7 @@
         compiler_params=pltpu.CompilerParams(vmem_limit_bytes=50 * MIB),
         cost_estimate=pl.CostEstimate(flops=4_000_000_000, bytes_accessed=16_000_000, transcendentals=200_000),
         name="backward",
-    )(place, *cohort, own, obs, x2, parents_fine, nb_mid, parents_mid, saved, x0, tiles)
+    )(place, cohort, own, obs, x2, parents_fine, nb_mid, parents_mid, saved, x0, tiles)
 
 
 def shift(v, axis, n, by):
@@ -448,11 +450,10 @@
 
     tiles = fine_tiles(x0.reshape(LOCAL * CHANNELS, CELLS_IN), neighbours_fine)
     mine, other = gather_weights(weight_first, weight_second, weight_head, x, tiles)
-    x2, pred, saved = forward(
+    x2, pred, copies, saved = forward(
         place, mine, other, x0, tiles, parents_fine, neighbours_mid, parents_mid
     )
-    pair = jnp.stack([pred, shift(pred, "z_lo", 2, 1)])
-    cohort = [pair] + [shift(pair, "x", 4, s) for s in (1, 2, 3)]
+    cohort = lax.all_to_all(copies, MEM, 0, 0)
     kept, sent = backward(place, cohort, pred, truth, x2, saved, x0, tiles, parents_fine, neighbours_mid, parents_mid)
     grad_first, grad_second, grad_head = reduce_gradients(kept, sent, x)
     return grad_first, grad_second, grad_head.T

time: 112 us -> 112 us (level)
    ppermute x12 -> x8, waiting for transfers between devices: 18.6 us -> 12.2 us  [shift(): return lax.ppermute(v, axis, [(i, (i + by) % n) for i in range(n)])]
    all_to_all x0 -> x1, waiting for transfers between devices: none -> 5.46 us  [per_device(): cohort = lax.all_to_all(copies, MEM, 0, 0)]
    all_to_all x0 -> x1, starting transfers between devices: none -> 5.38 us  [per_device(): cohort = lax.all_to_all(copies, MEM, 0, 0)]
    ppermute x12 -> x8, starting transfers between devices: 19.3 us -> 14.3 us  [shift(): return lax.ppermute(v, axis, [(i, (i + by) % n) for i in range(n)])]
  transfers between devices with their start and end apart: 13 -> 10, of which waited for: 11 -> 8; matrix products, arithmetic and copies ran while one was open for 0% -> 0% of each run, Pallas kernels for 8% -> 8%
where the time goes in v6:
time: 112 us
  blocking collectives  33.5 us (30%)
  Pallas kernels  27.2 us (24%)
  starting transfers between devices  27.1 us (24%)
  waiting for transfers between devices  21.6 us (19%)
  local copies, waits for them, and re-layouts  1.22 us (1%)
    all_to_all x1, blocking collectives, reduce_gradients(): column = fold(lax.all_to_all(total.reshape(16, 8, WIDTH), ('x', 'y'), 0, 0))  19.4 us
    ppermute x8, starting transfers between devices, shift(): return lax.ppermute(v, axis, [(i, (i + by) % n) for i in range(n)])  14.3 us
    all_to_all x1, blocking collectives, reduce_gradients(): column = lax.all_to_all(column, ('z_hi', 'z_lo'), 0, 0)  14 us
    ppermute x8, waiting for transfers between devices, shift(): return lax.ppermute(v, axis, [(i, (i + by) % n) for i in range(n)])  12.2 us
    pallas_call x1, Pallas kernels, forward(): pl.pallas_call(forward_kernel, in_specs=[SMEM, VMEM, VMEM, VMEM, VMEM, VM...  9.24 us
    pallas_call x1, Pallas kernels, fine_tiles(): pl.pallas_call(tiles_kernel, grid=(SLOTS - 1,), in_specs=[pl.BlockSpec((L...  8.69 us
    pallas_call x1, Pallas kernels, backward(): pl.pallas_call(backward_kernel, in_specs=[SMEM] + [VMEM] * 7 + [HBM] * 3,...  7.44 us
    all_to_all x1, starting transfers between devices, gather_weights(): plane = after(lax.all_to_all(column, ('x', 'y'), 0, 0), tiles)  7.43 us
  transfers between devices with their start and end apart: 10, of which 8 were waited for; matrix products, arithmetic and copies ran while one was open for 0% of the time, Pallas kernels for 8%

profile of v6, /device:TPU:6, one launch (start us, length us, event | category | flops | bytes accessed | tf_op | source)
XLA Modules:
  0.0 111.8 jit_solution(5767650929452994783)
XLA Ops:
  0.7 0.9 concatenate.9
  1.6 0.1 constant_dynamic-slice_fusion
  1.7 0.1 pad.9.clone
  1.8 6.4 %collective-permute-start.2 = (bf16[8,1024]{1,0:T(8,128)(2,1)S(1)}, bf16[8,1024]{1,0:T(8,128)(2,1)S(1)}, u32[]{:S(2)}, u32[]{:S(2)}) collective-permute-start(bf16[8,1024]{1,0:T(8,128)(2,1)S(1)} %maximum_maximum_fusion.own_ref), channel_id=1, source_target_pairs={{0,24},{8,0},{16,8},{24,16},{1,25},{9,1},{17,9},{25,17},{2,26},{10... | collective-permute-start | bytes 49160 | tf_op jit(solution)/shard_map/ppermute | solution.py:351
  8.2 1.0 collective-permute-start.1
  9.1 2.8 %collective-permute-start = (bf16[8,1024]{1,0:T(8,128)(2,1)S(1)}, bf16[8,1024]{1,0:T(8,128)(2,1)S(1)}, u32[]{:S(2)}, u32[]{:S(2)}) collective-permute-start(bf16[8,1024]{1,0:T(8,128)(2,1)S(1)} %maximum_maximum_fusion.own_ref), channel_id=1, source_target_pairs={{0,8},{8,16},{16,24},{24,0},{1,9},{9,17},{17,25},{25,1},{2,10},{10... | collective-permute-start | bytes 49160 | tf_op jit(solution)/shard_map/ppermute | solution.py:351
  12.0 3.8 %collective-permute-done.1.back2_ref = bf16[8,1024]{1,0:T(8,128)(2,1)S(1)} collective-permute-done((bf16[8,1024]{1,0:T(8,128)(2,1)S(1)}, bf16[8,1024]{1,0:T(8,128)(2,1)S(1)}, u32[]{:S(2)}, u32[]{:S(2)}) %collective-permute-start.1) | collective-permute-done | bytes 16416 | tf_op jit(solution)/shard_map/ppermute | solution.py:351
  15.8 1.0 spread.1
  16.8 7.4 %all-to-all-start = ((bf16[16,8,3712]{2,1,0:T(8,128)(2,1)}), bf16[16,8,3712]{2,1,0:T(8,128)(2,1)S(1)}, u32[]{:S(2)}, u32[]{:S(2)}) async-start(bf16[16,8,3712]{2,1,0:T(8,128)(2,1)} %spread.1), calls=%async_computation | async-start | bytes 1900544 | tf_op jit(solution)/shard_map/all_to_all | solution.py:374
  24.3 8.7 %fine_tiles.1.first_ref.tiles_hbm = bf16[2,6,256,1024]{3,2,1,0:T(8,128)(2,1)} custom-call(bf16[512,1024]{1,0:T(8,128)(2,1)S(1)} %bitcast.17, s32[7,1024]{1,0:T(8,128)S(1)} %copy-done.1), custom_call_target="tpu_custom_call" | custom-call | flops 6499999744 | bytes 8000000 | tf_op jit(solution)/shard_map/fine_tiles/pallas_call | solution.py:66
  33.0 4.0 %all-to-all-done.value_ref = bf16[16,8,3712]{2,1,0:T(8,128)(2,1)S(1)} async-done(((bf16[16,8,3712]{2,1,0:T(8,128)(2,1)}), bf16[16,8,3712]{2,1,0:T(8,128)(2,1)S(1)}, u32[]{:S(2)}, u32[]{:S(2)}) %all-to-all-start) | async-done | bytes 950304 | tf_op jit(solution)/shard_map/all_to_all | solution.py:374
  36.9 0.1 pad_add_fusion.place_ref
  37.0 2.4 %collective-permute-done.3.other_ref = bf16[16,8,3712]{2,1,0:T(8,128)(2,1)S(1)} collective-permute-done((bf16[16,8,3712]{2,1,0:T(8,128)(2,1)S(1)}, bf16[16,8,3712]{2,1,0:T(8,128)(2,1)S(1)}, u32[]{:S(2)}, u32[]{:S(2)}) %collective-permute-start.3) | collective-permute-done | bytes 950304 | tf_op jit(solution)/shard_map/ppermute | solution.py:351
  39.5 9.2 %forward.1 = (bf16[256,128]{1,0:T(8,128)(2,1)S(1)}, f32[72,128]{1,0:T(8,128)S(1)}, f32[8,72,128]{2,1,0:T(8,128)}, bf16[8192,256]{1,0:T(8,128)(2,1)}) custom-call(s32[2]{0:T(128)S(1)} %pad_add_fusion.place_ref, bf16[16,8,3712]{2,1,0:T(8,128)(2,1)S(1)} %after.1.mine_ref, bf16[16,8,3712]{2,1,0:T(8,128)(2,1)S(1)} %collective-permute-done.3.other_ref, ...), custom_call_target="tpu_custom_call" | custom-call | flops 3200000000 | bytes 14000000 | tf_op jit(solution)/shard_map/forward/pallas_call | solution.py:217
  48.7 5.4 %all-to-all-start.1 = ((f32[8,72,128]{2,1,0:T(8,128)}), f32[8,72,128]{2,1,0:T(8,128)S(1)}, u32[]{:S(2)}, u32[]{:S(2)}) async-start(f32[8,72,128]{2,1,0:T(8,128)} %get-tuple-element.12), calls=%async_computation.1 | async-start | bytes 589824 | tf_op jit(solution)/shard_map/all_to_all | solution.py:456
  54.1 0.1 copy.13
  54.2 0.1 pad_maximum_fusion.obs_ref
  54.3 5.5 %all-to-all-done.1.cohort_ref = f32[8,72,128]{2,1,0:T(8,128)S(1)} async-done(((f32[8,72,128]{2,1,0:T(8,128)}), f32[8,72,128]{2,1,0:T(8,128)S(1)}, u32[]{:S(2)}, u32[]{:S(2)}) %all-to-all-start.1) | async-done | bytes 294944 | tf_op jit(solution)/shard_map/all_to_all | solution.py:456
  59.8 7.4 %backward.1 = (bf16[4,4,8,3712]{3,2,1,0:T(8,128)(2,1)S(1)}, bf16[4,4,8,3712]{3,2,1,0:T(8,128)(2,1)S(1)}) custom-call(s32[2]{0:T(128)S(1)} %pad_add_fusion.place_ref, f32[8,72,128]{2,1,0:T(8,128)S(1)} %all-to-all-done.1.cohort_ref, f32[72,128]{1,0:T(8,128)S(1)} %get-tuple-element.13.own_ref, f32[72,128]{1,0:T(8,128)S(1)} %pad_maximum_fusion.obs_ref, ...), custom_call_target="tpu_custom_call" | custom-call | flops 4000000000 | bytes 16000000 | tf_op jit(solution)/shard_map/backward/pallas_call | solution.py:330
  67.2 0.1 collective-permute-start.4
  67.3 2.5 %collective-permute-done.4 = bf16[4,4,8,3712]{3,2,1,0:T(8,128)(2,1)S(1)} collective-permute-done((bf16[4,4,8,3712]{3,2,1,0:T(8,128)(2,1)S(1)}, bf16[4,4,8,3712]{3,2,1,0:T(8,128)(2,1)S(1)}, u32[]{:S(2)}, u32[]{:S(2)}) %collective-permute-start.4) | collective-permute-done | bytes 950304 | tf_op jit(solution)/shard_map/ppermute | solution.py:351
  69.8 0.2 add_convert_fusion
  70.0 19.4 %all_to_all.20.plane_ref = bf16[16,8,3712]{2,1,0:T(8,128)(2,1)S(1)} all-to-all(bf16[16,8,3712]{2,1,0:T(8,128)(2,1)S(1)} %bitcast.24), channel_id=1, replica_groups=mesh['z_lo'=2,'x'=4,'z_hi'=4,'y'=4,'core'=2] {'x','y'}, dimensions={0} | all-to-all | bytes 1900544 | tf_op jit(solution)/shard_map/all_to_all | solution.py:403
  89.5 0.2 fold.1
  89.7 14.0 %all_to_all.21 = bf16[8,8,1024]{2,1,0:T(8,128)(2,1)S(1)} all-to-all(bf16[8,8,1024]{2,1,0:T(8,128)(2,1)S(1)} %fold.1), channel_id=1, replica_groups=mesh['z_lo'=2,'x'=4,'z_hi'=4,'y'=4,'core'=2] {'z_hi','z_lo'}, dimensions={0} | all-to-all | bytes 262144 | tf_op jit(solution)/shard_map/all_to_all | solution.py:404
  103.7 0.6 collective-permute-start.7
  104.3 3.0 %collective-permute-start.6 = (bf16[8,1024]{1,0:T(8,128)(2,1)S(1)}, bf16[8,1024]{1,0:T(8,128)(2,1)S(1)}, u32[]{:S(2)}, u32[]{:S(2)}) collective-permute-start(bf16[8,1024]{1,0:T(8,128)(2,1)S(1)} %reduce_sum.12.own_ref), channel_id=1, source_target_pairs={{0,64},{32,96},{64,0},{96,32},{1,65},{33,97},{65,1},{97,33},{2,66}... | collective-permute-start | bytes 49160 | tf_op jit(solution)/shard_map/ppermute | solution.py:351
  107.4 0.3 collective-permute-start.5
  107.7 1.0 collective-permute-done.7.back3_ref
  108.7 0.9 collective-permute-done.6.back2_ref
  109.6 1.5 %collective-permute-done.5.back1_ref = bf16[8,1024]{1,0:T(8,128)(2,1)S(1)} collective-permute-done((bf16[8,1024]{1,0:T(8,128)(2,1)S(1)}, bf16[8,1024]{1,0:T(8,128)(2,1)S(1)}, u32[]{:S(2)}, u32[]{:S(2)}) %collective-permute-start.5) | collective-permute-done | bytes 16416 | tf_op jit(solution)/shard_map/ppermute | solution.py:351
  111.1 0.7 finish.1
  (22 shorter events, 0.1 us)
Async XLA Ops:
  0.6 23.6 %copy-start = (bf16[1,2,256,1024]{3,2,1,0:T(8,128)(2,1)S(1)}, bf16[1,2,256,1024]{3,2,1,0:T(8,128)(2,1)}, u32[]{:S(2)}) copy-start(bf16[1,2,256,1024]{3,2,1,0:T(8,128)(2,1)} %param.9) | copy-start | bytes 3145732
  0.6 23.6 %copy-start.1 = (s32[7,1024]{1,0:T(8,128)S(1)}, s32[7,1024]{1,0:T(8,128)}, u32[]{:S(2)}) copy-start(s32[7,1024]{1,0:T(8,128)} %nb_ref.1) | copy-start | bytes 86020
  1.8 10.2 %collective-permute-start.2 = (bf16[8,1024]{1,0:T(8,128)(2,1)S(1)}, bf16[8,1024]{1,0:T(8,128)(2,1)S(1)}, u32[]{:S(2)}, u32[]{:S(2)}) collective-permute-start(bf16[8,1024]{1,0:T(8,128)(2,1)S(1)} %maximum_maximum_fusion.own_ref), channel_id=1, source_target_pairs={{0,24},{8,0},{16,8},{24,16},{1,25},{9,1},{17,9},{25,17},{2,26},{10... | collective-permute-start | bytes 49160 | tf_op jit(solution)/shard_map/ppermute | solution.py:351
  8.2 7.6 %collective-permute-start.1 = (bf16[8,1024]{1,0:T(8,128)(2,1)S(1)}, bf16[8,1024]{1,0:T(8,128)(2,1)S(1)}, u32[]{:S(2)}, u32[]{:S(2)}) collective-permute-start(bf16[8,1024]{1,0:T(8,128)(2,1)S(1)} %maximum_maximum_fusion.own_ref), channel_id=1, source_target_pairs={{0,16},{8,24},{16,0},{24,8},{1,17},{9,25},{17,1},{25,9},{2,18},{10... | collective-permute-start | bytes 49160 | tf_op jit(solution)/shard_map/ppermute | solution.py:351
  9.1 6.7 %collective-permute-start = (bf16[8,1024]{1,0:T(8,128)(2,1)S(1)}, bf16[8,1024]{1,0:T(8,128)(2,1)S(1)}, u32[]{:S(2)}, u32[]{:S(2)}) collective-permute-start(bf16[8,1024]{1,0:T(8,128)(2,1)S(1)} %maximum_maximum_fusion.own_ref), channel_id=1, source_target_pairs={{0,8},{8,16},{16,24},{24,0},{1,9},{9,17},{17,25},{25,1},{2,10},{10... | collective-permute-start | bytes 49160 | tf_op jit(solution)/shard_map/ppermute | solution.py:351
  16.8 20.1 %all-to-all-start = ((bf16[16,8,3712]{2,1,0:T(8,128)(2,1)}), bf16[16,8,3712]{2,1,0:T(8,128)(2,1)S(1)}, u32[]{:S(2)}, u32[]{:S(2)}) async-start(bf16[16,8,3712]{2,1,0:T(8,128)(2,1)} %spread.1), calls=%async_computation | async-start | bytes 1900544 | tf_op jit(solution)/shard_map/all_to_all | solution.py:374
  33.0 6.5 %copy-start.2 = (s32[7,256]{1,0:T(8,128)S(1)}, s32[7,256]{1,0:T(8,128)}, u32[]{:S(2)}) copy-start(s32[7,256]{1,0:T(8,128)} %nb_mid_ref.3) | copy-start | bytes 21508
  33.0 6.5 %copy-start.3 = (s32[1024]{0:T(1024)S(1)}, s32[1024]{0:T(1024)}, u32[]{:S(2)}) copy-start(s32[1024]{0:T(1024)} %param.15) | copy-start | bytes 12292
  33.0 6.5 %copy-start.4 = (s32[256]{0:T(256)S(1)}, s32[256]{0:T(256)}, u32[]{:S(2)}) copy-start(s32[256]{0:T(256)} %param.16) | copy-start | bytes 3076
  36.9 2.5 %collective-permute-start.3 = (bf16[16,8,3712]{2,1,0:T(8,128)(2,1)S(1)}, bf16[16,8,3712]{2,1,0:T(8,128)(2,1)S(1)}, u32[]{:S(2)}, u32[]{:S(2)}) collective-permute-start(bf16[16,8,3712]{2,1,0:T(8,128)(2,1)S(1)} %after.1.mine_ref), channel_id=1, source_target_pairs={{0,1},{1,0},{2,3},{3,2},{4,5},{5,4},{6,7},{7,6},{8,9},{9,8},{10,11... | collective-permute-start | bytes 2850824 | tf_op jit(solution)/shard_map/ppermute | solution.py:351
  39.5 14.6 %copy-start.5 = (f32[1,69,64]{1,2,0:T(8,128)S(1)}, f32[1,69,64]{1,2,0:T(8,128)}, u32[]{:S(2)}) copy-start(f32[1,69,64]{1,2,0:T(8,128)} %param.17) | copy-start | bytes 52996
  48.7 11.0 %all-to-all-start.1 = ((f32[8,72,128]{2,1,0:T(8,128)}), f32[8,72,128]{2,1,0:T(8,128)S(1)}, u32[]{:S(2)}, u32[]{:S(2)}) async-start(f32[8,72,128]{2,1,0:T(8,128)} %get-tuple-element.12), calls=%async_computation.1 | async-start | bytes 589824 | tf_op jit(solution)/shard_map/all_to_all | solution.py:456
  67.2 2.6 %collective-permute-start.4 = (bf16[4,4,8,3712]{3,2,1,0:T(8,128)(2,1)S(1)}, bf16[4,4,8,3712]{3,2,1,0:T(8,128)(2,1)S(1)}, u32[]{:S(2)}, u32[]{:S(2)}) collective-permute-start(bf16[4,4,8,3712]{3,2,1,0:T(8,128)(2,1)S(1)} %get-tuple-element.17), channel_id=1, source_target_pairs={{0,1},{1,0},{2,3},{3,2},{4,5},{5,4},{6,7},{7,6},{8,9},{9,8},{10,11... | collective-permute-start | bytes 2850824 | tf_op jit(solution)/shard_map/ppermute | solution.py:351
  103.7 5.0 %collective-permute-start.7 = (bf16[8,1024]{1,0:T(8,128)(2,1)S(1)}, bf16[8,1024]{1,0:T(8,128)(2,1)S(1)}, u32[]{:S(2)}, u32[]{:S(2)}) collective-permute-start(bf16[8,1024]{1,0:T(8,128)(2,1)S(1)} %reduce_sum.12.own_ref), channel_id=1, source_target_pairs={{0,96},{32,0},{64,32},{96,64},{1,97},{33,1},{65,33},{97,65},{2,98}... | collective-permute-start | bytes 49160 | tf_op jit(solution)/shard_map/ppermute | solution.py:351
  104.3 5.2 %collective-permute-start.6 = (bf16[8,1024]{1,0:T(8,128)(2,1)S(1)}, bf16[8,1024]{1,0:T(8,128)(2,1)S(1)}, u32[]{:S(2)}, u32[]{:S(2)}) collective-permute-start(bf16[8,1024]{1,0:T(8,128)(2,1)S(1)} %reduce_sum.12.own_ref), channel_id=1, source_target_pairs={{0,64},{32,96},{64,0},{96,32},{1,65},{33,97},{65,1},{97,33},{2,66}... | collective-permute-start | bytes 49160 | tf_op jit(solution)/shard_map/ppermute | solution.py:351
  107.4 3.7 %collective-permute-start.5 = (bf16[8,1024]{1,0:T(8,128)(2,1)S(1)}, bf16[8,1024]{1,0:T(8,128)(2,1)S(1)}, u32[]{:S(2)}, u32[]{:S(2)}) collective-permute-start(bf16[8,1024]{1,0:T(8,128)(2,1)S(1)} %reduce_sum.12.own_ref), channel_id=1, source_target_pairs={{0,32},{32,64},{64,96},{96,0},{1,33},{33,65},{65,97},{97,1},{2,34}... | collective-permute-start | bytes 49160 | tf_op jit(solution)/shard_map/ppermute | solution.py:351
